TPU v7x, 32 devices: a whole 2x2x4 slice. The times are simulated.
32 devices in a mesh: dp: 16 (over z, y, x), tensor: 2 (over core).
Axes of the slice: x: 2, y: 2, z: 4, core: 2. Of those that a mesh axis runs over, the one named last changes fastest.
Arguments:
- patches: bfloat16 [2048, 1152], P('dp'), may hold values from -6 to 6
- cotangent: bfloat16 [2048, 1152], P('dp'), may hold values from -6 to 6
- image_lengths: int32 [64], replicated, may hold values from 4 to 256, as said below
- image_owner: int32 [64], replicated, may hold values from 0 to 15, as said below
- first_gain: float32 [1152], replicated, may hold values from 0.1 to 1.9
- first_shift: float32 [1152], replicated, may hold values from -3 to 3
- query_weight: bfloat16 [1152, 1152], P(None, 'tensor'), may hold values from -0.25 to 0.25
- query_bias: float32 [1152], P('tensor'), may hold values from -3 to 3
- key_weight: bfloat16 [1152, 1152], P(None, 'tensor'), may hold values from -0.25 to 0.25
- value_weight: bfloat16 [1152, 1152], P(None, 'tensor'), may hold values from -0.1875 to 0.1875
- value_bias: float32 [1152], P('tensor'), may hold values from -3 to 3
- output_weight: bfloat16 [1152, 1152], P(None, 'tensor'), may hold values from -0.75 to 0.75
- output_bias: float32 [1152], replicated, may hold values from -3 to 3
- second_gain: float32 [1152], replicated, may hold values from 0.1 to 1.9
- second_shift: float32 [1152], replicated, may hold values from -3 to 3
- expand_weight: bfloat16 [1152, 4304], P(None, 'tensor'), may hold values from -0.1875 to 0.1875
- expand_bias: float32 [4304], P('tensor'), may hold values from -3 to 3
- reduce_weight: bfloat16 [1152, 4304], P(None, 'tensor'), may hold values from -0.125 to 0.125
- reduce_bias: float32 [1152], replicated, may hold values from -3 to 3
Outputs:
- mixed: bfloat16 [2048, 1152], P('dp')
- patch_gradient: bfloat16 [2048, 1152], P('dp')
- first_gain_gradient: float32 [1152], replicated
- first_shift_gradient: float32 [1152], replicated
- query_weight_gradient: float32 [1152, 1152], P('dp', 'tensor')
- query_bias_gradient: float32 [1152], P('tensor')
- key_weight_gradient: float32 [1152, 1152], P('dp', 'tensor')
- value_weight_gradient: float32 [1152, 1152], P('dp', 'tensor')
- value_bias_gradient: float32 [1152], P('tensor')
- output_weight_gradient: float32 [1152, 1152], P('dp', 'tensor')
- output_bias_gradient: float32 [1152], replicated
- second_gain_gradient: float32 [1152], replicated
- second_shift_gradient: float32 [1152], replicated
- expand_weight_gradient: float32 [1152, 4304], P('dp', 'tensor')
- expand_bias_gradient: float32 [4304], P('tensor')
- reduce_weight_gradient: float32 [1152, 4304], P('dp', 'tensor')
- reduce_bias_gradient: float32 [1152], replicated
Inputs may be any that keep to these rules, and one draw needn't show every extreme that they name: `image_lengths`: images of one owner stand together in the stream; all lengths add up to 2048, and one image has exactly 256 patches. `image_owner`: never falls from one image to the next; every index of dp owns 1 to 7 images, whose patches add up to at most 256, and to exactly 256 for some index.
All inputs are finite; a program needn't handle non-finite values.
Results may differ from a plain program's by a relative error of at most 0.015.
Values may be sent and summed in bfloat16 or wider, within the bound.
No kernel may reach another device: no remote copies, remote signals or barrier semaphores. Data moves between devices by JAX's collectives and lax.ppermute only.
A program may use at most 192 MiB of HBM per device.

v0:
```python
import jax
import jax.numpy as jnp
from jax import lax
from jax.sharding import PartitionSpec as P

HD = 72


masked_score = -1000000000.0
norm_eps = 1e-06


def layer_norm(values, gain_row, shift_row):
    centered = values - jnp.mean(values, axis=-1, keepdims=True)
    variance = jnp.mean(centered * centered, axis=-1, keepdims=True)
    return centered * lax.rsqrt(variance + norm_eps) * gain_row + shift_row


def gelu_tanh(values):
    return jax.nn.gelu(values, approximate=True)


def matmul(left_side, right_side):
    return jnp.dot(left_side, right_side, preferred_element_type=jnp.float32)


def contract_rows(left_side, right_side):
    return lax.dot_general(
        left_side, right_side, (((0,), (0,)), ((), ())), preferred_element_type=jnp.float32
    )


def contract_cols(left_side, right_side):
    return lax.dot_general(
        left_side, right_side, (((1,), (1,)), ((), ())), preferred_element_type=jnp.float32
    )


def to_low(values):
    return values.astype(jnp.bfloat16)


def split_heads(values, local_heads):
    return values.reshape(values.shape[0], local_heads, HD).transpose(1, 0, 2)


def merge_heads(values):
    return values.transpose(1, 0, 2).reshape(values.shape[1], values.shape[0] * values.shape[2])


def head_scores(query_head, key_head, same_image):
    return jnp.where(same_image, contract_cols(query_head, key_head) * HD ** (-0.5), masked_score)


def attend_head(query_head, key_head, value_head, same_image):
    scores = head_scores(query_head, key_head, same_image)
    row_top = jnp.max(scores, axis=1, keepdims=True)
    exp_scores = jnp.exp(scores - row_top)
    row_total = jnp.sum(exp_scores, axis=1, keepdims=True)
    prob_rows = exp_scores / row_total
    head_out = matmul(to_low(prob_rows), value_head)
    return (to_low(head_out), (row_top + jnp.log(row_total))[:, 0])


def attend_back(query_head, key_head, value_head, out_grad, log_total, same_image):
    scores = head_scores(query_head, key_head, same_image)
    prob_rows = jnp.exp(scores - log_total[:, None])
    low_probs = to_low(prob_rows)
    prob_grad = contract_cols(out_grad, value_head)
    row_inner = jnp.sum(prob_rows * prob_grad, axis=1, keepdims=True)
    score_grad = to_low(prob_rows * (prob_grad - row_inner))
    query_grad = to_low(matmul(score_grad, key_head) * HD ** (-0.5))
    key_grad = to_low(contract_rows(score_grad, query_head) * HD ** (-0.5))
    value_grad = to_low(contract_rows(low_probs, out_grad))
    return (query_grad, key_grad, value_grad)


def on_device(
    patches,
    cotangent,
    image_lengths,
    image_owner,
    first_gain,
    first_shift,
    query_weight,
    query_bias,
    key_weight,
    value_weight,
    value_bias,
    output_weight,
    output_bias,
    second_gain,
    second_shift,
    expand_weight,
    expand_bias,
    reduce_weight,
    reduce_bias,
):
    dev_count = lax.axis_size("dp")
    my_index = lax.axis_index("dp")
    tok_rows = patches.shape[0]
    width = patches.shape[1]
    cap_rows = 2 * tok_rows
    slot_rows = cap_rows // dev_count
    owners = jnp.arange(dev_count, dtype=jnp.int32)
    base_rows = jnp.sum(
        jnp.where(image_owner[None, :] < owners[:, None], image_lengths[None, :], 0), axis=1
    )
    used_rows = jnp.sum(
        jnp.where(image_owner[None, :] == owners[:, None], image_lengths[None, :], 0), axis=1
    )
    starts = jnp.cumsum(image_lengths) - image_lengths
    stream_pos = jnp.arange(tok_rows, dtype=jnp.int32) * dev_count + my_index
    target = jnp.sum((base_rows[None, :] <= stream_pos[:, None]).astype(jnp.int32), axis=1) - 1
    offset_in = stream_pos - jnp.take(base_rows, target)
    send_slot = target * slot_rows + offset_in // dev_count
    empty_rows = jnp.zeros((cap_rows, width), jnp.bfloat16)
    send_rows = empty_rows.at[send_slot].set(patches)
    send_grads = empty_rows.at[send_slot].set(cotangent)
    recv_rows, recv_grads = (
        lax.all_to_all(send_rows, "dp", split_axis=0, concat_axis=0, tiled=True),
        lax.all_to_all(send_grads, "dp", split_axis=0, concat_axis=0, tiled=True),
    )
    my_base = base_rows[my_index]
    positions = jnp.arange(cap_rows, dtype=jnp.int32)
    source = (my_base + positions) % dev_count
    recv_slot = source * slot_rows + positions // dev_count
    block_rows = jnp.take(recv_rows, recv_slot, axis=0)
    block_grads = jnp.take(recv_grads, recv_slot, axis=0)
    is_valid = positions < used_rows[my_index]
    image_index = (
        jnp.sum((starts[None, :] <= (my_base + positions)[:, None]).astype(jnp.int32), axis=1) - 1
    )
    segment = jnp.where(is_valid, image_index, -1)
    same_image = segment[:, None] == segment[None, :]
    rows_in = block_rows.astype(jnp.float32)
    normed, first_pull = jax.vjp(layer_norm, rows_in, first_gain, first_shift)
    normed_low = to_low(normed)
    query_rows = to_low(matmul(normed_low, query_weight) + query_bias)
    key_rows = to_low(matmul(normed_low, key_weight))
    value_rows = to_low(matmul(normed_low, value_weight) + value_bias)
    local_heads = query_weight.shape[1] // HD
    query_heads = split_heads(query_rows, local_heads)
    key_heads = split_heads(key_rows, local_heads)
    value_heads = split_heads(value_rows, local_heads)

    def forward_head(operands):
        return attend_head(operands[0], operands[1], operands[2], same_image)

    attended_heads, log_totals = lax.map(forward_head, (query_heads, key_heads, value_heads))
    attended = merge_heads(attended_heads)
    branch = lax.psum(contract_cols(attended, output_weight), "tensor") + output_bias
    middle = rows_in + branch
    normed_two, second_pull = jax.vjp(layer_norm, middle, second_gain, second_shift)
    normed_two_low = to_low(normed_two)
    expanded = matmul(normed_two_low, expand_weight) + expand_bias
    hidden, gelu_pull = jax.vjp(gelu_tanh, expanded)
    hidden_low = to_low(hidden)
    branch_two = (
        lax.psum(contract_cols(hidden_low, reduce_weight).astype(jnp.bfloat16), "tensor").astype(
            jnp.float32
        )
        + reduce_bias
    )
    output_rows = middle + branch_two
    grad_rows = block_grads.astype(jnp.float32)
    reduce_grad = contract_rows(block_grads, hidden_low)
    reduce_bias_grad = jnp.sum(grad_rows, axis=0)
    hidden_grad = matmul(block_grads, reduce_weight)
    expanded_grad = to_low(gelu_pull(hidden_grad)[0])
    expand_grad = contract_rows(normed_two_low, expanded_grad)
    expand_bias_grad = jnp.sum(expanded_grad.astype(jnp.float32), axis=0)
    normed_two_grad = lax.psum(contract_cols(expanded_grad, expand_weight), "tensor")
    middle_part, second_gain_grad, second_shift_grad = second_pull(normed_two_grad)
    middle_grad = grad_rows + middle_part
    branch_grad = to_low(middle_grad)
    output_grad = contract_rows(branch_grad, attended)
    output_bias_grad = jnp.sum(branch_grad.astype(jnp.float32), axis=0)
    attended_grad = to_low(matmul(branch_grad, output_weight))
    attended_grad_heads = split_heads(attended_grad, local_heads)

    def backward_head(operands):
        return attend_back(
            operands[0], operands[1], operands[2], operands[3], operands[4], same_image
        )

    query_grad_heads, key_grad_heads, value_grad_heads = lax.map(
        backward_head, (query_heads, key_heads, value_heads, attended_grad_heads, log_totals)
    )
    query_grad = merge_heads(query_grad_heads)
    key_grad = merge_heads(key_grad_heads)
    value_grad = merge_heads(value_grad_heads)
    query_weight_grad = contract_rows(normed_low, query_grad)
    key_weight_grad = contract_rows(normed_low, key_grad)
    value_weight_grad = contract_rows(normed_low, value_grad)
    query_bias_grad = jnp.sum(query_grad.astype(jnp.float32), axis=0)
    value_bias_grad = jnp.sum(value_grad.astype(jnp.float32), axis=0)
    normed_partial = (
        contract_cols(query_grad, query_weight)
        + contract_cols(key_grad, key_weight)
        + contract_cols(value_grad, value_weight)
    )
    normed_grad = lax.psum(normed_partial.astype(jnp.bfloat16), "tensor").astype(jnp.float32)
    input_part, first_gain_grad, first_shift_grad = first_pull(normed_grad)
    input_grad = middle_grad + input_part
    back_rows = empty_rows.at[recv_slot].set(to_low(output_rows))
    back_grads = empty_rows.at[recv_slot].set(to_low(input_grad))
    home_rows, home_grads = (
        lax.all_to_all(back_rows, "dp", split_axis=0, concat_axis=0, tiled=True),
        lax.all_to_all(back_grads, "dp", split_axis=0, concat_axis=0, tiled=True),
    )
    mixed = jnp.take(home_rows, send_slot, axis=0)
    patch_gradient = jnp.take(home_grads, send_slot, axis=0)
    query_share, key_share, value_share, output_share, expand_share, reduce_share = (
        lax.psum_scatter(query_weight_grad, "dp", scatter_dimension=0, tiled=True),
        lax.psum_scatter(key_weight_grad, "dp", scatter_dimension=0, tiled=True),
        lax.psum_scatter(value_weight_grad, "dp", scatter_dimension=0, tiled=True),
        lax.psum_scatter(output_grad, "dp", scatter_dimension=0, tiled=True),
        lax.psum_scatter(expand_grad, "dp", scatter_dimension=0, tiled=True),
        lax.psum_scatter(reduce_grad, "dp", scatter_dimension=0, tiled=True),
    )
    (
        first_gain_sum,
        first_shift_sum,
        query_bias_sum,
        value_bias_sum,
        output_bias_sum,
        second_gain_sum,
        second_shift_sum,
        expand_bias_sum,
        reduce_bias_sum,
    ) = lax.psum(
        (
            first_gain_grad,
            first_shift_grad,
            query_bias_grad,
            value_bias_grad,
            output_bias_grad,
            second_gain_grad,
            second_shift_grad,
            expand_bias_grad,
            reduce_bias_grad,
        ),
        "dp",
    )
    return (
        mixed,
        patch_gradient,
        first_gain_sum,
        first_shift_sum,
        query_share,
        query_bias_sum,
        key_share,
        value_share,
        value_bias_sum,
        output_share,
        output_bias_sum,
        second_gain_sum,
        second_shift_sum,
        expand_share,
        expand_bias_sum,
        reduce_share,
        reduce_bias_sum,
    )


def solution(mesh):
    in_specs = (
        P("dp", None),
        P("dp", None),
        P(),
        P(),
        P(),
        P(),
        P(None, "tensor"),
        P("tensor"),
        P(None, "tensor"),
        P(None, "tensor"),
        P("tensor"),
        P(None, "tensor"),
        P(),
        P(),
        P(),
        P(None, "tensor"),
        P("tensor"),
        P(None, "tensor"),
        P(),
    )
    out_specs = (
        P("dp", None),
        P("dp", None),
        P(),
        P(),
        P("dp", "tensor"),
        P("tensor"),
        P("dp", "tensor"),
        P("dp", "tensor"),
        P("tensor"),
        P("dp", "tensor"),
        P(),
        P(),
        P(),
        P("dp", "tensor"),
        P("tensor"),
        P("dp", "tensor"),
        P(),
    )
    return jax.shard_map(
        on_device, mesh=mesh, in_specs=in_specs, out_specs=out_specs, check_vma=False
    )
```

profile of v0, /device:TPU:0, one launch (start us, length us, event | category | flops | bytes accessed | tf_op | source)
XLA Modules:
  0.0 1141.7 jit_solution(2155769623716502887)
XLA Ops:
  8.9 10.9 compare_and_fusion
  22.3 8.3 all-to-all-start
  34.2 12.6 %all-to-all-done = bf16[16,16,1152]{2,1,0:T(8,128)(2,1)S(1)} async-done(((bf16[16,16,1152]{2,1,0:T(8,128)(2,1)}), bf16[16,16,1152]{2,1,0:T(8,128)(2,1)S(1)}, u32[]{:S(2)}, u32[]{:S(2)}) %all-to-all-start) | async-done | bytes 589856 | tf_op jit(solution)/shard_map/all_to_all | solution.py:121
  59.4 21.5 %while.28 = (s32[]{:T(128)}, bf16[8,256,72]{1,2,0:T(8,128)(2,1)S(1)}, f32[8,256]{1,0:T(8,128)}, bf16[8,256,72]{2,1,0:T(8,128)(2,1)S(1)}, bf16[8,256,72]{2,1,0:T(...) while((s32[]{:T(128)}, ...), condition=%wide.region_11.13_spmd.clone, body=%wide.region_8.12_spmd.clone.sunk | while | flops 19482368 | bytes 1034345 | solution.py:150
  85.2 20.8 %all_to_all.48 = bf16[16,16,1152]{2,1,0:T(8,128)(2,1)S(1)} all-to-all(bf16[16,16,1152]{2,1,0:T(8,128)(2,1)} %bitcast.258), channel_id=1, replica_groups=mesh['dp'=16,'tensor'=2] {'dp'}, dimensions={0} | all-to-all | bytes 1179648 | tf_op jit(solution)/shard_map/all_to_all | solution.py:122
  110.7 4.6 convolution_add_fusion
  122.4 5.7 convolution_convert_fusion.2
  128.1 11.3 all-reduce.14.cloned.1.call-done
  145.2 48.8 %while.29 = (s32[]{:T(128)}, bf16[8,256,72]{1,2,0:T(8,128)(2,1)S(1)}, bf16[8,256,72]{1,2,0:T(8,128)(2,1)S(1)}, bf16[8,256,72]{1,2,0:T(8,128)(2,1)S(1)}, bf16[8,2...) while((s32[]{:T(128)}, ...), condition=%wide.region_23.26_spmd.clone, body=%wide.region_21.25_spmd.clone.sunk | while | flops 47933184 | bytes 2547833 | solution.py:187
  200.0 3.4 fusion.115
  212.7 7.2 fusion.96
  220.3 6.8 fusion.95
  227.8 3.0 scatter_custom_fusion.1
  230.9 6.8 all-to-all-start.1
  240.3 3.6 scatter_custom_fusion.3
  243.9 15.7 %all-to-all-done.1 = bf16[16,16,1152]{2,1,0:T(8,128)(2,1)S(1)} async-done(((bf16[16,16,1152]{2,1,0:T(8,128)(2,1)}), bf16[16,16,1152]{2,1,0:T(8,128)(2,1)S(1)}, u32[]{:S(2)}, u32[]{:S(2)}) %all-to-all-start.1) | async-done | bytes 589856 | tf_op jit(solution)/shard_map/all_to_all | solution.py:209
  259.5 5.0 all-to-all-start.3
  265.1 84.0 %all-reduce.6 = (f32[1152]{0:T(1024)}, f32[1152]{0:T(1024)}, f32[576]{0:T(1024)}, f32[576]{0:T(1024)}, f32[1152]{0:T(1024)}, /*index=5*/f32[1152]{0:T(1024)}, f32[1152]{0:T(1024)}, f32[2152]{0:T(1024)}, f32[1152]{0:T(1024)}) all-reduce(f32[1152]{0:T(1024)S(1)} %get-tuple-element.158, ...), channel_id=1, replica_groups=mesh['dp'=16,'tensor'=2] {'dp'}, use_global_device_ids=true, to_apply=%region_29.32 | all-reduce | flops 10216 | bytes 81728 | tf_op jit(solution)/shard_map/psum | solution.py:232
  351.9 12.0 %reduce-scatter.25.cloned.1.call-done = f32[72,576]{1,0:T(8,128)} async-done(((f32[1152,576]{1,0:T(8,128)}), f32[72,576]{1,0:T(8,128)}) %reduce-scatter.25.cloned.1.call-update) | async-done | bytes 165904
  363.9 135.2 %reduce-scatter.23.cloned.1.call-done = f32[72,576]{1,0:T(8,128)} async-done(((f32[1152,576]{1,0:T(8,128)}), f32[72,576]{1,0:T(8,128)}) %reduce-scatter.23.cloned.1.call-update) | async-done | bytes 165904
  499.1 135.4 %reduce-scatter.21.cloned.1.call-done = f32[72,576]{1,0:T(8,128)} async-done(((f32[1152,576]{1,0:T(8,128)}), f32[72,576]{1,0:T(8,128)}) %reduce-scatter.21.cloned.1.call-update) | async-done | bytes 165904
  634.5 135.5 %reduce-scatter.19.cloned.1.call-done = f32[72,576]{1,0:T(8,128)} async-done(((f32[1152,576]{1,0:T(8,128)}), f32[72,576]{1,0:T(8,128)}) %reduce-scatter.19.cloned.1.call-update) | async-done | bytes 165904
  770.0 182.9 %reduce-scatter.29.cloned.1.call-done = f32[72,2152]{1,0:T(8,128)} async-done(((f32[1152,2152]{1,0:T(8,128)}), f32[72,2152]{1,0:T(8,128)}) %reduce-scatter.29.cloned.1.call-update) | async-done | bytes 619792
  952.9 182.2 %reduce-scatter.27.cloned.1.call-done = f32[72,2152]{1,0:T(8,128)} async-done(((f32[1152,2152]{1,0:T(8,128)}), f32[72,2152]{1,0:T(8,128)}) %reduce-scatter.27.cloned.1.call-update) | async-done | bytes 619792
  (272 shorter events, 133.6 us)
Async XLA Ops:
  7.2 73.7 %copy-start = (bf16[1152,576]{0,1:T(8,128)(2,1)S(1)}, bf16[1152,576]{0,1:T(8,128)(2,1)}, u32[]{:S(2)}) copy-start(bf16[1152,576]{0,1:T(8,128)(2,1)} %param.38) | copy-start | bytes 3981316
  7.2 24.0 %copy-start.33 = (s32[64]{0:T(128)S(1)}, s32[64]{0:T(128)}, u32[]{:S(2)}) copy-start(s32[64]{0:T(128)} %param.29) | copy-start | bytes 772
  19.8 11.4 copy-start.36
  22.3 24.6 %all-to-all-start = ((bf16[16,16,1152]{2,1,0:T(8,128)(2,1)}), bf16[16,16,1152]{2,1,0:T(8,128)(2,1)S(1)}, u32[]{:S(2)}, u32[]{:S(2)}) async-start(bf16[16,16,1152]{2,1,0:T(8,128)(2,1)} %bitcast.32), calls=%async_computation | async-start | bytes 1179648 | tf_op jit(solution)/shard_map/all_to_all | solution.py:121
  30.6 77.7 %all-reduce.12.cloned.1.call-start = ((), (), s32[]{:S(2)}) async-start(), calls=%async_computation.10 | async-start | bytes 2359296 | tf_op jit(solution)/shard_map/psum | solution.py:152
  33.5 13.4 %copy-start.28 = (s32[1024]{0:T(1024)}, s32[1024]{0:T(1024)S(1)}, u32[]{:S(2)}) copy-start(s32[1024]{0:T(1024)S(1)} %pad_clamp_fusion.1) | copy-start | bytes 12292
  49.4 7.6 copy-start.25
  80.9 27.4 %copy-start.12 = (bf16[8,256,72]{2,1,0:T(8,128)(2,1)}, bf16[8,256,72]{2,1,0:T(8,128)(2,1)S(1)}, u32[]{:S(2)}) copy-start(bf16[8,256,72]{2,1,0:T(8,128)(2,1)S(1)} %get-tuple-element.452) | copy-start | bytes 884740
  82.7 56.7 %all-reduce.14.cloned.1.call-start = ((), (), s32[]{:S(2)}) async-start(), calls=%async_computation.11 | async-start | bytes 2359296 | tf_op jit(solution)/shard_map/psum | solution.py:173
  110.0 5.3 slice-start.2
  110.7 8.6 slice-start
  122.1 105.7 %all-reduce.16.cloned.1.call-start = ((), (), s32[]{:S(2)}) async-start(), calls=%async_computation.18 | async-start | bytes 2359296 | tf_op jit(solution)/shard_map/psum | solution.py:160
  194.0 15.2 %copy-start.8 = (bf16[8,256,72]{1,2,0:T(8,128)(2,1)}, bf16[8,256,72]{1,2,0:T(8,128)(2,1)S(1)}, u32[]{:S(2)}) copy-start(bf16[8,256,72]{1,2,0:T(8,128)(2,1)S(1)} %get-tuple-element.113) | copy-start | bytes 884740
  199.0 164.9 %reduce-scatter.25.cloned.1.call-start = ((), (), s32[]{:S(2)}) async-start(), calls=%async_computation.15 | async-start | bytes 3133440
  203.4 295.7 %reduce-scatter.23.cloned.1.call-start = ((), (), s32[]{:S(2)}) async-start(), calls=%async_computation.14 | async-start | bytes 3133440
  206.5 428.0 %reduce-scatter.21.cloned.1.call-start = ((), (), s32[]{:S(2)}) async-start(), calls=%async_computation.13 | async-start | bytes 3133440
  209.1 560.9 %reduce-scatter.19.cloned.1.call-start = ((), (), s32[]{:S(2)}) async-start(), calls=%async_computation.12 | async-start | bytes 3133440
  211.7 741.2 %reduce-scatter.29.cloned.1.call-start = ((), (), s32[]{:S(2)}) async-start(), calls=%async_computation.17 | async-start | bytes 10653696
  220.0 915.2 %reduce-scatter.27.cloned.1.call-start = ((), (), s32[]{:S(2)}) async-start(), calls=%async_computation.16 | async-start | bytes 10653696
  230.9 28.7 %all-to-all-start.1 = ((bf16[16,16,1152]{2,1,0:T(8,128)(2,1)}), bf16[16,16,1152]{2,1,0:T(8,128)(2,1)S(1)}, u32[]{:S(2)}, u32[]{:S(2)}) async-start(bf16[16,16,1152]{2,1,0:T(8,128)(2,1)} %bitcast.259), calls=%async_computation.1 | async-start | bytes 1179648 | tf_op jit(solution)/shard_map/all_to_all | solution.py:209
  243.9 20.7 %copy-start.35 = (s32[128]{0:T(128)S(1)}, s32[128]{0:T(128)}, u32[]{:S(2)}) copy-start(s32[128]{0:T(128)} %get-tuple-element.214) | copy-start | bytes 1540
  243.9 20.7 %copy-start.9 = (bf16[8,256,72]{1,2,0:T(8,128)(2,1)S(1)}, bf16[8,256,72]{1,2,0:T(8,128)(2,1)}, u32[]{:S(2)}) copy-start(bf16[8,256,72]{1,2,0:T(8,128)(2,1)} %copy-done.8) | copy-start | bytes 884740
  259.5 90.4 %all-to-all-start.3 = ((bf16[16,16,1152]{2,1,0:T(8,128)(2,1)}), bf16[16,16,1152]{2,1,0:T(8,128)(2,1)S(1)}, u32[]{:S(2)}, u32[]{:S(2)}) async-start(bf16[16,16,1152]{2,1,0:T(8,128)(2,1)} %bitcast.260), calls=%async_computation.3 | async-start | bytes 1179648 | tf_op jit(solution)/shard_map/all_to_all | solution.py:210
  350.0 785.2 %copy-start.1 = (bf16[1152,576]{0,1:T(8,128)(2,1)S(1)}, bf16[1152,576]{0,1:T(8,128)(2,1)}, u32[]{:S(2)}) copy-start(bf16[1152,576]{0,1:T(8,128)(2,1)} %param.38) | copy-start | bytes 3981316
  (31 other events, 56.4 us)
Sparse Core Ops, SparseCore 0:
  82.8 18.3 all-reduce.11
  122.2 17.1 all-reduce.13
  199.2 21.0 all-reduce.15
  226.5 137.3 reduce-scatter.24
  370.1 128.9 reduce-scatter.22
  505.3 129.1 reduce-scatter.20
  640.9 129.1 reduce-scatter.18
  777.3 175.5 reduce-scatter.28
  959.3 175.8 reduce-scatter.26
where the time goes:
time: 1150 us; the launch traced here: 1140 us
  waiting for transfers between devices  823 us (72%)
  matrix products  107 us (9%)
  blocking collectives  105 us (9%)
  local copies, waits for them, and re-layouts  39.4 us (3%)
  other arithmetic  31.8 us (3%)
  starting transfers between devices  21 us (2%)
  between operations  14.5 us (1%)
    unnamed x15, waiting for transfers between devices  783 us
    psum x1, blocking collectives, on_device(): lax.psum((first_gain_grad, first_shift_grad, query_bias_grad, value_bias_...  84 us
    dot_general x22, matrix products, contract_rows(): lax.dot_general(left_side, right_side, (((0,), (0,)), ((), ())), preferre...  41.6 us
    dot_general x30, matrix products, contract_cols(): lax.dot_general(left_side, right_side, (((1,), (1,)), ((), ())), preferre...  33.8 us
    dot_general x22, matrix products, matmul(): return jnp.dot(left_side, right_side, preferred_element_type=jnp.float32)  31.2 us
  transfers between devices with their start and end apart: 12, of which 9 were waited for; matrix products, arithmetic and copies ran while one was open for 5% of the time, Pallas kernels for 0%

commit v1 on v0

v1 whole, which is shorter than its diff:
```python
import functools

import jax
import jax.numpy as jnp
from jax import lax
from jax.experimental import pallas as pl
from jax.experimental.pallas import tpu as pltpu
from jax.sharding import PartitionSpec as P

HD = 72
masked_score = -1000000000.0
norm_eps = 1e-06
gelu_scale = 0.7978845608028654
gelu_cubic = 0.044715
f32 = jnp.float32
bf16 = jnp.bfloat16
MIB = 1024 * 1024


def dot(left, right):
    return lax.dot_general(left, right, (((1,), (0,)), ((), ())), preferred_element_type=f32)


def dot_cols(left, right):
    return lax.dot_general(left, right, (((1,), (1,)), ((), ())), preferred_element_type=f32)


def dot_rows(left, right):
    return lax.dot_general(left, right, (((0,), (0,)), ((), ())), preferred_element_type=f32)


def iota(shape, dim):
    return lax.broadcasted_iota(jnp.int32, shape, dim).astype(f32)


def row_sum(values):
    return jnp.sum(values, axis=0, keepdims=True)


def lane_sum(values):
    return jnp.sum(values, axis=1, keepdims=True)


def lane_mean(values):
    return jnp.mean(values, axis=1, keepdims=True)


def my_span(lengths, owners, me):
    base = lane_sum(jnp.where(owners < me, lengths, 0.0))
    used = lane_sum(jnp.where(owners == me, lengths, 0.0))
    return base, used


def token_slots(lengths, owners, me, n_dev, tokens, half_rows):
    device = iota((n_dev, lengths.shape[1]), 0)
    base = lane_sum(jnp.where(owners < device, lengths, 0.0))
    pos = iota((1, tokens), 1) * n_dev + me
    below = base <= pos
    target = row_sum(jnp.where(below, 1.0, 0.0)) - 1.0
    start = jnp.max(jnp.where(below, base, -1.0), axis=0, keepdims=True)
    slot = jnp.floor((pos - start) * (1.0 / n_dev))
    half = jnp.floor(slot * (1.0 / half_rows))
    return half, target * half_rows + slot - half * half_rows


def block_slots(base, n_dev, cap, half_rows):
    p = iota((cap, 1), 0)
    pos = base + p
    source = pos - n_dev * jnp.floor(pos * (1.0 / n_dev))
    slot = jnp.floor(p * (1.0 / n_dev))
    half = jnp.floor(slot * (1.0 / half_rows))
    return half, source * half_rows + slot - half * half_rows


def one_hot(index, shape, dim):
    return jnp.where(index == iota(shape, dim), 1.0, 0.0).astype(bf16)


def place():
    return lax.axis_index("dp").astype(f32), lax.axis_index("tensor").astype(f32)


def norm_parts(values):
    centered = values - lane_mean(values)
    scale = lax.rsqrt(lane_mean(centered * centered) + norm_eps)
    return centered * scale, scale


def norm_back(normed, scale, grad, gain):
    inner = grad * gain
    return scale * (inner - lane_mean(inner) - normed * lane_mean(inner * normed))


def gelu_both(values):
    square = values * values
    bent = jnp.tanh(gelu_scale * values * (1.0 + gelu_cubic * square))
    half = 0.5 * (1.0 + bent)
    slope = half + 0.5 * values * (1.0 - bent * bent) * (
        gelu_scale * (1.0 + 3.0 * gelu_cubic * square)
    )
    return values * half, slope


def pack_kernel(n_dev, half_rows, len_ref, own_ref, x_ref, g_ref, send_x, send_g):
    me, core = place()
    half, index = token_slots(
        len_ref[...].astype(f32), own_ref[...].astype(f32), me, n_dev, x_ref.shape[0], half_rows
    )
    index = jnp.where(half == core, index, -1.0)
    pick = one_hot(index, (n_dev * half_rows, x_ref.shape[0]), 0)
    send_x[...] = dot(pick, x_ref[...]).astype(bf16)
    send_g[...] = dot(pick, g_ref[...]).astype(bf16)


def block_pick(len_ref, own_ref, n_dev, cap, half_rows):
    me, core = place()
    base, used = my_span(len_ref[...].astype(f32), own_ref[...].astype(f32), me)
    half, index = block_slots(base, n_dev, cap, half_rows)
    index = jnp.where(half == core, index, index + n_dev * half_rows)
    return one_hot(index, (cap, cap), 1)


def unpack_kernel(n_dev, half_rows, len_ref, own_ref, mine_ref, other_ref, out_ref):
    cap = out_ref.shape[0]
    pick = block_pick(len_ref, own_ref, n_dev, cap, half_rows)
    rows = jnp.concatenate([mine_ref[...], other_ref[...]], axis=0)
    out_ref[...] = dot(pick, rows).astype(bf16)


def image_mask(len_ref, own_ref, cap):
    lengths, owners = len_ref[...].astype(f32), own_ref[...].astype(f32)
    me, _ = place()
    base, used = my_span(lengths, owners, me)
    n_img = lengths.shape[1]
    starts = lane_sum(
        jnp.where(iota((n_img, n_img), 1) < iota((n_img, n_img), 0), lengths, 0.0)
    )
    p = iota((1, cap), 1)
    count = row_sum(jnp.where(starts <= base + p, 1.0, 0.0))
    seg_row = jnp.where(p < used, count, 0.0)
    on_diagonal = iota((cap, cap), 0) == iota((cap, cap), 1)
    seg_col = lane_sum(jnp.where(on_diagonal, seg_row, 0.0))
    return jnp.where(seg_col == seg_row, 1.0, 0.0)


def attend_kernel(
    n_dev, half_rows, len_ref, own_ref, mine_ref, other_ref, gain_ref, shift_ref,
    wq_ref, bq_ref, wk_ref, wv_ref, bv_ref, wo_ref,
    x_ref, h1_ref, q_ref, k_ref, v_ref, log_ref, mask_ref, att_ref, part_ref,
):
    cap = x_ref.shape[0]
    pick = block_pick(len_ref, own_ref, n_dev, cap, half_rows)
    rows = jnp.concatenate([mine_ref[...], other_ref[...]], axis=0)
    x = dot(pick, rows)
    x_ref[...] = x.astype(bf16)
    same = image_mask(len_ref, own_ref, cap)
    mask_ref[...] = same
    normed, _ = norm_parts(x)
    h1 = (normed * gain_ref[...] + shift_ref[...]).astype(bf16)
    h1_ref[...] = h1
    q_ref[...] = (dot(h1, wq_ref[...]) + bq_ref[...]).astype(bf16)
    k_ref[...] = dot(h1, wk_ref[...]).astype(bf16)
    v_ref[...] = (dot(h1, wv_ref[...]) + bv_ref[...]).astype(bf16)
    for h in range(q_ref.shape[1] // HD):
        cols = slice(h * HD, (h + 1) * HD)
        s = dot_cols(q_ref[:, cols], k_ref[:, cols]) * HD ** (-0.5)
        s = jnp.where(same > 0.5, s, masked_score)
        top = jnp.max(s, axis=1, keepdims=True)
        e = jnp.exp(s - top)
        total = lane_sum(e)
        log_ref[:, h : h + 1] = top + jnp.log(total)
        att_ref[:, cols] = dot((e / total).astype(bf16), v_ref[:, cols]).astype(bf16)
    part_ref[...] = dot_cols(att_ref[...], wo_ref[...])


def middle_kernel(x_ref, mine_ref, other_ref, bias_ref, gain_ref, shift_ref, mid_ref, h2_ref):
    middle = x_ref[...].astype(f32) + (mine_ref[...] + other_ref[...] + bias_ref[...])
    mid_ref[...] = middle
    normed, _ = norm_parts(middle)
    h2_ref[...] = (normed * gain_ref[...] + shift_ref[...]).astype(bf16)


def column_chunks(width, step):
    full = width // step
    return full, full * step, width - full * step


def mlp_kernel(h2_ref, g_ref, we_ref, be_ref, wr_ref, out_ref, dh2_ref, be_grad_ref):
    full, done, rest = column_chunks(we_ref.shape[1], 512)
    out_ref[...] = jnp.zeros_like(out_ref)
    dh2_ref[...] = jnp.zeros_like(dh2_ref)

    def chunk(cols):
        we, wr = we_ref[:, cols], wr_ref[:, cols]
        hidden, slope = gelu_both(dot(h2_ref[...], we) + be_ref[:, cols])
        dexp = (dot(g_ref[...], wr) * slope).astype(bf16)
        be_grad_ref[:, cols] = row_sum(dexp.astype(f32))
        out_ref[...] += dot_cols(hidden.astype(bf16), wr)
        dh2_ref[...] += dot_cols(dexp, we)

    @pl.loop(0, full)
    def _(i):
        chunk(pl.ds(pl.multiple_of(i * 512, 512), 512))

    if rest:
        chunk(slice(done, done + rest))


def middle_back_kernel(
    mid_ref, mine_ref, other_ref, g_ref, gain_ref, wo_ref, att_ref,
    dmid_ref, datt_ref, wo_grad_ref, gain_grad_ref, shift_grad_ref, bo_grad_ref, br_grad_ref,
):
    dh2 = mine_ref[...] + other_ref[...]
    normed, scale = norm_parts(mid_ref[...])
    gain_grad_ref[...] = row_sum(dh2 * normed)
    shift_grad_ref[...] = row_sum(dh2)
    g = g_ref[...].astype(f32)
    br_grad_ref[...] = row_sum(g)
    dmid = g + norm_back(normed, scale, dh2, gain_ref[...])
    dmid_ref[...] = dmid
    branch = dmid.astype(bf16)
    bo_grad_ref[...] = row_sum(branch.astype(f32))
    datt_ref[...] = dot(branch, wo_ref[...]).astype(bf16)
    wo_grad_ref[...] = dot_rows(branch, att_ref[...]).astype(bf16)


def attend_back_kernel(
    q_ref, k_ref, v_ref, log_ref, mask_ref, datt_ref, wq_ref, wk_ref, wv_ref,
    dq_ref, dk_ref, dv_ref, part_ref, bq_grad_ref, bv_grad_ref,
):
    same = mask_ref[...] > 0.5
    for h in range(q_ref.shape[1] // HD):
        cols = slice(h * HD, (h + 1) * HD)
        q, k, v, datt = q_ref[:, cols], k_ref[:, cols], v_ref[:, cols], datt_ref[:, cols]
        s = jnp.where(same, dot_cols(q, k) * HD ** (-0.5), masked_score)
        prob = jnp.exp(s - log_ref[:, h : h + 1])
        dprob = dot_cols(datt, v)
        ds = (prob * (dprob - lane_sum(prob * dprob))).astype(bf16)
        dq_ref[:, cols] = (dot(ds, k) * HD ** (-0.5)).astype(bf16)
        dk_ref[:, cols] = (dot_rows(ds, q) * HD ** (-0.5)).astype(bf16)
        dv_ref[:, cols] = dot_rows(prob.astype(bf16), datt).astype(bf16)
    part_ref[...] = (
        dot_cols(dq_ref[...], wq_ref[...])
        + dot_cols(dk_ref[...], wk_ref[...])
        + dot_cols(dv_ref[...], wv_ref[...])
    )
    bq_grad_ref[...] = row_sum(dq_ref[...].astype(f32))
    bv_grad_ref[...] = row_sum(dv_ref[...].astype(f32))


def attend_weights_kernel(h1_ref, dq_ref, dk_ref, dv_ref, wq_ref, wk_ref, wv_ref):
    wq_ref[...] = dot_rows(h1_ref[...], dq_ref[...]).astype(bf16)
    wk_ref[...] = dot_rows(h1_ref[...], dk_ref[...]).astype(bf16)
    wv_ref[...] = dot_rows(h1_ref[...], dv_ref[...]).astype(bf16)


def back_pick(len_ref, own_ref, n_dev, cap, half_rows):
    me, core = place()
    base, _ = my_span(len_ref[...].astype(f32), own_ref[...].astype(f32), me)
    half, index = block_slots(base, n_dev, cap, half_rows)
    index = jnp.where(half == core, index, -1.0)
    return one_hot(index, (cap, n_dev * half_rows), 1)


def out_kernel(n_dev, half_rows, len_ref, own_ref, mid_ref, mine_ref, other_ref, bias_ref, back_ref):
    out = mid_ref[...] + (mine_ref[...] + other_ref[...] + bias_ref[...])
    pick = back_pick(len_ref, own_ref, n_dev, out.shape[0], half_rows)
    back_ref[...] = dot_rows(pick, out.astype(bf16)).astype(bf16)


def first_back_kernel(
    n_dev, half_rows, len_ref, own_ref, x_ref, mine_ref, other_ref, gain_ref, dmid_ref,
    back_ref, gain_grad_ref, shift_grad_ref,
):
    dh1 = mine_ref[...] + other_ref[...]
    normed, scale = norm_parts(x_ref[...].astype(f32))
    gain_grad_ref[...] = row_sum(dh1 * normed)
    shift_grad_ref[...] = row_sum(dh1)
    dx = dmid_ref[...] + norm_back(normed, scale, dh1, gain_ref[...])
    pick = back_pick(len_ref, own_ref, n_dev, dx.shape[0], half_rows)
    back_ref[...] = dot_rows(pick, dx.astype(bf16)).astype(bf16)


def home_kernel(n_dev, half_rows, len_ref, own_ref, mine_ref, other_ref, out_ref):
    me, core = place()
    tokens = out_ref.shape[0]
    half, index = token_slots(
        len_ref[...].astype(f32), own_ref[...].astype(f32), me, n_dev, tokens, half_rows
    )
    index = jnp.where(half == core, index, index + n_dev * half_rows)
    rows = jnp.concatenate([mine_ref[...], other_ref[...]], axis=0)
    pick = one_hot(index, (rows.shape[0], tokens), 0)
    out_ref[...] = dot_rows(pick, rows).astype(bf16)


def mlp_weights_kernel(line, h2_ref, g_ref, *refs):
    n_far = 2 * (line - 1)
    h2_far, g_far = refs[:n_far], refs[n_far : 2 * n_far]
    we_ref, be_ref, wr_ref, wr_grad_ref, we_grad_ref, h2_all, g_all, h2_t, g_t = refs[2 * n_far :]
    cap, width = h2_ref.shape
    part = wr_grad_ref.shape[0]
    for rows, first, far in ((h2_all, h2_ref, h2_far), (g_all, g_ref, g_far)):
        rows[:cap, :] = first[...]
        for i, ref in enumerate(far):
            rows[cap + i * (cap // 2) : cap + (i + 1) * (cap // 2), :] = ref[...]
    share = lax.axis_index("dp") // (lax.axis_size("dp") // line)
    first_row = (share * part).astype(f32)
    pick = one_hot(iota((part, width), 0) + first_row, (part, width), 1)
    h2_t[...] = dot_cols(pick, h2_all[...]).astype(bf16)
    g_t[...] = dot_cols(pick, g_all[...]).astype(bf16)
    full, done, rest = column_chunks(we_ref.shape[1], 256)

    def chunk(cols):
        hidden, slope = gelu_both(dot(h2_all[...], we_ref[:, cols]) + be_ref[:, cols])
        dexp = (dot(g_all[...], wr_ref[:, cols]) * slope).astype(bf16)
        wr_grad_ref[:, cols] = dot(g_t[...], hidden.astype(bf16)).astype(bf16)
        we_grad_ref[:, cols] = dot(h2_t[...], dexp).astype(bf16)

    @pl.loop(0, full)
    def _(i):
        chunk(pl.ds(pl.multiple_of(i * 256, 256), 256))

    if rest:
        chunk(slice(done, done + rest))


def call(kernel, name, outs, *ins, scratch=(), vmem=40):
    return pl.pallas_call(
        kernel,
        name=name,
        out_shape=[jax.ShapeDtypeStruct(shape, dtype) for shape, dtype in outs],
        in_specs=[pl.BlockSpec(memory_space=pltpu.VMEM)] * len(ins),
        out_specs=[pl.BlockSpec(memory_space=pltpu.VMEM)] * len(outs),
        scratch_shapes=list(scratch),
        compiler_params=pltpu.CompilerParams(vmem_limit_bytes=vmem * MIB),
    )(*ins)


def swap_cores(values):
    return lax.ppermute(values, "tensor", [(0, 1), (1, 0)])


def swap_dp(values, flip):
    return lax.ppermute(values, "dp", [(i, i ^ flip) for i in range(lax.axis_size("dp"))])


def spread(rows):
    return lax.all_to_all(rows, "dp", split_axis=0, concat_axis=0, tiled=True)


def scatter_sum(partial, order):
    me = lax.axis_index("dp")
    bits = sorted(order, reverse=True)
    rows = partial.shape[0] // 2 ** len(bits)
    value = partial.reshape((2,) * len(bits) + (rows, partial.shape[1]))
    for step, bit in enumerate(order):
        axis = bits.index(bit)
        bits.remove(bit)
        mine = (me >> bit) & 1
        keep = lax.dynamic_index_in_dim(value, mine, axis, keepdims=False)
        give = lax.dynamic_index_in_dim(value, 1 - mine, axis, keepdims=False)
        total = keep.astype(f32) + swap_dp(give, 1 << bit).astype(f32)
        value = total if step == len(order) - 1 else total.astype(bf16)
    return value


def sum_dp(values):
    flip = 1
    while flip < lax.axis_size("dp"):
        values = values + swap_dp(values, flip)
        flip *= 2
    return values


def on_device(
    patches, cotangent, image_lengths, image_owner, first_gain, first_shift, query_weight,
    query_bias, key_weight, value_weight, value_bias, output_weight, output_bias, second_gain,
    second_shift, expand_weight, expand_bias, reduce_weight, reduce_bias,
):
    n_dev = lax.axis_size("dp")
    tokens, width = patches.shape
    cap = 2 * tokens
    half_rows = cap // n_dev // 2
    heads_width, hidden_width = query_weight.shape[1], expand_weight.shape[1]
    heads = heads_width // HD
    n_bits = n_dev.bit_length() - 1
    line = 4

    def row(vector):
        return vector.reshape(1, -1)

    sizes = (row(image_lengths), row(image_owner))
    half_shape = ((n_dev * half_rows, width), bf16)
    wide32, wide16 = ((cap, width), f32), ((cap, width), bf16)
    head16 = ((cap, heads_width), bf16)
    vector_d, vector_h = ((1, width), f32), ((1, heads_width), f32)
    place_args = (n_dev, half_rows)

    send_x, send_g = call(
        functools.partial(pack_kernel, *place_args), "pack",
        [half_shape, half_shape], *sizes, patches, cotangent,
    )
    recv_x = spread(send_x)
    recv_g = spread(send_g)

    x, h1, q, k, v, logs, mask, attended, branch = call(
        functools.partial(attend_kernel, *place_args), "attend",
        [wide16, wide16, head16, head16, head16, ((cap, heads), f32), ((cap, cap), f32), head16, wide32],
        *sizes, recv_x, swap_cores(recv_x), row(first_gain), row(first_shift),
        query_weight, row(query_bias), key_weight, value_weight, row(value_bias), output_weight,
    )

    (g,) = call(
        functools.partial(unpack_kernel, *place_args), "unpack",
        [wide16], *sizes, recv_g, swap_cores(recv_g),
    )
    core = lax.axis_index("tensor")
    stride = n_dev // line

    def along_line(block):
        half = lax.dynamic_slice_in_dim(block, core * (cap // 2), cap // 2, 0)
        far = [swap_dp(half, stride * i) for i in range(1, line)]
        return far + [swap_cores(rows) for rows in far]

    g_far = along_line(g)

    middle, h2 = call(
        middle_kernel, "middle", [wide32, wide16],
        x, branch, swap_cores(branch), row(output_bias), row(second_gain), row(second_shift),
    )
    h2_far = along_line(h2)
    out_part, dh2, be_grad = call(
        mlp_kernel, "mlp", [wide32, wide32, ((1, hidden_width), f32)],
        h2, g, expand_weight, row(expand_bias), reduce_weight,
    )
    dmid, datt, wo_part, gain2_grad, shift2_grad, bo_grad, br_grad = call(
        middle_back_kernel, "middle_back",
        [wide32, head16, ((width, heads_width), bf16), vector_d, vector_d, vector_d, vector_d],
        middle, dh2, swap_cores(dh2), g, row(second_gain), output_weight, attended,
    )
    dq, dk, dv, dh1, bq_grad, bv_grad = call(
        attend_back_kernel, "attend_back", [head16, head16, head16, wide32, vector_h, vector_h],
        q, k, v, logs, mask, datt, query_weight, key_weight, value_weight,
    )
    wq_part, wk_part, wv_part = call(
        attend_weights_kernel, "attend_weights", [((width, heads_width), bf16)] * 3, h1, dq, dk, dv
    )
    back_grad, gain1_grad, shift1_grad = call(
        functools.partial(first_back_kernel, *place_args), "first_back",
        [half_shape, vector_d, vector_d],
        *sizes, x, dh1, swap_cores(dh1), row(first_gain), dmid,
    )
    (back_out,) = call(
        functools.partial(out_kernel, *place_args), "out", [half_shape],
        *sizes, middle, out_part, swap_cores(out_part), row(reduce_bias),
    )
    home_out = spread(back_out)
    home_grad = spread(back_grad)
    token_shape = ((tokens, width), bf16)
    (mixed,) = call(
        functools.partial(home_kernel, *place_args), "home_out", [token_shape],
        *sizes, home_out, swap_cores(home_out),
    )
    (patch_gradient,) = call(
        functools.partial(home_kernel, *place_args), "home_grad", [token_shape],
        *sizes, home_grad, swap_cores(home_grad),
    )

    wr_part, we_part = call(
        functools.partial(mlp_weights_kernel, line), "mlp_weights",
        [((width // line, hidden_width), bf16)] * 2,
        h2, g, *h2_far, *g_far, expand_weight, row(expand_bias), reduce_weight,
        scratch=[pltpu.VMEM((line * cap, width), bf16)] * 2
        + [pltpu.VMEM((width // line, line * cap), bf16)] * 2,
        vmem=56,
    )

    low_bits, line_bits = list(range(n_bits - 2)), [n_bits - 2, n_bits - 1]
    one_way, other_way = low_bits, low_bits[1::-1] + low_bits[2:]
    wo_sum = scatter_sum(wo_part, one_way + line_bits)
    wv_sum = scatter_sum(wv_part, one_way + line_bits)
    wk_sum = scatter_sum(wk_part, other_way + line_bits)
    wq_sum = scatter_sum(wq_part, line_bits + one_way)
    wr_sum = scatter_sum(wr_part, one_way)
    we_sum = scatter_sum(we_part, other_way)

    vectors = [
        gain1_grad, shift1_grad, bq_grad, bv_grad, bo_grad, gain2_grad, shift2_grad, be_grad, br_grad,
    ]
    total = sum_dp(jnp.concatenate([v.reshape(-1) for v in vectors]))
    sums, at = [], 0
    for vector in vectors:
        sums.append(total[at : at + vector.size])
        at += vector.size
    gain1_sum, shift1_sum, bq_sum, bv_sum, bo_sum, gain2_sum, shift2_sum, be_sum, br_sum = sums
    return (
        mixed, patch_gradient, gain1_sum, shift1_sum, wq_sum, bq_sum, wk_sum, wv_sum, bv_sum,
        wo_sum, bo_sum, gain2_sum, shift2_sum, we_sum, be_sum, wr_sum, br_sum,
    )


def solution(mesh):
    rows, all_same = P("dp", None), P()
    cols, vector = P(None, "tensor"), P("tensor")
    both = P("dp", "tensor")
    in_specs = (
        rows, rows, all_same, all_same, all_same, all_same, cols, vector, cols, cols, vector, cols,
        all_same, all_same, all_same, cols, vector, cols, all_same,
    )
    out_specs = (
        rows, rows, all_same, all_same, both, vector, both, both, vector, both, all_same, all_same,
        all_same, both, vector, both, all_same,
    )
    return jax.shard_map(
        on_device, mesh=mesh, in_specs=in_specs, out_specs=out_specs, check_vma=False
    )
```

time: 1150 us -> 327 us (0.28)
  waiting for transfers between devices: 823 us -> 73.4 us
  matrix products: 107 us -> 0 us
  blocking collectives: 105 us -> 18.8 us
  Pallas kernels: 0 us -> 69 us
  local copies, waits for them, and re-layouts: 39.4 us -> 81.5 us
  starting transfers between devices: 21 us -> 60.2 us
  between operations: 14.5 us -> 1.59 us
    unnamed x15 -> x0, waiting for transfers between devices: 783 us -> none
    dot_general x74 -> x0, matrix products: 107 us -> none  [the longest x22 41.6 us: contract_rows(): lax.dot_general(left_side, right_side, (((0,), (0,)), ((), ())), preferre...]
    psum x1 -> x0, blocking collectives: 84 us -> none  [on_device(): lax.psum((first_gain_grad, first_shift_grad, query_bias_grad, value_bias_...]
    ppermute x0 -> x44, waiting for transfers between devices: none -> 73.4 us  [the longest x30 69 us: swap_dp(): lax.ppermute(values, 'dp', [(i, i ^ flip) for i in range(lax.axis_size('d...]
    pallas_call x0 -> x13, Pallas kernels: none -> 69 us  [call(): pl.pallas_call(kernel, name=name, out_shape=[jax.ShapeDtypeStruct(shape,...]
    unnamed x86 -> x178, local copies, waits for them, and re-layouts: 6.83 us -> 63.4 us
    ppermute x0 -> x44, starting transfers between devices: none -> 47.5 us  [the longest x30 45.3 us: swap_dp(): lax.ppermute(values, 'dp', [(i, i ^ flip) for i in range(lax.axis_size('d...]
    all_to_all x3, waiting for transfers between devices: 28.3 us -> 0.01 us  [spread(): return lax.all_to_all(rows, 'dp', split_axis=0, concat_axis=0, tiled=True)]
  transfers between devices with their start and end apart: 12 -> 47, of which waited for: 9 -> 17; matrix products, arithmetic and copies ran while one was open for 5% -> 20% of each run, Pallas kernels for 0% -> 21%
where the time goes in v1:
time: 327 us; the launch traced here: 325 us
  local copies, waits for them, and re-layouts  81.5 us (25%)
  waiting for transfers between devices  73.4 us (22%)
  Pallas kernels  69 us (21%)
  starting transfers between devices  60.2 us (18%)
  other arithmetic  20.4 us (6%)
  blocking collectives  18.8 us (6%)
    pallas_call x13, Pallas kernels, call(): pl.pallas_call(kernel, name=name, out_shape=[jax.ShapeDtypeStruct(shape,...  69 us
    ppermute x30, waiting for transfers between devices, swap_dp(): lax.ppermute(values, 'dp', [(i, i ^ flip) for i in range(lax.axis_size('d...  69 us
    unnamed x178, local copies, waits for them, and re-layouts  63.4 us
    ppermute x30, starting transfers between devices, swap_dp(): lax.ppermute(values, 'dp', [(i, i ^ flip) for i in range(lax.axis_size('d...  45.3 us
    all_to_all x1, blocking collectives, spread(): return lax.all_to_all(rows, 'dp', split_axis=0, concat_axis=0, tiled=True)  18.8 us
    all_to_all x3, starting transfers between devices, spread(): return lax.all_to_all(rows, 'dp', split_axis=0, concat_axis=0, tiled=True)  12.6 us
    convert_element_type x14, other arithmetic, scatter_sum(): value = total if step == len(order) - 1 else total.astype(bf16)  8.56 us
    pallas_call x9, other arithmetic, call(): pl.pallas_call(kernel, name=name, out_shape=[jax.ShapeDtypeStruct(shape,...  7.2 us
  transfers between devices with their start and end apart: 47, of which 17 were waited for; matrix products, arithmetic and copies ran while one was open for 20% of the time, Pallas kernels for 21%

profile of v1, /device:TPU:0, one launch (start us, length us, event | category | flops | bytes accessed | tf_op | source)
XLA Modules:
  0.0 324.7 jit_solution(16415429284780417263)
XLA Ops:
  5.0 18.8 %all_to_all.44 = bf16[16,8,1152]{2,1,0:T(8,128)(2,1)S(1)} all-to-all(bf16[16,8,1152]{2,1,0:T(8,128)(2,1)S(1)} %bitcast.141), channel_id=1, replica_groups=mesh['dp'=16,'tensor'=2] {'dp'}, dimensions={0} | all-to-all | bytes 589824 | tf_op jit(solution)/shard_map/all_to_all | solution.py:348
  23.8 3.5 %all-to-all-start.1 = ((bf16[16,8,1152]{2,1,0:T(8,128)(2,1)}), bf16[16,8,1152]{2,1,0:T(8,128)(2,1)S(1)}, u32[]{:S(2)}, u32[]{:S(2)}) async-start(bf16[16,8,1152]{2,1,0:T(8,128)(2,1)} %bitcast.4), calls=%async_computation.1 | async-start | bytes 589824 | tf_op jit(solution)/shard_map/all_to_all | solution.py:348
  31.8 2.7 copy.38.wv_ref
  35.8 2.6 copy.39.wo_ref
  43.2 7.3 %attend.1 = (bf16[256,1152]{1,0:T(8,128)(2,1)S(1)}, bf16[256,1152]{1,0:T(8,128)(2,1)S(1)}, bf16[256,576]{1,0:T(8,128)(2,1)S(1)}, bf16[256,576]{1,0:T(8,128)(2,1)...) custom-call(s32[1,64]{1,0:T(1,128)S(1)} %bitcast.143, ...), custom_call_target="tpu_custom_call" | custom-call | tf_op jit(solution)/shard_map/attend/pallas_call | solution.py:328
  67.4 10.6 %collective-permute-done.34.refs_6_ = bf16[128,1152]{1,0:T(8,128)(2,1)S(1)} collective-permute-done((bf16[128,1152]{1,0:T(8,128)(2,1)S(1)}, bf16[128,1152]{1,0:T(8,128)(2,1)S(1)}, u32[]{:S(2)}, u32[]{:S(2)}) %collective-permute-start.34) | collective-permute-done | bytes 294944 | tf_op jit(solution)/shard_map/ppermute | solution.py:344
  78.0 10.3 %collective-permute-done.35.refs_7_ = bf16[128,1152]{1,0:T(8,128)(2,1)} collective-permute-done((bf16[128,1152]{1,0:T(8,128)(2,1)S(1)}, bf16[128,1152]{1,0:T(8,128)(2,1)}, u32[]{:S(2)}, u32[]{:S(2)}) %collective-permute-start.35) | collective-permute-done | bytes 294944 | tf_op jit(solution)/shard_map/ppermute | solution.py:344
  93.6 5.4 %collective-permute-start.28 = (bf16[128,1152]{1,0:T(8,128)(2,1)}, bf16[128,1152]{1,0:T(8,128)(2,1)}, u32[]{:S(2)}, u32[]{:S(2)}) collective-permute-start(bf16[128,1152]{1,0:T(8,128)(2,1)} %constant_dynamic-slice_fusion.1), channel_id=1, source_target_pairs={{0,8},{2,10},{4,12},{6,14},{8,0},{10,2},{12,4},{14,6},{16,24},{18,... | collective-permute-start | bytes 884744 | tf_op jit(solution)/shard_map/ppermute | solution.py:344
  102.1 8.4 %copy.40.we_ref.refs_12_ = bf16[1152,2152]{1,0:T(8,128)(2,1)} copy(bf16[1152,2152]{0,1:T(8,128)(2,1)} %param.34) | data formatting | bytes 9916416 | tf_op args[15]
  111.2 8.4 %copy.41.wr_ref.refs_14_ = bf16[1152,2152]{1,0:T(8,128)(2,1)} copy(bf16[1152,2152]{0,1:T(8,128)(2,1)} %param.36) | data formatting | bytes 9916416 | tf_op args[17]
  125.5 8.9 %mlp.1 = (f32[256,1152]{1,0:T(8,128)}, f32[256,1152]{1,0:T(8,128)}, f32[1,2152]{1,0:T(1,128)S(1)}) custom-call(bf16[256,1152]{1,0:T(8,128)(2,1)S(1)} %copy-done.12, bf16[256,1152]{1,0:T(8,128)(2,1)S(1)} %unpack.1.g_ref, bf16[1152,2152]{1,0:T(8,128)(2,1)S(1)} %copy-done, f32[1,2152]{1,0:T(1,128)S(1)} %reshape.172.be_ref.refs_13_, bf16[1152,2152]{1,0:T(8,128)(2,1)S(1)} %copy-done.1), custom_call_target="tpu_custom_call" | custom-call | tf_op jit(solution)/shard_map/mlp/pallas_call | solution.py:328
  141.2 28.6 %mlp_weights.1 = (bf16[288,2152]{1,0:T(8,128)(2,1)}, bf16[288,2152]{1,0:T(8,128)(2,1)}) custom-call(bf16[256,1152]{1,0:T(8,128)(2,1)} %copy-done.11, bf16[256,1152]{1,0:T(8,128)(2,1)} %copy-done.6, bf16[128,1152]{1,0:T(8,128)(2,1)} %collective-permute-done.28.refs_0_, bf16[128,1152]{1,0:T(8,128)(2,1)} %collective-permute-done.29.refs_1_, ...), custom_call_target="tpu_custom_call" | custom-call | tf_op jit(solution)/shard_map/mlp_weights/pallas_call | solution.py:328
  179.6 4.2 %all-to-all-start.2 = ((bf16[16,8,1152]{2,1,0:T(8,128)(2,1)}), bf16[16,8,1152]{2,1,0:T(8,128)(2,1)}, u32[]{:S(2)}, u32[]{:S(2)}) async-start(bf16[16,8,1152]{2,1,0:T(8,128)(2,1)} %bitcast.140), calls=%async_computation.2 | async-start | bytes 589824 | tf_op jit(solution)/shard_map/all_to_all | solution.py:348
  187.5 3.8 %middle_back.1 = (f32[256,1152]{1,0:T(8,128)S(1)}, bf16[256,576]{1,0:T(8,128)(2,1)S(1)}, bf16[1152,576]{1,0:T(8,128)(2,1)S(1)}, f32[1,1152]{1,0:T(1,128)S(1)}, f...) custom-call(f32[256,1152]{1,0:T(8,128)S(1)} %copy-done.10, ...), custom_call_target="tpu_custom_call" | custom-call | tf_op jit(solution)/shard_map/middle_back/pallas_call | solution.py:328
  193.5 6.6 %attend_back.1 = (bf16[256,576]{1,0:T(8,128)(2,1)S(1)}, bf16[256,576]{1,0:T(8,128)(2,1)S(1)}, bf16[256,576]{1,0:T(8,128)(2,1)S(1)}, f32[256,1152]{1,0:T(8,128)},...) custom-call(bf16[256,576]{1,0:T(8,128)(2,1)S(1)} %copy-done.26, bf16[256,576]{1,0:T(8,128)(2,1)S(1)} %copy-done.28, ...), custom_call_target="tpu_custom_call" | custom-call | tf_op jit(solution)/shard_map/attend_back/pallas_call | solution.py:328
  226.8 20.6 %collective-permute-done.41 = bf16[72,2152]{1,0:T(8,128)(2,1)S(1)} collective-permute-done((bf16[72,2152]{1,0:T(8,128)(2,1)S(1)}, bf16[72,2152]{1,0:T(8,128)(2,1)S(1)}, u32[]{:S(2)}, u32[]{:S(2)}) %collective-permute-start.41) | collective-permute-done | bytes 309920 | tf_op jit(solution)/shard_map/ppermute | solution.py:344
  249.2 6.6 %collective-permute-done.43 = bf16[72,2152]{1,0:T(8,128)(2,1)S(1)} collective-permute-done((bf16[72,2152]{1,0:T(8,128)(2,1)S(1)}, bf16[72,2152]{1,0:T(8,128)(2,1)S(1)}, u32[]{:S(2)}, u32[]{:S(2)}) %collective-permute-start.43) | collective-permute-done | bytes 309920 | tf_op jit(solution)/shard_map/ppermute | solution.py:344
  259.9 2.5 collective-permute-start.13
  265.7 9.9 %collective-permute-done.24 = bf16[2,2,2,72,576]{4,3,0,1,2:T(8,128)(2,1)} collective-permute-done((bf16[2,2,2,72,576]{4,3,0,1,2:T(8,128)(2,1)}, bf16[2,2,2,72,576]{4,3,0,1,2:T(8,128)(2,1)}, u32[]{:S(2)}, u32[]{:S(2)}) %collective-permute-start.24) | collective-permute-done | bytes 663584 | tf_op jit(solution)/shard_map/ppermute | solution.py:344
  285.4 4.0 %collective-permute-done.25 = bf16[2,2,72,576]{3,2,0,1:T(8,128)(2,1)S(1)} collective-permute-done((bf16[2,2,72,576]{3,2,0,1:T(8,128)(2,1)S(1)}, bf16[2,2,72,576]{3,2,0,1:T(8,128)(2,1)S(1)}, u32[]{:S(2)}, u32[]{:S(2)}) %collective-permute-start.25) | collective-permute-done | bytes 331808 | tf_op jit(solution)/shard_map/ppermute | solution.py:344
  297.1 3.2 first_back.1
  300.5 2.5 collective-permute-start.8
  303.1 4.9 %all-to-all-start.3 = ((bf16[16,8,1152]{2,1,0:T(8,128)(2,1)}), bf16[16,8,1152]{2,1,0:T(8,128)(2,1)S(1)}, u32[]{:S(2)}, u32[]{:S(2)}) async-start(bf16[16,8,1152]{2,1,0:T(8,128)(2,1)} %bitcast.8), calls=%async_computation.3 | async-start | bytes 589824 | tf_op jit(solution)/shard_map/all_to_all | solution.py:348
  316.7 2.6 collective-permute-start.11
  (333 shorter events, 136.3 us)
Async XLA Ops:
  23.8 33.2 %all-to-all-start.1 = ((bf16[16,8,1152]{2,1,0:T(8,128)(2,1)}), bf16[16,8,1152]{2,1,0:T(8,128)(2,1)S(1)}, u32[]{:S(2)}, u32[]{:S(2)}) async-start(bf16[16,8,1152]{2,1,0:T(8,128)(2,1)} %bitcast.4), calls=%async_computation.1 | async-start | bytes 589824 | tf_op jit(solution)/shard_map/all_to_all | solution.py:348
  56.5 32.3 %collective-permute-start.1 = (f32[256,1152]{1,0:T(8,128)}, f32[256,1152]{1,0:T(8,128)}, u32[]{:S(2)}, u32[]{:S(2)}) collective-permute-start(f32[256,1152]{1,0:T(8,128)} %get-tuple-element.56.mine_ref), channel_id=1, source_target_pairs={{0,1},{1,0},{2,3},{3,2},{4,5},{5,4},{6,7},{7,6},{8,9},{9,8},{10,11... | collective-permute-start | bytes 3538952 | tf_op jit(solution)/shard_map/ppermute | solution.py:340
  64.8 23.5 %collective-permute-start.35 = (bf16[128,1152]{1,0:T(8,128)(2,1)S(1)}, bf16[128,1152]{1,0:T(8,128)(2,1)}, u32[]{:S(2)}, u32[]{:S(2)}) collective-permute-start(bf16[128,1152]{1,0:T(8,128)(2,1)S(1)} %constant_dynamic-slice_fusion), channel_id=1, source_target_pairs={{0,16},{2,18},{4,20},{6,22},{8,24},{10,26},{12,28},{14,30},{16,0},... | collective-permute-start | bytes 884744 | tf_op jit(solution)/shard_map/ppermute | solution.py:344
  67.2 21.1 %collective-permute-start.36 = (bf16[128,1152]{1,0:T(8,128)(2,1)S(1)}, bf16[128,1152]{1,0:T(8,128)(2,1)}, u32[]{:S(2)}, u32[]{:S(2)}) collective-permute-start(bf16[128,1152]{1,0:T(8,128)(2,1)S(1)} %constant_dynamic-slice_fusion), channel_id=1, source_target_pairs={{0,24},{2,26},{4,28},{6,30},{8,16},{10,18},{12,20},{14,22},{16,8},... | collective-permute-start | bytes 884744 | tf_op jit(solution)/shard_map/ppermute | solution.py:344
  77.9 22.0 %collective-permute-start.37 = (bf16[128,1152]{1,0:T(8,128)(2,1)S(1)}, bf16[128,1152]{1,0:T(8,128)(2,1)S(1)}, u32[]{:S(2)}, u32[]{:S(2)}) collective-permute-start(bf16[128,1152]{1,0:T(8,128)(2,1)S(1)} %collective-permute-done.34.refs_6_), channel_id=1, source_target_pairs={{0,1},{1,0},{2,3},{3,2},{4,5},{5,4},{6,7},{7,6},{8,9},{9,8},{10,11... | collective-permute-start | bytes 884744 | tf_op jit(solution)/shard_map/ppermute | solution.py:340
  88.3 46.7 %collective-permute-start.38 = (bf16[128,1152]{1,0:T(8,128)(2,1)}, bf16[128,1152]{1,0:T(8,128)(2,1)}, u32[]{:S(2)}, u32[]{:S(2)}) collective-permute-start(bf16[128,1152]{1,0:T(8,128)(2,1)} %collective-permute-done.35.refs_7_), channel_id=1, source_target_pairs={{0,1},{1,0},{2,3},{3,2},{4,5},{5,4},{6,7},{7,6},{8,9},{9,8},{10,11... | collective-permute-start | bytes 884744 | tf_op jit(solution)/shard_map/ppermute | solution.py:340
  88.3 46.7 %collective-permute-start.39 = (bf16[128,1152]{1,0:T(8,128)(2,1)}, bf16[128,1152]{1,0:T(8,128)(2,1)}, u32[]{:S(2)}, u32[]{:S(2)}) collective-permute-start(bf16[128,1152]{1,0:T(8,128)(2,1)} %collective-permute-done.36.refs_8_), channel_id=1, source_target_pairs={{0,1},{1,0},{2,3},{3,2},{4,5},{5,4},{6,7},{7,6},{8,9},{9,8},{10,11... | collective-permute-start | bytes 884744 | tf_op jit(solution)/shard_map/ppermute | solution.py:340
  93.6 42.0 %collective-permute-start.28 = (bf16[128,1152]{1,0:T(8,128)(2,1)}, bf16[128,1152]{1,0:T(8,128)(2,1)}, u32[]{:S(2)}, u32[]{:S(2)}) collective-permute-start(bf16[128,1152]{1,0:T(8,128)(2,1)} %constant_dynamic-slice_fusion.1), channel_id=1, source_target_pairs={{0,8},{2,10},{4,12},{6,14},{8,0},{10,2},{12,4},{14,6},{16,24},{18,... | collective-permute-start | bytes 884744 | tf_op jit(solution)/shard_map/ppermute | solution.py:344
  99.0 36.7 %collective-permute-start.29 = (bf16[128,1152]{1,0:T(8,128)(2,1)}, bf16[128,1152]{1,0:T(8,128)(2,1)}, u32[]{:S(2)}, u32[]{:S(2)}) collective-permute-start(bf16[128,1152]{1,0:T(8,128)(2,1)} %constant_dynamic-slice_fusion.1), channel_id=1, source_target_pairs={{0,16},{2,18},{4,20},{6,22},{8,24},{10,26},{12,28},{14,30},{16,0},... | collective-permute-start | bytes 884744 | tf_op jit(solution)/shard_map/ppermute | solution.py:344
  100.6 35.5 %collective-permute-start.30 = (bf16[128,1152]{1,0:T(8,128)(2,1)}, bf16[128,1152]{1,0:T(8,128)(2,1)}, u32[]{:S(2)}, u32[]{:S(2)}) collective-permute-start(bf16[128,1152]{1,0:T(8,128)(2,1)} %constant_dynamic-slice_fusion.1), channel_id=1, source_target_pairs={{0,24},{2,26},{4,28},{6,30},{8,16},{10,18},{12,20},{14,22},{16,8},... | collective-permute-start | bytes 884744 | tf_op jit(solution)/shard_map/ppermute | solution.py:344
  135.0 41.7 %collective-permute-start.3 = (f32[256,1152]{1,0:T(8,128)}, f32[256,1152]{1,0:T(8,128)}, u32[]{:S(2)}, u32[]{:S(2)}) collective-permute-start(f32[256,1152]{1,0:T(8,128)} %get-tuple-element.60.mine_ref), channel_id=1, source_target_pairs={{0,1},{1,0},{2,3},{3,2},{4,5},{5,4},{6,7},{7,6},{8,9},{9,8},{10,11... | collective-permute-start | bytes 3538952 | tf_op jit(solution)/shard_map/ppermute | solution.py:340
  135.0 48.8 %collective-permute-start.5 = (f32[256,1152]{1,0:T(8,128)}, f32[256,1152]{1,0:T(8,128)}, u32[]{:S(2)}, u32[]{:S(2)}) collective-permute-start(f32[256,1152]{1,0:T(8,128)} %get-tuple-element.66.mine_ref), channel_id=1, source_target_pairs={{0,1},{1,0},{2,3},{3,2},{4,5},{5,4},{6,7},{7,6},{8,9},{9,8},{10,11... | collective-permute-start | bytes 3538952 | tf_op jit(solution)/shard_map/ppermute | solution.py:340
  171.8 50.3 %collective-permute-start.40 = (bf16[2,72,2152]{2,1,0:T(8,128)(2,1)}, bf16[2,72,2152]{2,1,0:T(8,128)(2,1)}, u32[]{:S(2)}, u32[]{:S(2)}) collective-permute-start(bf16[2,72,2152]{2,1,0:T(8,128)(2,1)} %dynamic-slice_bitcast_fusion.1), channel_id=1, source_target_pairs={{0,4},{2,6},{4,0},{6,2},{8,12},{10,14},{12,8},{14,10},{16,20},{18,... | collective-permute-start | bytes 1859336 | tf_op jit(solution)/shard_map/ppermute | solution.py:344
  175.2 49.7 %collective-permute-start.42 = (bf16[2,72,2152]{2,1,0:T(8,128)(2,1)}, bf16[2,72,2152]{2,1,0:T(8,128)(2,1)}, u32[]{:S(2)}, u32[]{:S(2)}) collective-permute-start(bf16[2,72,2152]{2,1,0:T(8,128)(2,1)} %dynamic-slice_bitcast_fusion), channel_id=1, source_target_pairs={{0,2},{2,0},{4,6},{6,4},{8,10},{10,8},{12,14},{14,12},{16,18},{18,... | collective-permute-start | bytes 1859336 | tf_op jit(solution)/shard_map/ppermute | solution.py:344
  179.6 78.6 %all-to-all-start.2 = ((bf16[16,8,1152]{2,1,0:T(8,128)(2,1)}), bf16[16,8,1152]{2,1,0:T(8,128)(2,1)}, u32[]{:S(2)}, u32[]{:S(2)}) async-start(bf16[16,8,1152]{2,1,0:T(8,128)(2,1)} %bitcast.140), calls=%async_computation.2 | async-start | bytes 589824 | tf_op jit(solution)/shard_map/all_to_all | solution.py:348
  202.3 94.6 %collective-permute-start.6 = (f32[256,1152]{1,0:T(8,128)}, f32[256,1152]{1,0:T(8,128)S(1)}, u32[]{:S(2)}, u32[]{:S(2)}) collective-permute-start(f32[256,1152]{1,0:T(8,128)} %get-tuple-element.69.mine_ref), channel_id=1, source_target_pairs={{0,1},{1,0},{2,3},{3,2},{4,5},{5,4},{6,7},{7,6},{8,9},{9,8},{10,11... | collective-permute-start | bytes 3538952 | tf_op jit(solution)/shard_map/ppermute | solution.py:340
  214.7 43.5 %collective-permute-start.12 = (bf16[2,2,2,72,576]{4,3,1,2,0:T(8,128)(2,1)}, bf16[2,2,2,72,576]{4,3,1,2,0:T(8,128)(2,1)}, u32[]{:S(2)}, u32[]{:S(2)}) collective-permute-start(bf16[2,2,2,72,576]{4,3,1,2,0:T(8,128)(2,1)} %bitcast.129), channel_id=1, source_target_pairs={{0,8},{2,10},{4,12},{6,14},{8,0},{10,2},{12,4},{14,6},{16,24},{18,... | collective-permute-start | bytes 1990664 | tf_op jit(solution)/shard_map/ppermute | solution.py:344
  218.4 41.4 %collective-permute-start.16 = (bf16[2,2,2,72,576]{4,3,0,1,2:T(8,128)(2,1)}, bf16[2,2,2,72,576]{4,3,0,1,2:T(8,128)(2,1)}, u32[]{:S(2)}, u32[]{:S(2)}) collective-permute-start(bf16[2,2,2,72,576]{4,3,0,1,2:T(8,128)(2,1)} %bitcast.128), channel_id=1, source_target_pairs={{0,4},{2,6},{4,0},{6,2},{8,12},{10,14},{12,8},{14,10},{16,20},{18,... | collective-permute-start | bytes 1990664 | tf_op jit(solution)/shard_map/ppermute | solution.py:344
  222.2 41.5 %collective-permute-start.20 = (bf16[2,2,2,72,576]{4,3,0,1,2:T(8,128)(2,1)}, bf16[2,2,2,72,576]{4,3,0,1,2:T(8,128)(2,1)}, u32[]{:S(2)}, u32[]{:S(2)}) collective-permute-start(bf16[2,2,2,72,576]{4,3,0,1,2:T(8,128)(2,1)} %bitcast.127), channel_id=1, source_target_pairs={{0,2},{2,0},{4,6},{6,4},{8,10},{10,8},{12,14},{14,12},{16,18},{18,... | collective-permute-start | bytes 1990664 | tf_op jit(solution)/shard_map/ppermute | solution.py:344
  224.9 22.5 %collective-permute-start.41 = (bf16[72,2152]{1,0:T(8,128)(2,1)S(1)}, bf16[72,2152]{1,0:T(8,128)(2,1)S(1)}, u32[]{:S(2)}, u32[]{:S(2)}) collective-permute-start(bf16[72,2152]{1,0:T(8,128)(2,1)S(1)} %dynamic-slice_bitcast_fusion.7), channel_id=1, source_target_pairs={{0,2},{2,0},{4,6},{6,4},{8,10},{10,8},{12,14},{14,12},{16,18},{18,... | collective-permute-start | bytes 929672 | tf_op jit(solution)/shard_map/ppermute | solution.py:344
  255.8 19.7 %collective-permute-start.24 = (bf16[2,2,2,72,576]{4,3,0,1,2:T(8,128)(2,1)}, bf16[2,2,2,72,576]{4,3,0,1,2:T(8,128)(2,1)}, u32[]{:S(2)}, u32[]{:S(2)}) collective-permute-start(bf16[2,2,2,72,576]{4,3,0,1,2:T(8,128)(2,1)} %bitcast.126), channel_id=1, source_target_pairs={{0,2},{2,0},{4,6},{6,4},{8,10},{10,8},{12,14},{14,12},{16,18},{18,... | collective-permute-start | bytes 1990664 | tf_op jit(solution)/shard_map/ppermute | solution.py:344
  258.2 20.2 %collective-permute-start.4 = (bf16[128,1152]{1,0:T(8,128)(2,1)}, bf16[128,1152]{1,0:T(8,128)(2,1)S(1)}, u32[]{:S(2)}, u32[]{:S(2)}) collective-permute-start(bf16[128,1152]{1,0:T(8,128)(2,1)} %bitcast.7.mine_ref), channel_id=1, source_target_pairs={{0,1},{1,0},{2,3},{3,2},{4,5},{5,4},{6,7},{7,6},{8,9},{9,8},{10,11... | collective-permute-start | bytes 884744 | tf_op jit(solution)/shard_map/ppermute | solution.py:340
  259.9 21.4 %collective-permute-start.13 = (bf16[2,2,72,576]{3,2,0,1:T(8,128)(2,1)S(1)}, bf16[2,2,72,576]{3,2,0,1:T(8,128)(2,1)S(1)}, u32[]{:S(2)}, u32[]{:S(2)}) collective-permute-start(bf16[2,2,72,576]{3,2,0,1:T(8,128)(2,1)S(1)} %dynamic-slice_bitcast_fusion.5), channel_id=1, source_target_pairs={{0,16},{2,18},{4,20},{6,22},{8,24},{10,26},{12,28},{14,30},{16,0},... | collective-permute-start | bytes 995336 | tf_op jit(solution)/shard_map/ppermute | solution.py:344
  290.3 19.7 %collective-permute-start.15 = (bf16[72,576]{1,0:T(8,128)(2,1)S(1)}, bf16[72,576]{1,0:T(8,128)(2,1)S(1)}, u32[]{:S(2)}, u32[]{:S(2)}) collective-permute-start(bf16[72,576]{1,0:T(8,128)(2,1)S(1)} %dynamic-slice_bitcast_fusion.15), channel_id=1, source_target_pairs={{0,4},{2,6},{4,0},{6,2},{8,12},{10,14},{12,8},{14,10},{16,20},{18,... | collective-permute-start | bytes 248840 | tf_op jit(solution)/shard_map/ppermute | solution.py:344
  (109 other events, 699.5 us)

commit v2 on v1

v2 whole, which is shorter than its diff:
```python
import functools

import jax
import jax.numpy as jnp
from jax import lax
from jax.experimental import pallas as pl
from jax.experimental.pallas import tpu as pltpu
from jax.sharding import PartitionSpec as P

HD = 72
masked_score = -1000000000.0
norm_eps = 1e-06
gelu_scale = 0.7978845608028654
gelu_cubic = 0.044715
f32 = jnp.float32
bf16 = jnp.bfloat16
MIB = 1024 * 1024


def dot(left, right):
    return lax.dot_general(left, right, (((1,), (0,)), ((), ())), preferred_element_type=f32)


def dot_cols(left, right):
    return lax.dot_general(left, right, (((1,), (1,)), ((), ())), preferred_element_type=f32)


def dot_rows(left, right):
    return lax.dot_general(left, right, (((0,), (0,)), ((), ())), preferred_element_type=f32)


def iota(shape, dim):
    return lax.broadcasted_iota(jnp.int32, shape, dim).astype(f32)


def row_sum(values):
    return jnp.sum(values, axis=0, keepdims=True)


def lane_sum(values):
    return jnp.sum(values, axis=1, keepdims=True)


def lane_mean(values):
    return jnp.mean(values, axis=1, keepdims=True)


def my_span(lengths, owners, me):
    base = lane_sum(jnp.where(owners < me, lengths, 0.0))
    used = lane_sum(jnp.where(owners == me, lengths, 0.0))
    return base, used


def token_slots(lengths, owners, me, n_dev, tokens, half_rows):
    device = iota((n_dev, lengths.shape[1]), 0)
    base = lane_sum(jnp.where(owners < device, lengths, 0.0))
    pos = iota((1, tokens), 1) * n_dev + me
    below = base <= pos
    target = row_sum(jnp.where(below, 1.0, 0.0)) - 1.0
    start = jnp.max(jnp.where(below, base, -1.0), axis=0, keepdims=True)
    slot = jnp.floor((pos - start) * (1.0 / n_dev))
    half = jnp.floor(slot * (1.0 / half_rows))
    return half, target * half_rows + slot - half * half_rows


def block_slots(base, n_dev, cap, half_rows):
    p = iota((cap, 1), 0)
    pos = base + p
    source = pos - n_dev * jnp.floor(pos * (1.0 / n_dev))
    slot = jnp.floor(p * (1.0 / n_dev))
    half = jnp.floor(slot * (1.0 / half_rows))
    return half, source * half_rows + slot - half * half_rows


def one_hot(index, shape, dim):
    return jnp.where(index == iota(shape, dim), 1.0, 0.0).astype(bf16)


def lane_pad(size):
    return -(-size // 128) * 128


def place():
    return lax.axis_index("dp").astype(f32), lax.axis_index("tensor").astype(f32)


def norm_parts(values):
    centered = values - lane_mean(values)
    scale = lax.rsqrt(lane_mean(centered * centered) + norm_eps)
    return centered * scale, scale


def norm_back(normed, scale, grad, gain):
    inner = grad * gain
    return scale * (inner - lane_mean(inner) - normed * lane_mean(inner * normed))


def gelu_both(values):
    square = values * values
    bent = jnp.tanh(gelu_scale * values * (1.0 + gelu_cubic * square))
    half = 0.5 * (1.0 + bent)
    slope = half + 0.5 * values * (1.0 - bent * bent) * (
        gelu_scale * (1.0 + 3.0 * gelu_cubic * square)
    )
    return values * half, slope


def flip_of(block, order):
    flip = 0 * block
    for step, bit in enumerate(order):
        flip = flip | (((block >> (len(order) - 1 - step)) & 1) << bit)
    return flip


def feature_pick(rows, width, n_dev, order):
    owner_rows = width // n_dev
    i = iota((rows, 1), 0)
    block = jnp.floor((i + 0.5) * (1.0 / owner_rows))
    owner = flip_of(block.astype(jnp.int32), order) ^ lax.axis_index("dp")
    return one_hot(owner.astype(f32) * owner_rows + (i - block * owner_rows), (rows, width), 1)


def pack_kernel(n_dev, half_rows, len_ref, own_ref, x_ref, g_ref, send_ref):
    me, core = place()
    half, index = token_slots(
        len_ref[...].astype(f32), own_ref[...].astype(f32), me, n_dev, x_ref.shape[0], half_rows
    )
    target = jnp.floor(index * (1.0 / half_rows))
    index = jnp.where(half == core, index + target * half_rows, -1e6)
    shape = (2 * n_dev * half_rows, x_ref.shape[0])
    rows = dot(one_hot(index, shape, 0), x_ref[...])
    rows += dot(one_hot(index + half_rows, shape, 0), g_ref[...])
    send_ref[...] = rows.astype(bf16)


def block_pick(len_ref, own_ref, n_dev, cap, half_rows, kind):
    me, core = place()
    base, _ = my_span(len_ref[...].astype(f32), own_ref[...].astype(f32), me)
    half, index = block_slots(base, n_dev, cap, half_rows)
    source = jnp.floor(index * (1.0 / half_rows))
    index = index + (source + kind) * half_rows
    index = jnp.where(half == core, index, index + 2 * n_dev * half_rows)
    return one_hot(index, (cap, 2 * cap), 1)


def unpack_kernel(n_dev, half_rows, len_ref, own_ref, mine_ref, other_ref, out_ref):
    cap = out_ref.shape[0]
    pick = block_pick(len_ref, own_ref, n_dev, cap, half_rows, 1)
    rows = jnp.concatenate([mine_ref[...], other_ref[...]], axis=0)
    out_ref[...] = dot(pick, rows).astype(bf16)


def image_mask(len_ref, own_ref, cap):
    lengths, owners = len_ref[...].astype(f32), own_ref[...].astype(f32)
    me, _ = place()
    base, used = my_span(lengths, owners, me)
    n_img = lengths.shape[1]
    starts = lane_sum(
        jnp.where(iota((n_img, n_img), 1) < iota((n_img, n_img), 0), lengths, 0.0)
    )
    p = iota((1, cap), 1)
    count = row_sum(jnp.where(starts <= base + p, 1.0, 0.0))
    seg_row = jnp.where(p < used, count, 0.0)
    on_diagonal = iota((cap, cap), 0) == iota((cap, cap), 1)
    seg_col = lane_sum(jnp.where(on_diagonal, seg_row, 0.0))
    return jnp.where(seg_col == seg_row, 1.0, 0.0)


class Vectors:
    def __init__(self, width, heads_width, hidden_width):
        self.at = {}
        end = 0
        for name, size in (
            ("gain1", width), ("shift1", width), ("bo", width), ("gain2", width),
            ("shift2", width), ("br", width), ("be", hidden_width), ("bq", heads_width),
            ("bv", heads_width),
        ):
            self.at[name] = slice(end, end + size)
            end += lane_pad(size)
        self.size = end


def attend_kernel(
    n_dev, half_rows, vec, len_ref, own_ref, mine_ref, other_ref, vec_ref,
    wq_ref, wk_ref, wv_ref, wo_ref,
    x_ref, h1_ref, q_ref, k_ref, v_ref, log_ref, mask_ref, att_ref, part_ref,
):
    cap = x_ref.shape[0]
    pick = block_pick(len_ref, own_ref, n_dev, cap, half_rows, 0)
    rows = jnp.concatenate([mine_ref[...], other_ref[...]], axis=0)
    x = dot(pick, rows)
    x_ref[...] = x.astype(bf16)
    same = image_mask(len_ref, own_ref, cap)
    mask_ref[...] = same
    normed, _ = norm_parts(x)
    h1 = (normed * vec_ref[:, vec.at["gain1"]] + vec_ref[:, vec.at["shift1"]]).astype(bf16)
    h1_ref[...] = h1
    q_ref[...] = (dot_cols(h1, wq_ref[...]) + vec_ref[:, vec.at["bq"]]).astype(bf16)
    k_ref[...] = dot_cols(h1, wk_ref[...]).astype(bf16)
    v_ref[...] = (dot_cols(h1, wv_ref[...]) + vec_ref[:, vec.at["bv"]]).astype(bf16)
    for h in range(q_ref.shape[1] // HD):
        cols = slice(h * HD, (h + 1) * HD)
        s = dot_cols(q_ref[:, cols], k_ref[:, cols]) * HD ** (-0.5)
        s = jnp.where(same > 0.5, s, masked_score)
        top = jnp.max(s, axis=1, keepdims=True)
        e = jnp.exp(s - top)
        total = lane_sum(e)
        log_ref[:, h : h + 1] = top + jnp.log(total)
        att_ref[:, cols] = dot((e / total).astype(bf16), v_ref[:, cols]).astype(bf16)
    part_ref[...] = dot(att_ref[...], wo_ref[...])


def middle_kernel(vec, x_ref, mine_ref, other_ref, vec_ref, mid_ref, h2_ref, h2_half_ref):
    middle = x_ref[...].astype(f32) + (
        mine_ref[...] + other_ref[...] + vec_ref[:, vec.at["bo"]]
    )
    mid_ref[...] = middle
    normed, _ = norm_parts(middle)
    h2_ref[...] = (
        normed * vec_ref[:, vec.at["gain2"]] + vec_ref[:, vec.at["shift2"]]
    ).astype(bf16)
    rows = h2_half_ref.shape[0]
    start = lax.axis_index("tensor") * rows
    h2_half_ref[...] = h2_ref[pl.ds(pl.multiple_of(start, rows), rows), :]


def chunks_of(width, step):
    full = width // step
    return full, full * step, width - full * step


def mlp_kernel(vec, h2_ref, g_ref, we_ref, vec_ref, wr_ref, out_ref, dh2_ref, be_grad_ref):
    step = 512
    full, done, rest = chunks_of(we_ref.shape[0], step)
    first = vec.at["be"].start
    out_ref[...] = jnp.zeros_like(out_ref)
    dh2_ref[...] = jnp.zeros_like(dh2_ref)
    be_grad_ref[...] = jnp.zeros_like(be_grad_ref)

    def chunk(rows, lanes, bias):
        we, wr = we_ref[rows, :], wr_ref[rows, :]
        hidden, slope = gelu_both(dot_cols(h2_ref[...], we) + vec_ref[:, bias])
        dexp = (dot_cols(g_ref[...], wr) * slope).astype(bf16)
        be_grad_ref[:, lanes] = row_sum(dexp.astype(f32))
        out_ref[...] += dot(hidden.astype(bf16), wr)
        dh2_ref[...] += dot(dexp, we)

    @pl.loop(0, full)
    def _(i):
        at = pl.multiple_of(i * step, step)
        lanes = pl.ds(at, step)
        chunk(lanes, lanes, pl.ds(pl.multiple_of(first + at, 128), step))

    if rest:
        lanes = slice(done, done + rest)
        chunk(lanes, lanes, slice(first + done, first + done + rest))


def middle_back_kernel(
    vec, mid_ref, mine_ref, other_ref, g_ref, vec_ref, wo_ref,
    dmid_ref, branch_ref, datt_ref, vec_grad_ref,
):
    width = mid_ref.shape[1]
    dh2 = mine_ref[...] + other_ref[...]
    normed, scale = norm_parts(mid_ref[...])
    g = g_ref[...].astype(f32)
    dmid = g + norm_back(normed, scale, dh2, vec_ref[:, vec.at["gain2"]])
    dmid_ref[...] = dmid
    branch = dmid.astype(bf16)
    branch_ref[...] = branch
    datt_ref[...] = dot_cols(branch, wo_ref[...]).astype(bf16)
    sums = [branch.astype(f32), dh2 * normed, dh2, g]
    for i, values in enumerate(sums):
        vec_grad_ref[:, i * width : (i + 1) * width] = row_sum(values)


def attend_back_kernel(
    q_ref, k_ref, v_ref, log_ref, mask_ref, datt_ref, wq_ref, wk_ref, wv_ref,
    dq_ref, dk_ref, dv_ref, part_ref, vec_grad_ref,
):
    same = mask_ref[...] > 0.5
    heads_width = q_ref.shape[1]
    for h in range(heads_width // HD):
        cols = slice(h * HD, (h + 1) * HD)
        q, k, v, datt = q_ref[:, cols], k_ref[:, cols], v_ref[:, cols], datt_ref[:, cols]
        s = jnp.where(same, dot_cols(q, k) * HD ** (-0.5), masked_score)
        prob = jnp.exp(s - log_ref[:, h : h + 1])
        dprob = dot_cols(datt, v)
        ds = (prob * (dprob - lane_sum(prob * dprob))).astype(bf16)
        dq_ref[:, cols] = (dot(ds, k) * HD ** (-0.5)).astype(bf16)
        dk_ref[:, cols] = (dot_rows(ds, q) * HD ** (-0.5)).astype(bf16)
        dv_ref[:, cols] = dot_rows(prob.astype(bf16), datt).astype(bf16)
    part_ref[...] = (
        dot(dq_ref[...], wq_ref[...])
        + dot(dk_ref[...], wk_ref[...])
        + dot(dv_ref[...], wv_ref[...])
    )
    vec_grad_ref[...] = jnp.zeros_like(vec_grad_ref)
    vec_grad_ref[:, :heads_width] = row_sum(dq_ref[...].astype(f32))
    second = lane_pad(heads_width)
    vec_grad_ref[:, second : second + heads_width] = row_sum(dv_ref[...].astype(f32))


def put_transposed(turned_ref, out_ref, values, n_dev, order):
    width = values.shape[1]
    owner_rows = width // n_dev
    if owner_rows % 8:
        out_ref[...] = dot_cols(feature_pick(width, width, n_dev, order), values)
        return
    me = lax.axis_index("dp")
    for block in range(n_dev):
        start = pl.multiple_of((me ^ flip_of(block, order)) * owner_rows, 8)
        rows = slice(block * owner_rows, (block + 1) * owner_rows)
        out_ref[rows, :] = turned_ref[pl.ds(start, owner_rows), :]


def attend_weights_kernel(
    n_dev, orders, h1_ref, branch_ref, dq_ref, dk_ref, dv_ref, att_ref, *refs
):
    (turned_ref, turned_branch, left_ref, branch_left_ref), outs = refs[-4:], refs[:-4]
    heads_width = dq_ref.shape[1]
    total = 4 * heads_width // len(orders)
    half = h1_ref.shape[1] // 2
    turned_ref[...] = jnp.transpose(h1_ref[...].astype(f32))
    turned_branch[...] = jnp.transpose(branch_ref[...].astype(f32))
    right = [dq_ref, dk_ref, dv_ref, att_ref]
    for group, order in enumerate(orders):
        put_transposed(turned_ref, left_ref, h1_ref[...], n_dev, order)
        keep_ref, give_ref = outs[2 * group], outs[2 * group + 1]
        for i, ref in enumerate(right):
            first = max(i * heads_width, group * total)
            last = min((i + 1) * heads_width, (group + 1) * total)
            if first >= last:
                continue
            if i == 3:
                put_transposed(turned_branch, branch_left_ref, branch_ref[...], n_dev, order)
            left = (branch_left_ref if i == 3 else left_ref)[...].astype(bf16)
            cols = ref[:, first - i * heads_width : last - i * heads_width]
            product = dot(left, cols).astype(bf16)
            lanes = slice(first - group * total, last - group * total)
            keep_ref[:, lanes] = product[:half, :]
            give_ref[:, lanes] = product[half:, :]


def back_slots(len_ref, own_ref, n_dev, cap, half_rows):
    me, core = place()
    base, _ = my_span(len_ref[...].astype(f32), own_ref[...].astype(f32), me)
    half, index = block_slots(base, n_dev, cap, half_rows)
    source = jnp.floor(index * (1.0 / half_rows))
    return jnp.where(half == core, index + source * half_rows, -1e6)


def first_back_kernel(
    n_dev, half_rows, vec, len_ref, own_ref, x_ref, mine_ref, other_ref, vec_ref, dmid_ref,
    mid_ref, out_mine_ref, out_other_ref, back_ref, vec_grad_ref,
):
    width = x_ref.shape[1]
    cap = x_ref.shape[0]
    dh1 = mine_ref[...] + other_ref[...]
    normed, scale = norm_parts(x_ref[...].astype(f32))
    vec_grad_ref[:, :width] = row_sum(dh1 * normed)
    vec_grad_ref[:, width:] = row_sum(dh1)
    dx = dmid_ref[...] + norm_back(normed, scale, dh1, vec_ref[:, vec.at["gain1"]])
    out = mid_ref[...] + (
        out_mine_ref[...] + out_other_ref[...] + vec_ref[:, vec.at["br"]]
    )
    index = back_slots(len_ref, own_ref, n_dev, cap, half_rows)
    rows = dot_rows(one_hot(index, (cap, cap), 1), out.astype(bf16))
    rows += dot_rows(one_hot(index + half_rows, (cap, cap), 1), dx.astype(bf16))
    back_ref[...] = rows.astype(bf16)


def home_kernel(n_dev, half_rows, len_ref, own_ref, mine_ref, other_ref, out_ref, grad_ref):
    me, core = place()
    tokens = out_ref.shape[0]
    half, index = token_slots(
        len_ref[...].astype(f32), own_ref[...].astype(f32), me, n_dev, tokens, half_rows
    )
    index = index + jnp.floor(index * (1.0 / half_rows)) * half_rows
    index = jnp.where(half == core, index, index + 2 * n_dev * half_rows)
    rows = jnp.concatenate([mine_ref[...], other_ref[...]], axis=0)
    shape = (rows.shape[0], tokens)
    out_ref[...] = dot_rows(one_hot(index, shape, 0), rows).astype(bf16)
    grad_ref[...] = dot_rows(one_hot(index + half_rows, shape, 0), rows).astype(bf16)


def mlp_weights_kernel(
    flips, orders, n_dev, half_rows, vec, len_ref, own_ref, h2_ref, h2_mine_ref, h2_other_ref, g_ref,
    g_mine_ref, g_other_ref, we_ref, vec_ref, wr_ref, wr_keep, wr_give, we_keep, we_give,
    h2_all, g_all, h2_t, g_t,
):
    cap, width = h2_ref.shape
    hidden_width = we_ref.shape[0]
    half_cap = cap // 2
    me = lax.axis_index("dp")
    _, core = place()
    lengths, owners = len_ref[...].astype(f32), own_ref[...].astype(f32)
    h2_all[:cap, :] = h2_ref[...]
    g_all[:cap, :] = g_ref[...]
    for i, flip in enumerate(flips):
        far = slice(i * half_cap, (i + 1) * half_cap)
        rows = slice((i + 1) * cap, (i + 2) * cap)
        h2_all[rows, :] = jnp.concatenate([h2_mine_ref[far, :], h2_other_ref[far, :]], axis=0)
        base, _ = my_span(lengths, owners, (me ^ flip).astype(f32))
        half, index = block_slots(base, n_dev, cap, half_rows)
        index = jnp.where(half == core, index, index + half_cap)
        index = jnp.where(core == 0.0, index, jnp.concatenate([index[half_cap:], index[:half_cap]]))
        g_rows = jnp.concatenate([g_mine_ref[far, :], g_other_ref[far, :]], axis=0)
        g_all[rows, :] = dot(one_hot(index, (cap, cap), 1), g_rows).astype(bf16)
    part = h2_t.shape[0]
    g_t[...] = dot_cols(feature_pick(part, width, n_dev, orders[0]), g_all[...]).astype(bf16)
    h2_t[...] = dot_cols(feature_pick(part, width, n_dev, orders[1]), h2_all[...]).astype(bf16)
    step = 256
    full, done, rest = chunks_of(hidden_width, step)
    first = vec.at["be"].start

    def chunk(rows, lanes, bias):
        we, wr = we_ref[rows, :], wr_ref[rows, :]
        hidden, slope = gelu_both(dot_cols(h2_all[...], we) + vec_ref[:, bias])
        dexp = (dot_cols(g_all[...], wr) * slope).astype(bf16)
        wr_grad = dot(g_t[...], hidden.astype(bf16)).astype(bf16)
        wr_keep[:, lanes] = wr_grad[: part // 2, :]
        wr_give[:, lanes] = wr_grad[part // 2 :, :]
        we_grad = dot(h2_t[...], dexp).astype(bf16)
        we_keep[:, lanes] = we_grad[: part // 2, :]
        we_give[:, lanes] = we_grad[part // 2 :, :]

    @pl.loop(0, full)
    def _(i):
        at = pl.multiple_of(i * step, step)
        chunk(pl.ds(at, step), pl.ds(at, step), pl.ds(pl.multiple_of(first + at, 128), step))

    if rest:
        end = done + rest
        chunk(slice(done, end), slice(done, end), slice(first + done, first + end))


def turn_kernel(*refs):
    count = len(refs) // 4
    for i in range(count):
        total = refs[2 * i][...].astype(f32) + refs[2 * i + 1][...].astype(f32)
        half = total.shape[0] // 2
        refs[2 * count + 2 * i][...] = total[:half, :]
        refs[2 * count + 2 * i + 1][...] = total[half:, :].astype(bf16)


def last_kernel(heads_width, *refs):
    count = (len(refs) - 4) // 2
    total = 4 * heads_width // count
    for group in range(count):
        value = refs[2 * group][...].astype(f32) + refs[2 * group + 1][...].astype(f32)
        for i, ref in enumerate(refs[2 * count :]):
            first = max(i * heads_width, group * total)
            last = min((i + 1) * heads_width, (group + 1) * total)
            if first < last:
                lanes = slice(first - i * heads_width, last - i * heads_width)
                ref[:, lanes] = value[:, first - group * total : last - group * total]


def call(kernel, name, outs, *ins, scratch=(), vmem=16):
    return pl.pallas_call(
        kernel,
        name=name,
        out_shape=[jax.ShapeDtypeStruct(shape, dtype) for shape, dtype in outs],
        in_specs=[pl.BlockSpec(memory_space=pltpu.VMEM)] * len(ins),
        out_specs=[pl.BlockSpec(memory_space=pltpu.VMEM)] * len(outs),
        scratch_shapes=list(scratch),
        compiler_params=pltpu.CompilerParams(vmem_limit_bytes=vmem * MIB),
    )(*ins)


def swap_cores(values):
    return lax.ppermute(values, "tensor", [(0, 1), (1, 0)])


def swap_dp(values, flip):
    return lax.ppermute(values, "dp", [(i, i ^ flip) for i in range(lax.axis_size("dp"))])


def spread(rows):
    return lax.all_to_all(rows, "dp", split_axis=0, concat_axis=0, tiled=True)


def after(values, earlier):
    return lax.optimization_barrier((values, earlier))[0]


def turn(name, pairs):
    rows = pairs[0][0].shape[0] // 2
    if rows % 8:
        totals = [keep.astype(f32) + got.astype(f32) for keep, got in pairs]
        return [(total[:rows], total[rows:].astype(bf16)) for total in totals]
    outs = []
    for keep, _ in pairs:
        shape = (rows, keep.shape[1])
        outs += [(shape, f32), (shape, bf16)]
    flat = call(turn_kernel, name, outs, *[values for pair in pairs for values in pair])
    return list(zip(flat[::2], flat[1::2]))


def sum_dp(values):
    flip = 1
    while flip < lax.axis_size("dp"):
        values = values + swap_dp(values, flip)
        flip *= 2
    return values


def on_device(
    patches, cotangent, image_lengths, image_owner, first_gain, first_shift, query_weight,
    query_bias, key_weight, value_weight, value_bias, output_weight, output_bias, second_gain,
    second_shift, expand_weight, expand_bias, reduce_weight, reduce_bias,
):
    n_dev = lax.axis_size("dp")
    tokens, width = patches.shape
    cap = 2 * tokens
    half_rows = cap // n_dev // 2
    heads_width, hidden_width = query_weight.shape[1], expand_weight.shape[1]
    heads = heads_width // HD
    n_bits = n_dev.bit_length() - 1
    far_bits = (1, n_bits - 2)
    flips = (1 << far_bits[0], 1 << far_bits[1], (1 << far_bits[0]) | (1 << far_bits[1]))
    rest = [bit for bit in range(n_bits) if bit not in far_bits]
    mlp_orders = (rest, rest[::-1])
    others = list(range(2, n_bits - 2))
    attend_orders = (
        [0, 1] + others + [n_bits - 1, n_bits - 2],
        [1, n_bits - 2, 0] + others + [n_bits - 1],
        [n_bits - 2, 0, 1] + others + [n_bits - 1],
    )
    wq, wk, wv, wo, we, wr = (
        w.T for w in (query_weight, key_weight, value_weight, output_weight, expand_weight, reduce_weight)
    )
    vec = Vectors(width, heads_width, hidden_width)
    named = dict(
        gain1=first_gain, shift1=first_shift, bo=output_bias, gain2=second_gain,
        shift2=second_shift, br=reduce_bias, be=expand_bias, bq=query_bias, bv=value_bias,
    )
    vectors = jnp.concatenate(
        [jnp.pad(named[n], (0, lane_pad(named[n].shape[0]) - named[n].shape[0])) for n in vec.at]
    ).reshape(1, -1)
    sizes = (image_lengths.reshape(1, -1), image_owner.reshape(1, -1))
    wide32, wide16 = ((cap, width), f32), ((cap, width), bf16)
    half16 = ((cap // 2, width), bf16)
    head16 = ((cap, heads_width), bf16)
    place_args = (n_dev, half_rows)

    (send,) = call(
        functools.partial(pack_kernel, *place_args), "pack", [wide16], *sizes, patches, cotangent
    )
    got = spread(send)
    got_other = swap_cores(got)

    x, h1, q, k, v, logs, mask, attended, branch = call(
        functools.partial(attend_kernel, *place_args, vec), "attend",
        [wide16, wide16, head16, head16, head16, ((cap, heads), f32), ((cap, cap), f32), head16, wide32],
        *sizes, got, got_other, vectors, wq, wk, wv, wo, vmem=20,
    )
    branch_other = swap_cores(branch)
    (g,) = call(
        functools.partial(unpack_kernel, *place_args), "unpack", [wide16], *sizes, got, got_other
    )
    g_half = got.reshape(n_dev, 2, half_rows, width)[:, 1].reshape(cap // 2, width)
    g_near = swap_dp(g_half, flips[0])
    g_next = swap_dp(jnp.concatenate([g_half, g_near]), flips[1])
    g_far = jnp.concatenate([g_near, g_next])

    middle, h2, h2_half = call(
        functools.partial(middle_kernel, vec), "middle", [wide32, wide16, half16],
        x, branch, branch_other, vectors,
    )
    h2_far = jnp.concatenate([swap_dp(h2_half, flip) for flip in flips])
    out_part, dh2, be_grad = call(
        functools.partial(mlp_kernel, vec), "mlp", [wide32, wide32, ((1, lane_pad(hidden_width)), f32)],
        h2, g, we, vectors, wr, vmem=24,
    )
    dmid, branch_grad, datt, vec_grad2 = call(
        functools.partial(middle_back_kernel, vec), "middle_back",
        [wide32, wide16, head16, ((1, 4 * width), f32)],
        middle, dh2, swap_cores(dh2), g, vectors, wo,
    )
    dq, dk, dv, dh1, vec_grad3 = call(
        attend_back_kernel, "attend_back",
        [head16, head16, head16, wide32, ((1, 2 * lane_pad(heads_width)), f32)],
        q, k, v, logs, mask, datt, wq, wk, wv,
    )
    dh1_other = swap_cores(dh1)
    n_groups = len(attend_orders)
    group_shape = ((width // 2, 4 * heads_width // n_groups), bf16)
    turned_scratch = pltpu.VMEM((width, cap), f32)
    pieces = call(
        functools.partial(attend_weights_kernel, n_dev, attend_orders), "attend_weights",
        [group_shape] * (2 * n_groups), h1, branch_grad, dq, dk, dv, attended,
        scratch=[turned_scratch] * 4, vmem=24,
    )
    attend_pairs = list(zip(pieces[::2], pieces[1::2]))

    def send(pairs, orders, step):
        return [(keep, swap_dp(give, 1 << order[step])) for (keep, give), order in zip(pairs, orders)]

    attend_pairs = send(attend_pairs, attend_orders, 0)
    back, vec_grad1 = call(
        functools.partial(first_back_kernel, *place_args, vec), "first_back",
        [wide16, ((1, 2 * width), f32)],
        *sizes, x, dh1, dh1_other, vectors, dmid, middle, out_part, swap_cores(out_part),
    )
    home = spread(back)
    token_shape = ((tokens, width), bf16)
    mixed, patch_gradient = call(
        functools.partial(home_kernel, *place_args), "home", [token_shape] * 2,
        *sizes, home, swap_cores(home),
    )

    far_mine, back = lax.optimization_barrier((jnp.concatenate([h2_far, g_far]), back))
    far_other = swap_cores(far_mine)
    far_rows = h2_far.shape[0]
    part = 4 * (width // n_dev) * (n_dev // 16)
    mlp_piece = ((part // 2, hidden_width), bf16)
    mlp_pieces = call(
        functools.partial(mlp_weights_kernel, flips, mlp_orders, *place_args, vec), "mlp_weights",
        [mlp_piece] * 4, *sizes, h2, far_mine[:far_rows], far_other[:far_rows],
        g, far_mine[far_rows:], far_other[far_rows:], we, vectors, wr,
        scratch=[pltpu.VMEM((4 * cap, width), bf16)] * 2 + [pltpu.VMEM((part, 4 * cap), bf16)] * 2,
        vmem=40,
    )
    mlp_pairs = send(list(zip(mlp_pieces[::2], mlp_pieces[1::2])), mlp_orders, 0)
    attend_pairs = after(attend_pairs, mlp_pieces[0])
    for step in range(1, n_bits):
        attend_pairs = send(turn(f"attend_turn_{step}", attend_pairs), attend_orders, step)
    for step in range(1, len(rest)):
        turned = [turn(f"mlp_turn_{step}_{i}", [pair])[0] for i, pair in enumerate(mlp_pairs)]
        mlp_pairs = send(turned, mlp_orders, step)
    own_shape = ((width // n_dev, heads_width), f32)
    wq_sum, wk_sum, wv_sum, wo_sum = call(
        functools.partial(last_kernel, heads_width), "last", [own_shape] * 4,
        *[values for pair in attend_pairs for values in pair],
    )
    wr_sum, we_sum = [keep.astype(f32) + got.astype(f32) for keep, got in mlp_pairs]

    grads = sum_dp(jnp.concatenate([vec_grad1, vec_grad2, be_grad, vec_grad3], axis=1))
    total = {name: grads[0, at] for name, at in vec.at.items()}
    return (
        mixed, patch_gradient, total["gain1"], total["shift1"], wq_sum, total["bq"], wk_sum, wv_sum,
        total["bv"], wo_sum, total["bo"], total["gain2"], total["shift2"], we_sum, total["be"],
        wr_sum, total["br"],
    )


def solution(mesh):
    rows, all_same = P("dp", None), P()
    cols, vector = P(None, "tensor"), P("tensor")
    both = P("dp", "tensor")
    in_specs = (
        rows, rows, all_same, all_same, all_same, all_same, cols, vector, cols, cols, vector, cols,
        all_same, all_same, all_same, cols, vector, cols, all_same,
    )
    out_specs = (
        rows, rows, all_same, all_same, both, vector, both, both, vector, both, all_same, all_same,
        all_same, both, vector, both, all_same,
    )
    return jax.shard_map(
        on_device, mesh=mesh, in_specs=in_specs, out_specs=out_specs, check_vma=False
    )
```

time: 327 us -> 226 us (0.69)
  local copies, waits for them, and re-layouts: 81.5 us -> 28.4 us
  blocking collectives: 18.8 us -> 0 us
  other arithmetic: 20.4 us -> 2.02 us
  starting transfers between devices: 60.2 us -> 46.7 us
  waiting for transfers between devices: 73.4 us -> 83.8 us
  Pallas kernels: 69 us -> 62.9 us
    unnamed x178 -> x97, local copies, waits for them, and re-layouts: 63.4 us -> 22.4 us
    all_to_all x1 -> x0, blocking collectives: 18.8 us -> none  [spread(): return lax.all_to_all(rows, 'dp', split_axis=0, concat_axis=0, tiled=True)]
    all_to_all x3 -> x2, waiting for transfers between devices: 0.01 us -> 16.2 us  [spread(): return lax.all_to_all(rows, 'dp', split_axis=0, concat_axis=0, tiled=True)]
    ppermute x30 -> x25, starting transfers between devices: 45.3 us -> 33.2 us  [swap_dp(): lax.ppermute(values, 'dp', [(i, i ^ flip) for i in range(lax.axis_size('d...]
    convert_element_type x14 -> x0, other arithmetic: 8.56 us -> none  [scatter_sum(): value = total if step == len(order) - 1 else total.astype(bf16)]
    pallas_call x9 -> x0, other arithmetic: 7.2 us -> none  [call(): pl.pallas_call(kernel, name=name, out_shape=[jax.ShapeDtypeStruct(shape,...]
    dynamic_slice x9 -> x0, local copies, waits for them, and re-layouts: 6.93 us -> none  [the longest x4 3.8 us: scatter_sum(): give = lax.dynamic_index_in_dim(value, 1 - mine, axis, keepdims=False)]
    pallas_call x13 -> x17, Pallas kernels: 69 us -> 62.9 us  [call(): pl.pallas_call(kernel, name=name, out_shape=[jax.ShapeDtypeStruct(shape,...]
  transfers between devices with their start and end apart: 47 -> 34, of which waited for: 17 -> 15; matrix products, arithmetic and copies ran while one was open for 20% -> 4% of each run, Pallas kernels for 21% -> 20%
where the time goes in v2:
time: 226 us; the launch traced here: 225 us
  waiting for transfers between devices  83.8 us (37%)
  Pallas kernels  62.9 us (28%)
  starting transfers between devices  46.7 us (21%)
  local copies, waits for them, and re-layouts  28.4 us (13%)
    ppermute x25, waiting for transfers between devices, swap_dp(): lax.ppermute(values, 'dp', [(i, i ^ flip) for i in range(lax.axis_size('d...  63.7 us
    pallas_call x17, Pallas kernels, call(): pl.pallas_call(kernel, name=name, out_shape=[jax.ShapeDtypeStruct(shape,...  62.9 us
    ppermute x25, starting transfers between devices, swap_dp(): lax.ppermute(values, 'dp', [(i, i ^ flip) for i in range(lax.axis_size('d...  33.2 us
    unnamed x97, local copies, waits for them, and re-layouts  22.4 us
    all_to_all x2, waiting for transfers between devices, spread(): return lax.all_to_all(rows, 'dp', split_axis=0, concat_axis=0, tiled=True)  16.2 us
    all_to_all x2, starting transfers between devices, spread(): return lax.all_to_all(rows, 'dp', split_axis=0, concat_axis=0, tiled=True)  12.4 us
  transfers between devices with their start and end apart: 34, of which 15 were waited for; matrix products, arithmetic and copies ran while one was open for 4% of the time, Pallas kernels for 20%

profile of v2, /device:TPU:0, one launch (start us, length us, event | category | flops | bytes accessed | tf_op | source)
XLA Modules:
  0.0 225.0 jit_solution(2942393027688558974)
XLA Ops:
  5.4 8.3 %all-to-all-start = ((bf16[16,16,1152]{2,1,0:T(8,128)(2,1)}), bf16[16,16,1152]{2,1,0:T(8,128)(2,1)S(1)}, u32[]{:S(2)}, u32[]{:S(2)}) async-start(bf16[16,16,1152]{2,1,0:T(8,128)(2,1)} %bitcast.2), calls=%async_computation | async-start | bytes 1179648 | tf_op jit(solution)/shard_map/all_to_all | solution.py:481
  13.8 16.2 %all-to-all-done = bf16[16,16,1152]{2,1,0:T(8,128)(2,1)S(1)} async-done(((bf16[16,16,1152]{2,1,0:T(8,128)(2,1)}), bf16[16,16,1152]{2,1,0:T(8,128)(2,1)S(1)}, u32[]{:S(2)}, u32[]{:S(2)}) %all-to-all-start) | async-done | bytes 589856 | tf_op jit(solution)/shard_map/all_to_all | solution.py:481
  36.4 5.1 %attend.1 = (bf16[256,1152]{1,0:T(8,128)(2,1)S(1)}, bf16[256,1152]{1,0:T(8,128)(2,1)S(1)}, bf16[256,576]{1,0:T(8,128)(2,1)S(1)}, bf16[256,576]{1,0:T(8,128)(2,1)...) custom-call(s32[1,64]{1,0:T(1,128)S(1)} %bitcast.36, ...), custom_call_target="tpu_custom_call" | custom-call | tf_op jit(solution)/shard_map/attend/pallas_call | solution.py:461
  45.0 7.9 %mlp.1 = (f32[256,1152]{1,0:T(8,128)S(1)}, f32[256,1152]{1,0:T(8,128)S(1)}, f32[1,2176]{1,0:T(1,128)S(1)}) custom-call(bf16[256,1152]{1,0:T(8,128)(2,1)S(1)} %get-tuple-element.96.h2_ref, bf16[256,1152]{1,0:T(8,128)(2,1)S(1)} %unpack.1.g_ref, bf16[2152,1152]{1,0:T(8,128)(2,1)S(1)} %bitcast.17, f32[1,10368]{1,0:T(1,128)S(1)} %reshape.53.vec_ref, ...), custom_call_target="tpu_custom_call" | custom-call | tf_op jit(solution)/shard_map/mlp/pallas_call | solution.py:461
  56.7 6.3 %collective-permute-done.16 = bf16[128,1152]{1,0:T(8,128)(2,1)S(1)} collective-permute-done((bf16[128,1152]{1,0:T(8,128)(2,1)S(1)}, bf16[128,1152]{1,0:T(8,128)(2,1)S(1)}, u32[]{:S(2)}, u32[]{:S(2)}) %collective-permute-start.16) | collective-permute-done | bytes 294944 | tf_op jit(solution)/shard_map/ppermute | solution.py:477
  67.9 5.5 %attend_back.1 = (bf16[256,576]{1,0:T(8,128)(2,1)S(1)}, bf16[256,576]{1,0:T(8,128)(2,1)S(1)}, bf16[256,576]{1,0:T(8,128)(2,1)S(1)}, f32[256,1152]{1,0:T(8,128)S(1)}, f32[1,1280]{1,0:T(1,128)S(1)}) custom-call(bf16[256,576]{1,0:T(8,128)(2,1)S(1)} %get-tuple-element.89.q_ref, bf16[256,576]{1,0:T(8,128)(2,1)S(1)} %get-tuple-element.90.k_ref, ...), custom_call_target="tpu_custom_call" | custom-call | tf_op jit(solution)/shard_map/attend_back/pallas_call | solution.py:461
  75.4 8.8 %collective-permute-done.15 = bf16[128,1152]{1,0:T(8,128)(2,1)S(1)} collective-permute-done((bf16[128,1152]{1,0:T(8,128)(2,1)S(1)}, bf16[128,1152]{1,0:T(8,128)(2,1)S(1)}, u32[]{:S(2)}, u32[]{:S(2)}) %collective-permute-start.15) | collective-permute-done | bytes 294944 | tf_op jit(solution)/shard_map/ppermute | solution.py:477
  89.0 3.8 %attend_weights.1 = (bf16[576,768]{1,0:T(8,128)(2,1)S(1)}, bf16[576,768]{1,0:T(8,128)(2,1)}, bf16[576,768]{1,0:T(8,128)(2,1)S(1)}, bf16[576,768]{1,0:T(8,128)(2,...) custom-call(bf16[256,1152]{1,0:T(8,128)(2,1)S(1)} %get-tuple-element.109.h1_ref, ...), custom_call_target="tpu_custom_call" | custom-call | tf_op jit(solution)/shard_map/attend_weights/pallas_call | solution.py:461
  98.6 4.1 %all-to-all-start.1 = ((bf16[16,16,1152]{2,1,0:T(8,128)(2,1)}), bf16[16,16,1152]{2,1,0:T(8,128)(2,1)S(1)}, u32[]{:S(2)}, u32[]{:S(2)}) async-start(bf16[16,16,1152]{2,1,0:T(8,128)(2,1)} %bitcast.10), calls=%async_computation.1 | async-start | bytes 1179648 | tf_op jit(solution)/shard_map/all_to_all | solution.py:481
  105.9 2.4 %copy-done = bf16[1152,2152]{0,1:T(8,128)(2,1)S(1)} copy-done((bf16[1152,2152]{0,1:T(8,128)(2,1)S(1)}, bf16[1152,2152]{0,1:T(8,128)(2,1)}, u32[]{:S(2)}) %copy-start) | copy-done | bytes 4958232
  108.3 26.1 %mlp_weights.1 = (bf16[144,2152]{1,0:T(8,128)(2,1)S(1)}, bf16[144,2152]{1,0:T(8,128)(2,1)S(1)}, bf16[144,2152]{1,0:T(8,128)(2,1)S(1)}, bf16[144,2152]{1,0:T(8,128)(2,1)}) custom-call(s32[1,64]{1,0:T(1,128)S(1)} %bitcast.39, s32[1,64]{1,0:T(1,128)S(1)} %bitcast.45, bf16[256,1152]{1,0:T(8,128)(2,1)S(1)} %get-tuple-element.96.h2_ref, ...), custom_call_target="tpu_custom_call" | custom-call | tf_op jit(solution)/shard_map/mlp_weights/pallas_call | solution.py:461
  138.2 2.9 %attend_turn_1.1 = (f32[288,768]{1,0:T(8,128)S(1)}, bf16[288,768]{1,0:T(8,128)(2,1)}, f32[288,768]{1,0:T(8,128)S(1)}, bf16[288,768]{1,0:T(8,128)(2,1)}, f32[288,...) custom-call(bf16[576,768]{1,0:T(8,128)(2,1)S(1)} %copy-done.12, bf16[576,768]{1,0:T(8,128)(2,1)S(1)} %copy-done.18, ...), custom_call_target="tpu_custom_call" | custom-call | tf_op jit(solution)/shard_map/attend_turn_1/pallas_call | solution.py:461
  146.9 2.4 %collective-permute-start.28 = (bf16[144,2152]{1,0:T(8,128)(2,1)}, bf16[144,2152]{1,0:T(8,128)(2,1)}, u32[]{:S(2)}, u32[]{:S(2)}) collective-permute-start(bf16[144,2152]{1,0:T(8,128)(2,1)} %get-tuple-element.153), channel_id=1, source_target_pairs={{0,16},{2,18},{4,20},{6,22},{8,24},{10,26},{12,28},{14,30},{16,0},... | collective-permute-start | bytes 1859336 | tf_op jit(solution)/shard_map/ppermute | solution.py:477
  149.4 4.4 %collective-permute-done.19.refs_1_ = bf16[288,768]{1,0:T(8,128)(2,1)S(1)} collective-permute-done((bf16[288,768]{1,0:T(8,128)(2,1)}, bf16[288,768]{1,0:T(8,128)(2,1)S(1)}, u32[]{:S(2)}, u32[]{:S(2)}) %collective-permute-start.19) | collective-permute-done | bytes 442400 | tf_op jit(solution)/shard_map/ppermute | solution.py:477
  155.4 7.8 %collective-permute-done.20.refs_3_ = bf16[288,768]{1,0:T(8,128)(2,1)S(1)} collective-permute-done((bf16[288,768]{1,0:T(8,128)(2,1)}, bf16[288,768]{1,0:T(8,128)(2,1)S(1)}, u32[]{:S(2)}, u32[]{:S(2)}) %collective-permute-start.20) | collective-permute-done | bytes 442400 | tf_op jit(solution)/shard_map/ppermute | solution.py:477
  171.3 3.4 %collective-permute-done.7 = f32[1,10368]{1,0:T(1,128)S(1)} collective-permute-done((f32[1,10368]{1,0:T(1,128)S(1)}, f32[1,10368]{1,0:T(1,128)S(1)}, u32[]{:S(2)}, u32[]{:S(2)}) %collective-permute-start.7) | collective-permute-done | bytes 41504 | tf_op jit(solution)/shard_map/ppermute | solution.py:477
  174.8 2.4 %collective-permute-start.8 = (f32[1,10368]{1,0:T(1,128)S(1)}, f32[1,10368]{1,0:T(1,128)S(1)}, u32[]{:S(2)}, u32[]{:S(2)}) collective-permute-start(f32[1,10368]{1,0:T(1,128)S(1)} %add.25), channel_id=1, source_target_pairs={{0,8},{2,10},{4,12},{6,14},{8,0},{10,2},{12,4},{14,6},{16,24},{18,... | collective-permute-start | bytes 124424 | tf_op jit(solution)/shard_map/ppermute | solution.py:477
  177.3 8.9 %collective-permute-done.8 = f32[1,10368]{1,0:T(1,128)S(1)} collective-permute-done((f32[1,10368]{1,0:T(1,128)S(1)}, f32[1,10368]{1,0:T(1,128)S(1)}, u32[]{:S(2)}, u32[]{:S(2)}) %collective-permute-start.8) | collective-permute-done | bytes 41504 | tf_op jit(solution)/shard_map/ppermute | solution.py:477
  186.7 4.6 %collective-permute-done.9 = f32[1,10368]{1,0:T(1,128)S(1)} collective-permute-done((f32[1,10368]{1,0:T(1,128)S(1)}, f32[1,10368]{1,0:T(1,128)S(1)}, u32[]{:S(2)}, u32[]{:S(2)}) %collective-permute-start.9) | collective-permute-done | bytes 41504 | tf_op jit(solution)/shard_map/ppermute | solution.py:477
  196.6 3.1 %collective-permute-done.23.refs_3_ = bf16[144,768]{1,0:T(8,128)(2,1)S(1)} collective-permute-done((bf16[144,768]{1,0:T(8,128)(2,1)S(1)}, bf16[144,768]{1,0:T(8,128)(2,1)S(1)}, u32[]{:S(2)}, u32[]{:S(2)}) %collective-permute-start.23) | collective-permute-done | bytes 221216 | tf_op jit(solution)/shard_map/ppermute | solution.py:477
  200.0 2.9 %collective-permute-start.26 = (bf16[72,768]{1,0:T(8,128)(2,1)S(1)}, bf16[72,768]{1,0:T(8,128)(2,1)S(1)}, u32[]{:S(2)}, u32[]{:S(2)}) collective-permute-start(bf16[72,768]{1,0:T(8,128)(2,1)S(1)} %get-tuple-element.145), channel_id=1, source_target_pairs={{0,16},{2,18},{4,20},{6,22},{8,24},{10,26},{12,28},{14,30},{16,0},... | collective-permute-start | bytes 331784 | tf_op jit(solution)/shard_map/ppermute | solution.py:477
  205.1 2.8 %collective-permute-start.31 = (bf16[72,2152]{1,0:T(8,128)(2,1)S(1)}, bf16[72,2152]{1,0:T(8,128)(2,1)S(1)}, u32[]{:S(2)}, u32[]{:S(2)}) collective-permute-start(bf16[72,2152]{1,0:T(8,128)(2,1)S(1)} %get-tuple-element.158), channel_id=1, source_target_pairs={{0,16},{2,18},{4,20},{6,22},{8,24},{10,26},{12,28},{14,30},{16,0},... | collective-permute-start | bytes 929672 | tf_op jit(solution)/shard_map/ppermute | solution.py:477
  207.9 8.6 %collective-permute-done.26.refs_3_ = bf16[72,768]{1,0:T(8,128)(2,1)S(1)} collective-permute-done((bf16[72,768]{1,0:T(8,128)(2,1)S(1)}, bf16[72,768]{1,0:T(8,128)(2,1)S(1)}, u32[]{:S(2)}, u32[]{:S(2)}) %collective-permute-start.26) | collective-permute-done | bytes 110624 | tf_op jit(solution)/shard_map/ppermute | solution.py:477
  220.8 3.4 %collective-permute-done.31 = bf16[72,2152]{1,0:T(8,128)(2,1)S(1)} collective-permute-done((bf16[72,2152]{1,0:T(8,128)(2,1)S(1)}, bf16[72,2152]{1,0:T(8,128)(2,1)S(1)}, u32[]{:S(2)}, u32[]{:S(2)}) %collective-permute-start.31) | collective-permute-done | bytes 309920 | tf_op jit(solution)/shard_map/ppermute | solution.py:477
  (177 shorter events, 71.7 us)
Async XLA Ops:
  5.4 24.6 %all-to-all-start = ((bf16[16,16,1152]{2,1,0:T(8,128)(2,1)}), bf16[16,16,1152]{2,1,0:T(8,128)(2,1)S(1)}, u32[]{:S(2)}, u32[]{:S(2)}) async-start(bf16[16,16,1152]{2,1,0:T(8,128)(2,1)} %bitcast.2), calls=%async_computation | async-start | bytes 1179648 | tf_op jit(solution)/shard_map/all_to_all | solution.py:481
  52.9 12.8 %collective-permute-start.2 = (f32[256,1152]{1,0:T(8,128)S(1)}, f32[256,1152]{1,0:T(8,128)S(1)}, u32[]{:S(2)}, u32[]{:S(2)}) collective-permute-start(f32[256,1152]{1,0:T(8,128)S(1)} %get-tuple-element.97.mine_ref), channel_id=1, source_target_pairs={{0,1},{1,0},{2,3},{3,2},{4,5},{5,4},{6,7},{7,6},{8,9},{9,8},{10,11... | collective-permute-start | bytes 3538952 | tf_op jit(solution)/shard_map/ppermute | solution.py:473
  54.3 19.0 %collective-permute-start.13 = (bf16[128,1152]{1,0:T(8,128)(2,1)S(1)}, bf16[128,1152]{1,0:T(8,128)(2,1)S(1)}, u32[]{:S(2)}, u32[]{:S(2)}) collective-permute-start(bf16[128,1152]{1,0:T(8,128)(2,1)S(1)} %get-tuple-element.121), channel_id=1, source_target_pairs={{0,4},{2,6},{4,0},{6,2},{8,12},{10,14},{12,8},{14,10},{16,20},{18,... | collective-permute-start | bytes 884744 | tf_op jit(solution)/shard_map/ppermute | solution.py:477
  55.3 19.4 %collective-permute-start.14 = (bf16[128,1152]{1,0:T(8,128)(2,1)S(1)}, bf16[128,1152]{1,0:T(8,128)(2,1)S(1)}, u32[]{:S(2)}, u32[]{:S(2)}) collective-permute-start(bf16[128,1152]{1,0:T(8,128)(2,1)S(1)} %get-tuple-element.121), channel_id=1, source_target_pairs={{0,8},{2,10},{4,12},{6,14},{8,0},{10,2},{12,4},{14,6},{16,24},{18,... | collective-permute-start | bytes 884744 | tf_op jit(solution)/shard_map/ppermute | solution.py:477
  63.1 22.6 %collective-permute-start.17 = (bf16[256,1152]{1,0:T(8,128)(2,1)S(1)}, bf16[256,1152]{1,0:T(8,128)(2,1)S(1)}, u32[]{:S(2)}, u32[]{:S(2)}) collective-permute-start(bf16[256,1152]{1,0:T(8,128)(2,1)S(1)} %pad_maximum_fusion), channel_id=1, source_target_pairs={{0,8},{2,10},{4,12},{6,14},{8,0},{10,2},{12,4},{14,6},{16,24},{18,... | collective-permute-start | bytes 1769480 | tf_op jit(solution)/shard_map/ppermute | solution.py:477
  64.7 19.6 %collective-permute-start.15 = (bf16[128,1152]{1,0:T(8,128)(2,1)S(1)}, bf16[128,1152]{1,0:T(8,128)(2,1)S(1)}, u32[]{:S(2)}, u32[]{:S(2)}) collective-permute-start(bf16[128,1152]{1,0:T(8,128)(2,1)S(1)} %get-tuple-element.121), channel_id=1, source_target_pairs={{0,12},{2,14},{4,8},{6,10},{8,4},{10,6},{12,0},{14,2},{16,28},{18,... | collective-permute-start | bytes 884744 | tf_op jit(solution)/shard_map/ppermute | solution.py:477
  65.7 20.9 %collective-permute-start.4 = (f32[256,1152]{1,0:T(8,128)S(1)}, f32[256,1152]{1,0:T(8,128)S(1)}, u32[]{:S(2)}, u32[]{:S(2)}) collective-permute-start(f32[256,1152]{1,0:T(8,128)S(1)} %get-tuple-element.101.out_mine_ref), channel_id=1, source_target_pairs={{0,1},{1,0},{2,3},{3,2},{4,5},{5,4},{6,7},{7,6},{8,9},{9,8},{10,11... | collective-permute-start | bytes 3538952 | tf_op jit(solution)/shard_map/ppermute | solution.py:473
  73.4 13.2 %collective-permute-start.3 = (f32[256,1152]{1,0:T(8,128)S(1)}, f32[256,1152]{1,0:T(8,128)S(1)}, u32[]{:S(2)}, u32[]{:S(2)}) collective-permute-start(f32[256,1152]{1,0:T(8,128)S(1)} %get-tuple-element.99.mine_ref), channel_id=1, source_target_pairs={{0,1},{1,0},{2,3},{3,2},{4,5},{5,4},{6,7},{7,6},{8,9},{9,8},{10,11... | collective-permute-start | bytes 3538952 | tf_op jit(solution)/shard_map/ppermute | solution.py:473
  89.0 15.4 %collective-permute-start.18 = (bf16[768,1152]{1,0:T(8,128)(2,1)}, bf16[768,1152]{1,0:T(8,128)(2,1)}, u32[]{:S(2)}, u32[]{:S(2)}) collective-permute-start(bf16[768,1152]{1,0:T(8,128)(2,1)} %constant_dynamic-update-slice_fusion.5), channel_id=1, source_target_pairs={{0,1},{1,0},{2,3},{3,2},{4,5},{5,4},{6,7},{7,6},{8,9},{9,8},{10,11... | collective-permute-start | bytes 5308424 | tf_op jit(solution)/shard_map/ppermute | solution.py:473
  95.6 40.4 %collective-permute-start.10 = (bf16[576,768]{1,0:T(8,128)(2,1)}, bf16[576,768]{1,0:T(8,128)(2,1)S(1)}, u32[]{:S(2)}, u32[]{:S(2)}) collective-permute-start(bf16[576,768]{1,0:T(8,128)(2,1)} %get-tuple-element.116), channel_id=1, source_target_pairs={{0,2},{2,0},{4,6},{6,4},{8,10},{10,8},{12,14},{14,12},{16,18},{18,... | collective-permute-start | bytes 2654216 | tf_op jit(solution)/shard_map/ppermute | solution.py:477
  96.2 40.9 %collective-permute-start.11 = (bf16[576,768]{1,0:T(8,128)(2,1)}, bf16[576,768]{1,0:T(8,128)(2,1)}, u32[]{:S(2)}, u32[]{:S(2)}) collective-permute-start(bf16[576,768]{1,0:T(8,128)(2,1)} %get-tuple-element.118), channel_id=1, source_target_pairs={{0,4},{2,6},{4,0},{6,2},{8,12},{10,14},{12,8},{14,10},{16,20},{18,... | collective-permute-start | bytes 2654216 | tf_op jit(solution)/shard_map/ppermute | solution.py:477
  97.1 40.0 %collective-permute-start.12 = (bf16[576,768]{1,0:T(8,128)(2,1)}, bf16[576,768]{1,0:T(8,128)(2,1)}, u32[]{:S(2)}, u32[]{:S(2)}) collective-permute-start(bf16[576,768]{1,0:T(8,128)(2,1)} %get-tuple-element.120), channel_id=1, source_target_pairs={{0,8},{2,10},{4,12},{6,14},{8,0},{10,2},{12,4},{14,6},{16,24},{18,... | collective-permute-start | bytes 2654216 | tf_op jit(solution)/shard_map/ppermute | solution.py:477
  98.6 50.7 %all-to-all-start.1 = ((bf16[16,16,1152]{2,1,0:T(8,128)(2,1)}), bf16[16,16,1152]{2,1,0:T(8,128)(2,1)S(1)}, u32[]{:S(2)}, u32[]{:S(2)}) async-start(bf16[16,16,1152]{2,1,0:T(8,128)(2,1)} %bitcast.10), calls=%async_computation.1 | async-start | bytes 1179648 | tf_op jit(solution)/shard_map/all_to_all | solution.py:481
  142.1 11.7 %collective-permute-start.19 = (bf16[288,768]{1,0:T(8,128)(2,1)}, bf16[288,768]{1,0:T(8,128)(2,1)S(1)}, u32[]{:S(2)}, u32[]{:S(2)}) collective-permute-start(bf16[288,768]{1,0:T(8,128)(2,1)} %get-tuple-element.131), channel_id=1, source_target_pairs={{0,4},{2,6},{4,0},{6,2},{8,12},{10,14},{12,8},{14,10},{16,20},{18,... | collective-permute-start | bytes 1327112 | tf_op jit(solution)/shard_map/ppermute | solution.py:477
  144.0 19.2 %collective-permute-start.20 = (bf16[288,768]{1,0:T(8,128)(2,1)}, bf16[288,768]{1,0:T(8,128)(2,1)S(1)}, u32[]{:S(2)}, u32[]{:S(2)}) collective-permute-start(bf16[288,768]{1,0:T(8,128)(2,1)} %get-tuple-element.133), channel_id=1, source_target_pairs={{0,8},{2,10},{4,12},{6,14},{8,0},{10,2},{12,4},{14,6},{16,24},{18,... | collective-permute-start | bytes 1327112 | tf_op jit(solution)/shard_map/ppermute | solution.py:477
  145.5 17.7 %collective-permute-start.21 = (bf16[288,768]{1,0:T(8,128)(2,1)}, bf16[288,768]{1,0:T(8,128)(2,1)}, u32[]{:S(2)}, u32[]{:S(2)}) collective-permute-start(bf16[288,768]{1,0:T(8,128)(2,1)} %get-tuple-element.135), channel_id=1, source_target_pairs={{0,2},{2,0},{4,6},{6,4},{8,10},{10,8},{12,14},{14,12},{16,18},{18,... | collective-permute-start | bytes 1327112 | tf_op jit(solution)/shard_map/ppermute | solution.py:477
  146.9 45.1 %collective-permute-start.28 = (bf16[144,2152]{1,0:T(8,128)(2,1)}, bf16[144,2152]{1,0:T(8,128)(2,1)}, u32[]{:S(2)}, u32[]{:S(2)}) collective-permute-start(bf16[144,2152]{1,0:T(8,128)(2,1)} %get-tuple-element.153), channel_id=1, source_target_pairs={{0,16},{2,18},{4,20},{6,22},{8,24},{10,26},{12,28},{14,30},{16,0},... | collective-permute-start | bytes 1859336 | tf_op jit(solution)/shard_map/ppermute | solution.py:477
  149.3 53.5 %collective-permute-start.5 = (bf16[256,1152]{1,0:T(8,128)(2,1)S(1)}, bf16[256,1152]{1,0:T(8,128)(2,1)S(1)}, u32[]{:S(2)}, u32[]{:S(2)}) collective-permute-start(bf16[256,1152]{1,0:T(8,128)(2,1)S(1)} %bitcast.33), channel_id=1, source_target_pairs={{0,1},{1,0},{2,3},{3,2},{4,5},{5,4},{6,7},{7,6},{8,9},{9,8},{10,11... | collective-permute-start | bytes 1769480 | tf_op jit(solution)/shard_map/ppermute | solution.py:473
  153.8 51.2 %collective-permute-start.30 = (bf16[144,2152]{1,0:T(8,128)(2,1)}, bf16[144,2152]{1,0:T(8,128)(2,1)S(1)}, u32[]{:S(2)}, u32[]{:S(2)}) collective-permute-start(bf16[144,2152]{1,0:T(8,128)(2,1)} %copy-done.29), channel_id=1, source_target_pairs={{0,2},{2,0},{4,6},{6,4},{8,10},{10,8},{12,14},{14,12},{16,18},{18,... | collective-permute-start | bytes 1859336 | tf_op jit(solution)/shard_map/ppermute | solution.py:477
  165.7 28.1 %collective-permute-start.22 = (bf16[144,768]{1,0:T(8,128)(2,1)S(1)}, bf16[144,768]{1,0:T(8,128)(2,1)S(1)}, u32[]{:S(2)}, u32[]{:S(2)}) collective-permute-start(bf16[144,768]{1,0:T(8,128)(2,1)S(1)} %get-tuple-element.137), channel_id=1, source_target_pairs={{0,16},{2,18},{4,20},{6,22},{8,24},{10,26},{12,28},{14,30},{16,0},... | collective-permute-start | bytes 663560 | tf_op jit(solution)/shard_map/ppermute | solution.py:477
  193.8 26.1 %collective-permute-start.29 = (bf16[72,2152]{1,0:T(8,128)(2,1)S(1)}, bf16[72,2152]{1,0:T(8,128)(2,1)S(1)}, u32[]{:S(2)}, u32[]{:S(2)}) collective-permute-start(bf16[72,2152]{1,0:T(8,128)(2,1)S(1)} %get-tuple-element.155), channel_id=1, source_target_pairs={{0,2},{2,0},{4,6},{6,4},{8,10},{10,8},{12,14},{14,12},{16,18},{18,... | collective-permute-start | bytes 929672 | tf_op jit(solution)/shard_map/ppermute | solution.py:477
  200.0 16.6 %collective-permute-start.26 = (bf16[72,768]{1,0:T(8,128)(2,1)S(1)}, bf16[72,768]{1,0:T(8,128)(2,1)S(1)}, u32[]{:S(2)}, u32[]{:S(2)}) collective-permute-start(bf16[72,768]{1,0:T(8,128)(2,1)S(1)} %get-tuple-element.145), channel_id=1, source_target_pairs={{0,16},{2,18},{4,20},{6,22},{8,24},{10,26},{12,28},{14,30},{16,0},... | collective-permute-start | bytes 331784 | tf_op jit(solution)/shard_map/ppermute | solution.py:477
  202.8 16.1 %collective-permute-start.27 = (bf16[72,768]{1,0:T(8,128)(2,1)S(1)}, bf16[72,768]{1,0:T(8,128)(2,1)S(1)}, u32[]{:S(2)}, u32[]{:S(2)}) collective-permute-start(bf16[72,768]{1,0:T(8,128)(2,1)S(1)} %get-tuple-element.147), channel_id=1, source_target_pairs={{0,16},{2,18},{4,20},{6,22},{8,24},{10,26},{12,28},{14,30},{16,0},... | collective-permute-start | bytes 331784 | tf_op jit(solution)/shard_map/ppermute | solution.py:477
  205.1 19.1 %collective-permute-start.31 = (bf16[72,2152]{1,0:T(8,128)(2,1)S(1)}, bf16[72,2152]{1,0:T(8,128)(2,1)S(1)}, u32[]{:S(2)}, u32[]{:S(2)}) collective-permute-start(bf16[72,2152]{1,0:T(8,128)(2,1)S(1)} %get-tuple-element.158), channel_id=1, source_target_pairs={{0,16},{2,18},{4,20},{6,22},{8,24},{10,26},{12,28},{14,30},{16,0},... | collective-permute-start | bytes 929672 | tf_op jit(solution)/shard_map/ppermute | solution.py:477
  (51 other events, 519.7 us)

commit v3 on v2

v3 whole, which is shorter than its diff:
```python
import functools

import jax
import jax.numpy as jnp
from jax import lax
from jax.experimental import pallas as pl
from jax.experimental.pallas import tpu as pltpu
from jax.sharding import PartitionSpec as P

HD = 72
masked_score = -1000000000.0
norm_eps = 1e-06
gelu_scale = 0.7978845608028654
gelu_cubic = 0.044715
f32 = jnp.float32
bf16 = jnp.bfloat16
MIB = 1024 * 1024


def dot(left, right):
    return lax.dot_general(left, right, (((1,), (0,)), ((), ())), preferred_element_type=f32)


def dot_cols(left, right):
    return lax.dot_general(left, right, (((1,), (1,)), ((), ())), preferred_element_type=f32)


def dot_rows(left, right):
    return lax.dot_general(left, right, (((0,), (0,)), ((), ())), preferred_element_type=f32)


def iota(shape, dim):
    return lax.broadcasted_iota(jnp.int32, shape, dim).astype(f32)


def row_sum(values):
    return jnp.sum(values, axis=0, keepdims=True)


def lane_sum(values):
    return jnp.sum(values, axis=1, keepdims=True)


def lane_mean(values):
    return jnp.mean(values, axis=1, keepdims=True)


def my_span(lengths, owners, me):
    base = lane_sum(jnp.where(owners < me, lengths, 0.0))
    used = lane_sum(jnp.where(owners == me, lengths, 0.0))
    return base, used


def token_slots(lengths, owners, me, n_dev, tokens, half_rows):
    device = iota((n_dev, lengths.shape[1]), 0)
    base = lane_sum(jnp.where(owners < device, lengths, 0.0))
    pos = iota((1, tokens), 1) * n_dev + me
    below = base <= pos
    target = row_sum(jnp.where(below, 1.0, 0.0)) - 1.0
    start = jnp.max(jnp.where(below, base, -1.0), axis=0, keepdims=True)
    slot = jnp.floor((pos - start) * (1.0 / n_dev))
    half = jnp.floor(slot * (1.0 / half_rows))
    return half, target * half_rows + slot - half * half_rows


def block_slots(base, n_dev, cap, half_rows):
    p = iota((cap, 1), 0)
    pos = base + p
    source = pos - n_dev * jnp.floor(pos * (1.0 / n_dev))
    slot = jnp.floor(p * (1.0 / n_dev))
    half = jnp.floor(slot * (1.0 / half_rows))
    return half, source * half_rows + slot - half * half_rows


def one_hot(index, shape, dim):
    return jnp.where(index == iota(shape, dim), 1.0, 0.0).astype(bf16)


def lane_pad(size):
    return -(-size // 128) * 128


def place():
    return lax.axis_index("dp").astype(f32), lax.axis_index("tensor").astype(f32)


def norm_parts(values):
    centered = values - lane_mean(values)
    scale = lax.rsqrt(lane_mean(centered * centered) + norm_eps)
    return centered * scale, scale


def norm_back(normed, scale, grad, gain):
    inner = grad * gain
    return scale * (inner - lane_mean(inner) - normed * lane_mean(inner * normed))


def gelu_both(values):
    square = values * values
    bent = jnp.tanh(gelu_scale * values * (1.0 + gelu_cubic * square))
    half = 0.5 * (1.0 + bent)
    slope = half + 0.5 * values * (1.0 - bent * bent) * (
        gelu_scale * (1.0 + 3.0 * gelu_cubic * square)
    )
    return values * half, slope


def flip_of(block, order):
    flip = 0 * block
    for step, bit in enumerate(order):
        flip = flip | (((block >> (len(order) - 1 - step)) & 1) << bit)
    return flip


def feature_pick(rows, width, n_dev, order):
    owner_rows = width // n_dev
    i = iota((rows, 1), 0)
    block = jnp.floor((i + 0.5) * (1.0 / owner_rows))
    owner = flip_of(block.astype(jnp.int32), order) ^ lax.axis_index("dp")
    return one_hot(owner.astype(f32) * owner_rows + (i - block * owner_rows), (rows, width), 1)


def ordered_rows(out_ref, from_ref, n_dev, order):
    width = from_ref.shape[0]
    owner_rows = width // n_dev
    if owner_rows % 8:
        pick = feature_pick(width, width, n_dev, order)
        out_ref[...] = dot(pick, from_ref[...].astype(bf16))
        return
    me = lax.axis_index("dp")
    for block in range(n_dev):
        start = pl.multiple_of((me ^ flip_of(block, order)) * owner_rows, 8)
        rows = slice(block * owner_rows, (block + 1) * owner_rows)
        out_ref[rows, :] = from_ref[pl.ds(start, owner_rows), :]


class Made:
    def __init__(self, refs):
        self.refs = refs

    def __getitem__(self, name):
        return self.refs[name]

    def put(self, name, value):
        self.refs[name][...] = value.astype(self.refs[name].dtype)


class Far:
    def __init__(self, refs, near, sems):
        self.near = near
        self.copies = {
            name: pltpu.make_async_copy(ref, near[name], sems.at[i])
            for i, (name, ref) in enumerate(refs.items())
        }
        for copy in self.copies.values():
            copy.start()

    def __getitem__(self, name):
        copy = self.copies.pop(name, None)
        if copy is not None:
            copy.wait()
        return self.near[name]


def call(body, name, ins, outs, scratch=(), vmem=16, far=False, us=0.0):
    in_names, out_names = list(ins), list(outs)
    n_in, n_out = len(in_names), len(out_names)

    def kernel(*refs):
        given = dict(zip(in_names, refs))
        made = Made(dict(zip(out_names, refs[n_in:])))
        rest = refs[n_in + n_out :]
        if far:
            given = Far(given, dict(zip(in_names, rest)), rest[n_in])
            rest = rest[n_in + 1 :]
        body(given, made, *rest)

    copies = [pltpu.VMEM(x.shape, x.dtype) for x in ins.values()]
    copies += [pltpu.SemaphoreType.DMA((n_in,))]
    results = pl.pallas_call(
        kernel,
        name=name,
        out_shape=[jax.ShapeDtypeStruct(shape, dtype) for shape, dtype in outs.values()],
        in_specs=[pl.BlockSpec(memory_space=pltpu.HBM if far else pltpu.VMEM)] * n_in,
        out_specs=[pl.BlockSpec(memory_space=pltpu.VMEM)] * n_out,
        scratch_shapes=(copies if far else []) + list(scratch),
        compiler_params=pltpu.CompilerParams(vmem_limit_bytes=vmem * MIB),
    )(*ins.values())
    return dict(zip(out_names, results))


def pack_kernel(n_dev, half_rows, tokens, given, made):
    me, core = place()
    lengths, owners = given["lengths"][...].astype(f32), given["owners"][...].astype(f32)
    half, index = token_slots(lengths, owners, me, n_dev, tokens, half_rows)
    target = jnp.floor(index * (1.0 / half_rows))
    index = jnp.where(half == core, index + target * half_rows, -1e6)
    shape = (2 * n_dev * half_rows, tokens)
    x_pick, g_pick = one_hot(index, shape, 0), one_hot(index + half_rows, shape, 0)
    rows = dot(x_pick, given["x"][...])
    made.put("send", rows + dot(g_pick, given["g"][...]))


def block_rows(given, n_dev, cap, half_rows, kind):
    me, core = place()
    lengths, owners = given["lengths"][...].astype(f32), given["owners"][...].astype(f32)
    base, _ = my_span(lengths, owners, me)
    half, index = block_slots(base, n_dev, cap, half_rows)
    source = jnp.floor(index * (1.0 / half_rows))
    index = index + (source + kind) * half_rows
    index = jnp.where(half == core, index, index + 2 * n_dev * half_rows)
    pick = one_hot(index, (cap, 2 * cap), 1)
    return dot(pick, jnp.concatenate([given["mine"][...], given["other"][...]], axis=0))


def unpack_kernel(n_dev, half_rows, given, made):
    made.put("g", block_rows(given, n_dev, made["g"].shape[0], half_rows, 1))


def image_mask(lengths, owners, cap):
    me, _ = place()
    base, used = my_span(lengths, owners, me)
    n_img = lengths.shape[1]
    starts = lane_sum(
        jnp.where(iota((n_img, n_img), 1) < iota((n_img, n_img), 0), lengths, 0.0)
    )
    p = iota((1, cap), 1)
    count = row_sum(jnp.where(starts <= base + p, 1.0, 0.0))
    seg_row = jnp.where(p < used, count, 0.0)
    on_diagonal = iota((cap, cap), 0) == iota((cap, cap), 1)
    seg_col = lane_sum(jnp.where(on_diagonal, seg_row, 0.0))
    return jnp.where(seg_col == seg_row, 1.0, 0.0)


class Vectors:
    def __init__(self, width, heads_width, hidden_width):
        self.at = {}
        end = 0
        for name, size in (
            ("gain1", width), ("shift1", width), ("bo", width), ("gain2", width),
            ("shift2", width), ("br", width), ("be", hidden_width), ("bq", heads_width),
            ("bv", heads_width),
        ):
            self.at[name] = slice(end, end + size)
            end += lane_pad(size)
        self.size = end


def attend_kernel(n_dev, half_rows, vec, given, made):
    cap = made["x"].shape[0]
    lengths, owners = given["lengths"][...].astype(f32), given["owners"][...].astype(f32)
    same = image_mask(lengths, owners, cap)
    made.put("mask", same)
    x = block_rows(given, n_dev, cap, half_rows, 0)
    made.put("x", x)
    row = given["vec"]
    normed, _ = norm_parts(x)
    h1 = (normed * row[:, vec.at["gain1"]] + row[:, vec.at["shift1"]]).astype(bf16)
    made.put("h1", h1)
    made.put("q", dot_cols(h1, given["wq"][...]) + row[:, vec.at["bq"]])
    made.put("k", dot_cols(h1, given["wk"][...]))
    made.put("v", dot_cols(h1, given["wv"][...]) + row[:, vec.at["bv"]])
    for h in range(made["q"].shape[1] // HD):
        cols = slice(h * HD, (h + 1) * HD)
        s = dot_cols(made["q"][:, cols], made["k"][:, cols]) * HD ** (-0.5)
        s = jnp.where(same > 0.5, s, masked_score)
        top = jnp.max(s, axis=1, keepdims=True)
        e = jnp.exp(s - top)
        total = lane_sum(e)
        made["log"][:, h : h + 1] = top + jnp.log(total)
        made["att"][:, cols] = dot((e / total).astype(bf16), made["v"][:, cols]).astype(bf16)
    made.put("branch", dot(made["att"][...], given["wo"][...]))


def add_cores(given, name):
    return given[name][...].astype(f32) + given[name + "_other"][...].astype(f32)


def add_halves(given, name):
    return jnp.concatenate([add_cores(given, f"{name}_{i}") for i in range(2)], axis=0)


def add_sums(given, which):
    rows = given["sums_0"].shape[0] // 2
    rows = slice(which * rows, (which + 1) * rows)
    halves = [given[f"sums_{i}"][rows, :].astype(f32) for i in range(2)]
    others = [given[f"sums_{i}_other"][rows, :].astype(f32) for i in range(2)]
    return jnp.concatenate([halves[i] + others[i] for i in range(2)], axis=0)


def chunks_of(width, step):
    full = width // step
    return full, full * step, width - full * step


def mlp_kernel(n_dev, half_rows, vec, given, made, out_total, dh2_total):
    cap = made["middle"].shape[0]
    row = given["vec"]
    x = given["x"][...].astype(f32)
    middle = x + (add_cores(given, "branch") + row[:, vec.at["bo"]])
    made.put("middle", middle)
    normed, _ = norm_parts(middle)
    made.put("h2", normed * row[:, vec.at["gain2"]] + row[:, vec.at["shift2"]])
    rows = cap // 2
    start = pl.multiple_of(lax.axis_index("tensor") * rows, rows)
    made["halves"][:rows, :] = made["h2"][pl.ds(start, rows), :]
    made["halves"][rows:, :] = given["g"][pl.ds(start, rows), :]
    step = 512
    full, done, rest = chunks_of(given["we"].shape[0], step)
    first = vec.at["be"].start
    out_total[...] = jnp.zeros_like(out_total)
    dh2_total[...] = jnp.zeros_like(dh2_total)
    made["be_grad"][...] = jnp.zeros_like(made["be_grad"])

    def chunk(rows, lanes, bias):
        we, wr = given["we"][rows, :], given["wr"][rows, :]
        hidden, slope = gelu_both(dot_cols(made["h2"][...], we) + given["vec"][:, bias])
        dexp = (dot_cols(given["g"][...], wr) * slope).astype(bf16)
        made["be_grad"][:, lanes] = row_sum(dexp.astype(f32))
        out_total[...] += dot(hidden.astype(bf16), wr)
        dh2_total[...] += dot(dexp, we)

    @pl.loop(0, full)
    def _(i):
        at = pl.multiple_of(i * step, step)
        lanes = pl.ds(at, step)
        chunk(lanes, lanes, pl.ds(pl.multiple_of(first + at, 128), step))

    if rest:
        lanes = slice(done, done + rest)
        chunk(lanes, lanes, slice(first + done, first + done + rest))
    half = cap // 2
    for i in range(2):
        rows = slice(i * half, (i + 1) * half)
        made[f"sums_{i}"][:half, :] = dh2_total[rows, :].astype(bf16)
        made[f"sums_{i}"][half:, :] = out_total[rows, :].astype(bf16)


def middle_back_kernel(vec, given, made):
    width = given["middle"].shape[1]
    g = given["g"][...].astype(f32)
    normed, scale = norm_parts(given["middle"][...])
    dh2 = add_sums(given, 0)
    dmid = g + norm_back(normed, scale, dh2, given["vec"][:, vec.at["gain2"]])
    made.put("dmid", dmid)
    branch = dmid.astype(bf16)
    made.put("branch_grad", branch)
    made.put("datt", dot_cols(branch, given["wo"][...]))
    for i, values in enumerate([branch.astype(f32), dh2 * normed, dh2, g]):
        made["vec_grad"][:, i * width : (i + 1) * width] = row_sum(values)


def attend_back_kernel(given, made):
    heads_width = made["dq"].shape[1]
    same = given["mask"][...] > 0.5
    for h in range(heads_width // HD):
        cols = slice(h * HD, (h + 1) * HD)
        q, k, v, datt = (given[name][:, cols] for name in ("q", "k", "v", "datt"))
        s = jnp.where(same, dot_cols(q, k) * HD ** (-0.5), masked_score)
        prob = jnp.exp(s - given["log"][:, h : h + 1])
        dprob = dot_cols(datt, v)
        ds = (prob * (dprob - lane_sum(prob * dprob))).astype(bf16)
        made["dq"][:, cols] = (dot(ds, k) * HD ** (-0.5)).astype(bf16)
        made["dk"][:, cols] = (dot_rows(ds, q) * HD ** (-0.5)).astype(bf16)
        made["dv"][:, cols] = dot_rows(prob.astype(bf16), datt).astype(bf16)
    dh1 = dot(made["dq"][...], given["wq"][...])
    dh1 += dot(made["dk"][...], given["wk"][...])
    dh1 += dot(made["dv"][...], given["wv"][...])
    half = dh1.shape[0] // 2
    made.put("dh1_0", dh1[:half, :])
    made.put("dh1_1", dh1[half:, :])
    row = made["vec_grad"]
    row[...] = jnp.zeros_like(row)
    row[:, :heads_width] = row_sum(made["dq"][...].astype(f32))
    second = lane_pad(heads_width)
    row[:, second : second + heads_width] = row_sum(made["dv"][...].astype(f32))


def put_vectors(give_ref, first, rows, values):
    high = values.astype(bf16)
    low = (values - high.astype(f32)).astype(bf16)
    give_ref[first : first + rows, :] = high
    give_ref[first + rows : first + 2 * rows, :] = low
    return high.astype(f32) + low.astype(f32)


def got_vectors(got_ref, rows):
    first = got_ref.shape[0] - 2 * rows
    high = got_ref[first : first + rows, :].astype(f32)
    return high + got_ref[first + rows :, :].astype(f32)


def column_parts(heads_width, total, group):
    for i in range(4):
        first = max(i * heads_width, group * total)
        last = min((i + 1) * heads_width, (group + 1) * total)
        if first < last:
            yield (
                i,
                slice(first - i * heads_width, last - i * heads_width),
                slice(first - group * total, last - group * total),
            )


def attend_weights_kernel(n_dev, orders, vec_names, given, made, h1_t, branch_t, left, branch_left):
    heads_width = given["dq"].shape[1]
    total = 4 * heads_width // len(orders)
    half = given["h1"].shape[1] // 2
    h1_t[...] = jnp.transpose(given["h1"][...].astype(f32))
    branch_t[...] = jnp.transpose(given["branch_grad"][...].astype(f32))
    vec_out = made["vec"]
    columns = vec_out.shape[1]
    vec_out[...] = jnp.zeros_like(vec_out)
    at = 0
    for name in vec_names:
        size = given[name].shape[1]
        done = 0
        while done < size:
            row, lane = (at + done) // columns, (at + done) % columns
            now = min(columns - lane, size - done)
            vec_out[row : row + 1, lane : lane + now] = given[name][:, done : done + now]
            done += now
        at += size
    made.put("vec", put_vectors(made["give0"], half, vec_out.shape[0], vec_out[...]))
    right = ("dq", "dk", "dv", "att")
    for group, order in enumerate(orders):
        ordered_rows(left, h1_t, n_dev, order)
        for i, cols, lanes in column_parts(heads_width, total, group):
            if i == 3:
                ordered_rows(branch_left, branch_t, n_dev, order)
            rows = (branch_left if i == 3 else left)[...].astype(bf16)
            product = dot(rows, given[right[i]][:, cols]).astype(bf16)
            made[f"keep{group}"][:, lanes] = product[:half, :]
            made[f"give{group}"][:half, lanes] = product[half:, :]


def first_back_kernel(vec, given, made):
    width = given["x"].shape[1]
    normed, scale = norm_parts(given["x"][...].astype(f32))
    dh1 = add_halves(given, "dh1")
    made["vec_grad"][:, :width] = row_sum(dh1 * normed)
    made["vec_grad"][:, width:] = row_sum(dh1)
    gain = given["vec"][:, vec.at["gain1"]]
    made.put("dx", given["dmid"][...] + norm_back(normed, scale, dh1, gain))


def back_kernel(n_dev, half_rows, vec, given, made):
    cap = given["dx"].shape[0]
    me, core = place()
    lengths, owners = given["lengths"][...].astype(f32), given["owners"][...].astype(f32)
    base, _ = my_span(lengths, owners, me)
    half, index = block_slots(base, n_dev, cap, half_rows)
    source = jnp.floor(index * (1.0 / half_rows))
    index = jnp.where(half == core, index + source * half_rows, -1e6)
    row = given["vec"]
    out = given["middle"][...] + (add_sums(given, 1) + row[:, vec.at["br"]])
    rows = dot_rows(one_hot(index, (cap, cap), 1), out.astype(bf16))
    rows += dot_rows(one_hot(index + half_rows, (cap, cap), 1), given["dx"][...])
    made.put("back", rows)


def home_kernel(n_dev, half_rows, given, made):
    me, core = place()
    tokens = made["mixed"].shape[0]
    lengths, owners = given["lengths"][...].astype(f32), given["owners"][...].astype(f32)
    half, index = token_slots(lengths, owners, me, n_dev, tokens, half_rows)
    index = index + jnp.floor(index * (1.0 / half_rows)) * half_rows
    index = jnp.where(half == core, index, index + 2 * n_dev * half_rows)
    rows = jnp.concatenate([given["mine"][...], given["other"][...]], axis=0)
    shape = (rows.shape[0], tokens)
    made.put("mixed", dot_rows(one_hot(index, shape, 0), rows))
    made.put("grad", dot_rows(one_hot(index + half_rows, shape, 0), rows))


def share_of(far_bits):
    me = lax.axis_index("dp")
    return 2 * ((me >> far_bits[0]) & 1) + ((me >> far_bits[1]) & 1)


def mlp_weights_kernel(
    far_bits, orders, n_dev, vec, given, made, h2_all, g_all, hidden_all, dexp_all, we_part,
    wr_part, natural, ordered,
):
    cap, width = given["h2"].shape
    half_cap = cap // 2
    me = lax.axis_index("dp")
    share = share_of(far_bits)
    part, hidden_width = we_part.shape[0], given["we"].shape[0]
    be = vec.at["be"].start
    row = given["vec"]
    bias = jnp.zeros((1, part), f32)
    for i in range(4):
        end = min((i + 1) * part, hidden_width)
        piece = row[:, be + i * part : be + end]
        if end < (i + 1) * part:
            piece = jnp.concatenate([piece, jnp.zeros((1, (i + 1) * part - end), f32)], axis=1)
        bias += jnp.where(share == i, piece, 0.0)
    for name, near in (("we", we_part), ("wr", wr_part)):
        source = given[name]

        @pl.when(share < 3)
        def _():
            near[...] = source[pl.ds(pl.multiple_of(share * part, 16), part), :]

        @pl.when(share == 3)
        def _():
            near[: hidden_width - 3 * part, :] = source[3 * part :, :]
            near[hidden_width - 3 * part :, :] = jnp.zeros((4 * part - hidden_width, width), bf16)

    for k in range(4):
        rows = slice(k * cap, (k + 1) * cap)
        if k == 0:
            h2_all[rows, :] = given["h2"][...]
            g_all[rows, :] = given["g"][...]
        else:
            name = f"far_{k}"
            for i, ref in enumerate((given[name], given[name + "_other"])):
                at = slice(k * cap + i * half_cap, k * cap + (i + 1) * half_cap)
                h2_all[at, :] = ref[:half_cap, :]
                g_all[at, :] = ref[half_cap:, :]
        hidden, slope = gelu_both(dot_cols(h2_all[rows, :], we_part[...]) + bias)
        hidden_all[rows, :] = hidden.astype(bf16)
        dexp_all[rows, :] = (dot_cols(g_all[rows, :], wr_part[...]) * slope).astype(bf16)
    half = width // 2
    for name, left, right, order in (
        ("wr", g_all, hidden_all, orders[0]), ("we", h2_all, dexp_all, orders[1]),
    ):
        natural[...] = dot_rows(left[...], right[...])
        ordered_rows(ordered, natural, n_dev, order)
        made.put(name + "_give", ordered[half:, :])
        made.put(name + "_keep", ordered[:half, :])


def turn_kernel(vec_rows, given, made):
    rows = given["keep"].shape[0]
    total = given["keep"][...].astype(f32) + given["got"][:rows, :].astype(f32)
    made.put("keep", total[: rows // 2, :])
    made["give"][: rows // 2, :] = total[rows // 2 :, :].astype(bf16)
    if vec_rows:
        vec = given["vec"][...] + got_vectors(given["got"], vec_rows)
        made.put("vec", put_vectors(made["give"], rows // 2, vec_rows, vec))


def last_kernel(heads_width, vec_rows, count, given, made):
    total = 4 * heads_width // count
    sums = given["vec"][...] + got_vectors(given["0_got"], vec_rows)
    made.put("vec", sums)
    for group in range(count):
        rows = given[f"{group}_keep"].shape[0]
        value = given[f"{group}_keep"][...].astype(f32)
        value += given[f"{group}_got"][:rows, :].astype(f32)
        for i, cols, lanes in column_parts(heads_width, total, group):
            made[("wq", "wk", "wv", "wo")[i]][:, cols] = value[:, lanes]


def mlp_cut_kernel(part, given, made):
    rows = given["wr_keep"].shape[0] // 4
    for name, first in (("wr", 0), ("we", lane_pad(part))):
        total = given[name + "_keep"][...].astype(f32) + given[name + "_got"][...].astype(f32)
        for k in range(4):
            made[f"cut{k}"][:, first : first + part] = total[k * rows : (k + 1) * rows, :].astype(bf16)


def mlp_last_kernel(far_bits, part, given, made):
    share = share_of(far_bits)
    hidden_width = made["wr"].shape[1]
    pieces = [given[f"cut{k}"][...].astype(f32) for k in range(4)]
    for name, first in (("wr", 0), ("we", lane_pad(part))):
        for i in range(4):
            piece = jnp.zeros((made[name].shape[0], part), f32)
            for k in range(4):
                piece += jnp.where((share ^ k) == i, pieces[k][:, first : first + part], 0.0)
            end = min((i + 1) * part, hidden_width)
            made[name][:, i * part : end] = piece[:, : end - i * part]


def swap_cores(values):
    return lax.ppermute(values, "tensor", [(0, 1), (1, 0)])


def swap_halves(values):
    return [swap_cores(rows) for rows in values]


def swap_dp(values, flip):
    return lax.ppermute(values, "dp", [(i, i ^ flip) for i in range(lax.axis_size("dp"))])


def spread(rows):
    return lax.all_to_all(rows, "dp", split_axis=0, concat_axis=0, tiled=True)


def after(values, earlier):
    return lax.optimization_barrier((values, earlier))[0]


def turn(name, pair, vec=None):
    keep, got = pair
    rows = keep.shape[0] // 2
    vec_rows = 0 if vec is None else vec.shape[0]
    if rows % 8:
        total = keep.astype(f32) + got[: 2 * rows].astype(f32)
        kept, give = total[:rows], total[rows:].astype(bf16)
        if vec is not None:
            got = got[2 * rows :].astype(f32)
            vec = vec + (got[:vec_rows] + got[vec_rows:])
            high = vec.astype(bf16)
            low = (vec - high.astype(f32)).astype(bf16)
            vec = high.astype(f32) + low.astype(f32)
            give = jnp.concatenate([give, high, low])
        return (kept, give), vec
    ins = dict(keep=keep, got=got)
    outs = dict(
        keep=((rows, keep.shape[1]), f32), give=((rows + 2 * vec_rows, keep.shape[1]), bf16)
    )
    if vec is not None:
        ins["vec"], outs["vec"] = vec, (vec.shape, f32)
    made = call(functools.partial(turn_kernel, vec_rows), name, ins, outs)
    return (made["keep"], made["give"]), made.get("vec")


def send(pairs, orders, step):
    return [(keep, swap_dp(give, 1 << order[step])) for (keep, give), order in zip(pairs, orders)]


class Chains:
    def __init__(self, pairs, orders, name, vec=None):
        self.pairs, self.orders, self.name, self.vec = list(pairs), orders, name, vec
        self.count = len(pairs)
        self.done = [1] * self.count

    def step(self, group, earlier=None):
        step = self.done[group]
        if step == len(self.orders[group]):
            return None
        self.done[group] += 1
        pair = self.pairs[group] if earlier is None else after(self.pairs[group], earlier)
        vec = None if group else self.vec
        (keep, give), vec = turn(f"{self.name}_turn_{step}_{group}", pair, vec)
        if not group:
            self.vec = vec
        self.pairs[group] = (keep, swap_dp(give, 1 << self.orders[group][step]))
        return keep

    def finish(self):
        for group in range(self.count):
            while self.step(group) is not None:
                pass


def on_device(
    patches, cotangent, image_lengths, image_owner, first_gain, first_shift, query_weight,
    query_bias, key_weight, value_weight, value_bias, output_weight, output_bias, second_gain,
    second_shift, expand_weight, expand_bias, reduce_weight, reduce_bias,
):
    n_dev = lax.axis_size("dp")
    tokens, width = patches.shape
    cap = 2 * tokens
    half_rows = cap // n_dev // 2
    heads_width, hidden_width = query_weight.shape[1], expand_weight.shape[1]
    heads = heads_width // HD
    n_bits = n_dev.bit_length() - 1
    far_bits = (1, n_bits - 2)
    flips = [flip_of(k, far_bits) for k in range(4)]
    rest = [bit for bit in range(n_bits) if bit not in far_bits]
    mlp_orders = (rest, rest[::-1])
    others = list(range(2, n_bits - 2))
    attend_orders = (
        [0, 1] + others + [n_bits - 2, n_bits - 1],
        [1, 0] + others + [n_bits - 2, n_bits - 1],
    )
    wq, wk, wv, wo, we, wr = (
        w.T for w in (query_weight, key_weight, value_weight, output_weight, expand_weight, reduce_weight)
    )
    vec = Vectors(width, heads_width, hidden_width)
    named = dict(
        gain1=first_gain, shift1=first_shift, bo=output_bias, gain2=second_gain,
        shift2=second_shift, br=reduce_bias, be=expand_bias, bq=query_bias, bv=value_bias,
    )
    vectors = jnp.concatenate(
        [jnp.pad(named[n], (0, lane_pad(named[n].shape[0]) - named[n].shape[0])) for n in vec.at]
    ).reshape(1, -1)
    sizes = dict(lengths=image_lengths.reshape(1, -1), owners=image_owner.reshape(1, -1))
    wide32, wide16 = ((cap, width), f32), ((cap, width), bf16)
    half16 = ((cap // 2, width), bf16)
    head16 = ((cap, heads_width), bf16)
    place_args = (n_dev, half_rows)

    packed = call(
        functools.partial(pack_kernel, *place_args, tokens), "pack",
        dict(**sizes, x=patches, g=cotangent), dict(send=wide16), far=True, vmem=62,
    )
    got = spread(packed["send"])
    got_other = swap_cores(got)
    arrived = dict(**sizes, mine=got, other=got_other)
    fwd = call(
        functools.partial(attend_kernel, *place_args, vec), "attend",
        dict(**arrived, vec=vectors, wq=wq, wk=wk, wv=wv, wo=wo),
        dict(
            mask=((cap, cap), f32), x=wide16, h1=wide16, q=head16, k=head16, v=head16,
            log=((cap, heads), f32), att=head16, branch=wide16,
        ),
    )
    branch_other = swap_cores(fwd["branch"])
    g = call(
        functools.partial(unpack_kernel, *place_args), "unpack", arrived, dict(g=wide16)
    )["g"]
    mlp = call(
        functools.partial(mlp_kernel, *place_args, vec), "mlp",
        dict(
            x=fwd["x"], branch=fwd["branch"], branch_other=branch_other, g=g, vec=vectors, we=we, wr=wr
        ),
        dict(
            middle=wide32, h2=wide16, halves=wide16, sums_0=wide16, sums_1=wide16,
            be_grad=((1, lane_pad(hidden_width)), f32),
        ),
        scratch=[pltpu.VMEM((cap, width), f32)] * 2, vmem=16,
    )
    halves = [swap_dp(mlp["halves"], flip) for flip in flips[1:]]
    sums_other = swap_halves([mlp["sums_0"], mlp["sums_1"]])
    sums = dict(
        sums_0=mlp["sums_0"], sums_1=mlp["sums_1"], sums_0_other=sums_other[0],
        sums_1_other=sums_other[1],
    )
    back = call(
        functools.partial(middle_back_kernel, vec), "middle_back",
        dict(
            g=g, middle=mlp["middle"], vec=vectors, wo=wo, **sums,
        ),
        dict(dmid=wide32, branch_grad=wide16, datt=head16, vec_grad=((1, 4 * width), f32)),
    )
    att_back = call(
        attend_back_kernel, "attend_back",
        dict(
            mask=fwd["mask"], q=fwd["q"], k=fwd["k"], v=fwd["v"], datt=back["datt"], log=fwd["log"],
            wq=wq, wk=wk, wv=wv,
        ),
        dict(
            dq=head16, dk=head16, dv=head16, dh1_0=half16, dh1_1=half16,
            vec_grad=((1, 2 * lane_pad(heads_width)), f32),
        ),
    )
    dh1_other = swap_halves([att_back["dh1_0"], att_back["dh1_1"]])
    first = call(
        functools.partial(first_back_kernel, vec), "first_back",
        dict(
            x=fwd["x"], dh1_0=att_back["dh1_0"], dh1_1=att_back["dh1_1"], dh1_0_other=dh1_other[0],
            dh1_1_other=dh1_other[1], vec=vectors, dmid=back["dmid"],
        ),
        dict(dx=wide16, vec_grad=((1, 2 * width), f32)),
    )

    n_groups = len(attend_orders)
    columns = 4 * heads_width // n_groups
    vec_rows = -(-vec.size // (16 * columns)) * 16
    vec_shape = ((vec_rows, columns), f32)
    group_outs = {}
    for i in range(n_groups):
        more = 0 if i else 2 * vec_rows
        group_outs[f"keep{i}"] = ((width // 2, columns), bf16)
        group_outs[f"give{i}"] = ((width // 2 + more, columns), bf16)
    vec_parts = dict(
        v1=first["vec_grad"], v2=back["vec_grad"], v3=mlp["be_grad"], v4=att_back["vec_grad"]
    )
    pieces = call(
        functools.partial(attend_weights_kernel, n_dev, attend_orders, list(vec_parts)),
        "attend_weights",
        dict(
            h1=fwd["h1"], branch_grad=back["branch_grad"], dq=att_back["dq"], dk=att_back["dk"],
            dv=att_back["dv"], att=fwd["att"], **vec_parts,
        ),
        dict(vec=vec_shape, **group_outs),
        scratch=[pltpu.VMEM((width, cap), f32)] * 4, vmem=16,
    )
    pairs = [(pieces[f"keep{i}"], pieces[f"give{i}"]) for i in range(n_groups)]
    attend = Chains(send(pairs, attend_orders, 0), attend_orders, "attend", pieces["vec"])
    dx = after(first["dx"], pieces["keep0"])
    packed = call(
        functools.partial(back_kernel, *place_args, vec), "back",
        dict(**sizes, vec=vectors, middle=mlp["middle"], dx=dx, **sums), dict(back=wide16),
    )
    home = spread(packed["back"])
    halves = after(halves, packed["back"])
    far = {f"far_{k + 1}": rows for k, rows in enumerate(halves)}
    for k in (1, 2):
        far[f"far_{k}_other"] = swap_cores(far[f"far_{k}"])
    far["far_3"] = after(far["far_3"], far["far_1_other"])
    far["far_3_other"] = swap_cores(far["far_3"])
    part = lane_pad(-(-hidden_width // 4))
    mlp_half = ((width // 2, part), bf16)
    all_rows = pltpu.VMEM((4 * cap, width), bf16)
    all_hidden = pltpu.VMEM((4 * cap, part), bf16)
    grads = call(
        functools.partial(
            mlp_weights_kernel, far_bits, [list(o) + list(far_bits) for o in mlp_orders], n_dev, vec
        ),
        "mlp_weights",
        dict(vec=vectors, we=we, wr=wr, h2=mlp["h2"], g=g, **far),
        dict(wr_give=mlp_half, wr_keep=mlp_half, we_give=mlp_half, we_keep=mlp_half),
        scratch=[all_rows, all_rows, all_hidden, all_hidden]
        + [pltpu.VMEM((part, width), bf16)] * 2 + [pltpu.VMEM((width, part), f32)] * 2,
        vmem=32,
    )
    pairs = [(grads["wr_keep"], grads["wr_give"]), (grads["we_keep"], grads["we_give"])]
    mlp_sums = Chains(send(pairs, mlp_orders, 0), mlp_orders, "mlp")
    last = grads["wr_keep"]
    last = attend.step(0, last)
    last = attend.step(1, last)
    last = mlp_sums.step(0, last)
    last = attend.step(0, last)
    last = attend.step(1, last)
    last = mlp_sums.step(1, last)
    last = attend.step(0, last)
    last = attend.step(1, last)
    for chain in (mlp_sums, attend):
        chain.finish()
    pairs, mlp_pairs, vec_sum = attend.pairs, mlp_sums.pairs, attend.vec
    cut_shape = ((width // n_dev, 2 * lane_pad(part)), bf16)
    cuts = call(
        functools.partial(mlp_cut_kernel, part), "mlp_cut",
        dict(
            wr_keep=mlp_pairs[0][0], wr_got=mlp_pairs[0][1],
            we_keep=mlp_pairs[1][0], we_got=mlp_pairs[1][1],
        ),
        {f"cut{k}": cut_shape for k in range(4)},
    )
    cuts = [cuts["cut0"]] + [swap_dp(cuts[f"cut{k}"], flips[k]) for k in range(1, 4)]
    mixed_grad = call(
        functools.partial(home_kernel, *place_args), "home",
        dict(**sizes, mine=home, other=swap_cores(home)),
        dict(mixed=((tokens, width), bf16), grad=((tokens, width), bf16)),
    )
    own_rows = width // n_dev
    mlp_own = call(
        functools.partial(mlp_last_kernel, far_bits, part), "mlp_last",
        {f"cut{k}": cut for k, cut in enumerate(cuts)},
        dict(wr=((own_rows, hidden_width), f32), we=((own_rows, hidden_width), f32)),
    )
    ins = dict(vec=vec_sum)
    for i, (keep, received) in enumerate(pairs):
        ins[f"{i}_keep"], ins[f"{i}_got"] = keep, received
    outs = dict(vec=vec_shape)
    outs.update({name: ((own_rows, heads_width), f32) for name in ("wq", "wk", "wv", "wo")})
    own = call(
        functools.partial(last_kernel, heads_width, vec_rows, n_groups), "last", ins, outs
    )
    grads = own["vec"].reshape(-1)
    total = {name: grads[at] for name, at in vec.at.items()}
    return (
        mixed_grad["mixed"], mixed_grad["grad"], total["gain1"], total["shift1"], own["wq"],
        total["bq"], own["wk"], own["wv"], total["bv"], own["wo"], total["bo"], total["gain2"],
        total["shift2"], mlp_own["we"], total["be"], mlp_own["wr"], total["br"],
    )


def solution(mesh):
    rows, all_same = P("dp", None), P()
    cols, vector = P(None, "tensor"), P("tensor")
    both = P("dp", "tensor")
    in_specs = (
        rows, rows, all_same, all_same, all_same, all_same, cols, vector, cols, cols, vector, cols,
        all_same, all_same, all_same, cols, vector, cols, all_same,
    )
    out_specs = (
        rows, rows, all_same, all_same, both, vector, both, both, vector, both, all_same, all_same,
        all_same, both, vector, both, all_same,
    )
    return jax.shard_map(
        on_device, mesh=mesh, in_specs=in_specs, out_specs=out_specs, check_vma=False
    )
```

time: 226 us -> 194 us (0.86)
  starting transfers between devices: 46.7 us -> 35.8 us
  Pallas kernels: 62.9 us -> 54.5 us
  local copies, waits for them, and re-layouts: 28.4 us -> 21.6 us
  waiting for transfers between devices: 83.8 us -> 80.3 us
    ppermute x25 -> x18, starting transfers between devices: 33.2 us -> 21.7 us  [swap_dp(): lax.ppermute(values, 'dp', [(i, i ^ flip) for i in range(lax.axis_size('d...]
    pallas_call x17 -> x22, Pallas kernels: 62.9 us -> 54.5 us  [call(): pl.pallas_call(kernel, name=name, out_shape=[jax.ShapeDtypeStruct(shape,...]
    ppermute x25 -> x18, waiting for transfers between devices: 63.7 us -> 59.5 us  [swap_dp(): lax.ppermute(values, 'dp', [(i, i ^ flip) for i in range(lax.axis_size('d...]
    slice x5 -> x3, local copies, waits for them, and re-layouts: 5.05 us -> 1.88 us  [on_device(): total = {name: grads[at] for name, at in vec.at.items()}]
    unnamed x97 -> x82, local copies, waits for them, and re-layouts: 22.4 us -> 19.7 us
    ppermute x7 -> x10, waiting for transfers between devices: 3.93 us -> 4.63 us  [swap_cores(): return lax.ppermute(values, 'tensor', [(0, 1), (1, 0)])]
  transfers between devices with their start and end apart: 34 -> 30, of which waited for: 15 -> 16; matrix products, arithmetic and copies ran while one was open for 4% -> 0% of each run, Pallas kernels for 20% -> 19%
where the time goes in v3:
time: 194 us; the launch traced here: 193 us
  waiting for transfers between devices  80.3 us (41%)
  Pallas kernels  54.5 us (28%)
  starting transfers between devices  35.8 us (18%)
  local copies, waits for them, and re-layouts  21.6 us (11%)
    ppermute x18, waiting for transfers between devices, swap_dp(): lax.ppermute(values, 'dp', [(i, i ^ flip) for i in range(lax.axis_size('d...  59.5 us
    pallas_call x22, Pallas kernels, call(): pl.pallas_call(kernel, name=name, out_shape=[jax.ShapeDtypeStruct(shape,...  54.5 us
    ppermute x18, starting transfers between devices, swap_dp(): lax.ppermute(values, 'dp', [(i, i ^ flip) for i in range(lax.axis_size('d...  21.7 us
    unnamed x82, local copies, waits for them, and re-layouts  19.7 us
    all_to_all x2, waiting for transfers between devices, spread(): return lax.all_to_all(rows, 'dp', split_axis=0, concat_axis=0, tiled=True)  16.2 us
    all_to_all x2, starting transfers between devices, spread(): return lax.all_to_all(rows, 'dp', split_axis=0, concat_axis=0, tiled=True)  12.3 us
    ppermute x10, waiting for transfers between devices, swap_cores(): return lax.ppermute(values, 'tensor', [(0, 1), (1, 0)])  4.63 us
  transfers between devices with their start and end apart: 30, of which 16 were waited for; matrix products, arithmetic and copies ran while one was open for 0% of the time, Pallas kernels for 19%

profile of v3, /device:TPU:0, one launch (start us, length us, event | category | flops | bytes accessed | tf_op | source)
XLA Modules:
  0.0 193.3 jit_solution(13537318743388043985)
XLA Ops:
  0.8 2.5 %pack.1 = bf16[256,1152]{1,0:T(8,128)(2,1)} custom-call(s32[1,64]{1,0:T(1,128)} %bitcast.31, s32[1,64]{1,0:T(1,128)} %bitcast.36, bf16[128,1152]{1,0:T(8,128)(2,1)} %refs_2_.1, bf16[128,1152]{1,0:T(8,128)(2,1)} %refs_3_.1), custom_call_target="tpu_custom_call" | custom-call | tf_op jit(solution)/shard_map/pack/pallas_call | solution.py:180
  3.3 8.5 %all-to-all-start = ((bf16[16,16,1152]{2,1,0:T(8,128)(2,1)}), bf16[16,16,1152]{2,1,0:T(8,128)(2,1)S(1)}, u32[]{:S(2)}, u32[]{:S(2)}) async-start(bf16[16,16,1152]{2,1,0:T(8,128)(2,1)} %bitcast.41), calls=%async_computation | async-start | bytes 1179648 | tf_op jit(solution)/shard_map/all_to_all | solution.py:590
  11.8 16.2 %all-to-all-done = bf16[16,16,1152]{2,1,0:T(8,128)(2,1)S(1)} async-done(((bf16[16,16,1152]{2,1,0:T(8,128)(2,1)}), bf16[16,16,1152]{2,1,0:T(8,128)(2,1)S(1)}, u32[]{:S(2)}, u32[]{:S(2)}) %all-to-all-start) | async-done | bytes 589856 | tf_op jit(solution)/shard_map/all_to_all | solution.py:590
  34.0 5.1 %attend.1 = (f32[256,256]{1,0:T(8,128)S(1)}, bf16[256,1152]{1,0:T(8,128)(2,1)S(1)}, bf16[256,1152]{1,0:T(8,128)(2,1)S(1)}, bf16[256,576]{1,0:T(8,128)(2,1)S(1)},...) custom-call(s32[1,64]{1,0:T(1,128)S(1)} %bitcast.32, ...), custom_call_target="tpu_custom_call" | custom-call | tf_op jit(solution)/shard_map/attend/pallas_call | solution.py:180
  41.3 2.4 %copy-done.1 = bf16[1152,2152]{0,1:T(8,128)(2,1)S(1)} copy-done((bf16[1152,2152]{0,1:T(8,128)(2,1)S(1)}, bf16[1152,2152]{0,1:T(8,128)(2,1)}, u32[]{:S(2)}) %copy-start.1) | copy-done | bytes 4958232
  43.7 8.5 %mlp.1 = (f32[256,1152]{1,0:T(8,128)S(1)}, bf16[256,1152]{1,0:T(8,128)(2,1)S(1)}, bf16[256,1152]{1,0:T(8,128)(2,1)S(1)}, bf16[256,1152]{1,0:T(8,128)(2,1)S(1)}, ...) custom-call(bf16[256,1152]{1,0:T(8,128)(2,1)S(1)} %get-tuple-element.106.refs_0_, ...), custom_call_target="tpu_custom_call" | custom-call | tf_op jit(solution)/shard_map/mlp/pallas_call | solution.py:180
  59.2 5.5 %attend_back.1 = (bf16[256,576]{1,0:T(8,128)(2,1)S(1)}, bf16[256,576]{1,0:T(8,128)(2,1)S(1)}, bf16[256,576]{1,0:T(8,128)(2,1)S(1)}, bf16[128,1152]{1,0:T(8,128)(...) custom-call(f32[256,256]{1,0:T(8,128)S(1)} %get-tuple-element.109.refs_0_, ...), custom_call_target="tpu_custom_call" | custom-call | tf_op jit(solution)/shard_map/attend_back/pallas_call | solution.py:180
  67.8 3.8 %attend_weights.1 = (f32[16,1152]{1,0:T(8,128)S(1)}, bf16[576,1152]{1,0:T(8,128)(2,1)S(1)}, bf16[608,1152]{1,0:T(8,128)(2,1)}, bf16[576,1152]{1,0:T(8,128)(2,1)S(1)}, bf16[576,1152]{1,0:T(8,128)(2,1)}) custom-call(bf16[256,1152]{1,0:T(8,128)(2,1)S(1)} %get-tuple-element.121.refs_0_, bf16[256,1152]{1,0:T(8,128)(2,1)S(1)} %get-tuple-element.122.refs_1_, ...), custom_call_target="tpu_custom_call" | custom-call | tf_op jit(solution)/shard_map/attend_weights/pallas_call | solution.py:180
  74.8 8.1 %collective-permute-done.9.refs_6_ = bf16[256,1152]{1,0:T(8,128)(2,1)} collective-permute-done((bf16[256,1152]{1,0:T(8,128)(2,1)S(1)}, bf16[256,1152]{1,0:T(8,128)(2,1)}, u32[]{:S(2)}, u32[]{:S(2)}) %collective-permute-start.9) | collective-permute-done | bytes 589856 | tf_op jit(solution)/shard_map/ppermute | solution.py:586
  86.0 3.8 %all-to-all-start.1 = ((bf16[16,16,1152]{2,1,0:T(8,128)(2,1)}), bf16[16,16,1152]{2,1,0:T(8,128)(2,1)S(1)}, u32[]{:S(2)}, u32[]{:S(2)}) async-start(bf16[16,16,1152]{2,1,0:T(8,128)(2,1)} %bitcast.10), calls=%async_computation.1 | async-start | bytes 1179648 | tf_op jit(solution)/shard_map/all_to_all | solution.py:590
  89.9 2.4 %copy-done = bf16[1152,2152]{0,1:T(8,128)(2,1)S(1)} copy-done((bf16[1152,2152]{0,1:T(8,128)(2,1)S(1)}, bf16[1152,2152]{0,1:T(8,128)(2,1)}, u32[]{:S(2)}) %copy-start) | copy-done | bytes 4958232
  92.3 2.4 %copy-done.2 = bf16[1152,2152]{0,1:T(8,128)(2,1)S(1)} copy-done((bf16[1152,2152]{0,1:T(8,128)(2,1)S(1)}, bf16[1152,2152]{0,1:T(8,128)(2,1)}, u32[]{:S(2)}) %copy-start.2) | copy-done | bytes 4958232
  96.8 11.4 %mlp_weights.1 = (bf16[576,640]{1,0:T(8,128)(2,1)}, bf16[576,640]{1,0:T(8,128)(2,1)S(1)}, bf16[576,640]{1,0:T(8,128)(2,1)}, bf16[576,640]{1,0:T(8,128)(2,1)S(1)}) custom-call(f32[1,10368]{1,0:T(1,128)S(1)} %reshape.58.refs_4_.refs_2_.refs_5_.refs_0_, bf16[2152,1152]{1,0:T(8,128)(2,1)S(1)} %bitcast.15, bf16[2152,1152]{1,0:T(8,128)(2,1)S(1)} %bitcast.17, ...), custom_call_target="tpu_custom_call" | custom-call | tf_op jit(solution)/shard_map/mlp_weights/pallas_call | solution.py:180
  111.3 2.5 %attend_turn_1_0.1 = (f32[288,1152]{1,0:T(8,128)S(1)}, bf16[320,1152]{1,0:T(8,128)(2,1)}, f32[16,1152]{1,0:T(8,128)S(1)}) custom-call(bf16[576,1152]{1,0:T(8,128)(2,1)S(1)} %copy-done.13, bf16[608,1152]{1,0:T(8,128)(2,1)} %collective-permute-done.7.refs_1_, f32[16,1152]{1,0:T(8,128)S(1)} %get-tuple-element.145.refs_2_), custom_call_target="tpu_custom_call" | custom-call | tf_op jit(solution)/shard_map/attend_turn_1_0/pallas_call | solution.py:180
  116.4 5.1 %collective-permute-done.16.refs_1_ = bf16[576,1152]{1,0:T(8,128)(2,1)} collective-permute-done((bf16[576,1152]{1,0:T(8,128)(2,1)}, bf16[576,1152]{1,0:T(8,128)(2,1)}, u32[]{:S(2)}, u32[]{:S(2)}) %collective-permute-start.16) | collective-permute-done | bytes 1327136 | tf_op jit(solution)/shard_map/ppermute | solution.py:586
  125.5 3.0 %collective-permute-done.15.refs_1_ = bf16[576,640]{1,0:T(8,128)(2,1)} collective-permute-done((bf16[576,640]{1,0:T(8,128)(2,1)}, bf16[576,640]{1,0:T(8,128)(2,1)}, u32[]{:S(2)}, u32[]{:S(2)}) %collective-permute-start.15) | collective-permute-done | bytes 737312 | tf_op jit(solution)/shard_map/ppermute | solution.py:586
  130.9 6.8 %collective-permute-done.14.refs_1_ = bf16[320,1152]{1,0:T(8,128)(2,1)} collective-permute-done((bf16[320,1152]{1,0:T(8,128)(2,1)}, bf16[320,1152]{1,0:T(8,128)(2,1)}, u32[]{:S(2)}, u32[]{:S(2)}) %collective-permute-start.14) | collective-permute-done | bytes 737312 | tf_op jit(solution)/shard_map/ppermute | solution.py:586
  142.1 8.2 %collective-permute-done.18.refs_1_ = bf16[576,640]{1,0:T(8,128)(2,1)} collective-permute-done((bf16[576,640]{1,0:T(8,128)(2,1)}, bf16[576,640]{1,0:T(8,128)(2,1)}, u32[]{:S(2)}, u32[]{:S(2)}) %collective-permute-start.18) | collective-permute-done | bytes 737312 | tf_op jit(solution)/shard_map/ppermute | solution.py:586
  152.7 12.5 %collective-permute-done.17.refs_1_ = bf16[176,1152]{1,0:T(8,128)(2,1)S(1)} collective-permute-done((bf16[176,1152]{1,0:T(8,128)(2,1)S(1)}, bf16[176,1152]{1,0:T(8,128)(2,1)S(1)}, u32[]{:S(2)}, u32[]{:S(2)}) %collective-permute-start.17) | collective-permute-done | bytes 405536 | tf_op jit(solution)/shard_map/ppermute | solution.py:586
  166.9 2.5 %collective-permute-start.25 = (bf16[72,1280]{1,0:T(8,128)(2,1)S(1)}, bf16[72,1280]{1,0:T(8,128)(2,1)S(1)}, u32[]{:S(2)}, u32[]{:S(2)}) collective-permute-start(bf16[72,1280]{1,0:T(8,128)(2,1)S(1)} %get-tuple-element.190), channel_id=1, source_target_pairs={{0,8},{2,10},{4,12},{6,14},{8,0},{10,2},{12,4},{14,6},{16,24},{18,... | collective-permute-start | bytes 552968 | tf_op jit(solution)/shard_map/ppermute | solution.py:586
  170.0 3.1 %collective-permute-done.21.refs_1_ = bf16[144,1152]{1,0:T(8,128)(2,1)S(1)} collective-permute-done((bf16[144,1152]{1,0:T(8,128)(2,1)S(1)}, bf16[144,1152]{1,0:T(8,128)(2,1)S(1)}, u32[]{:S(2)}, u32[]{:S(2)}) %collective-permute-start.21) | collective-permute-done | bytes 331808 | tf_op jit(solution)/shard_map/ppermute | solution.py:586
  173.1 4.0 %collective-permute-start.22 = (bf16[72,1152]{1,0:T(8,128)(2,1)S(1)}, bf16[72,1152]{1,0:T(8,128)(2,1)S(1)}, u32[]{:S(2)}, u32[]{:S(2)}) collective-permute-start(bf16[72,1152]{1,0:T(8,128)(2,1)S(1)} %get-tuple-element.181), channel_id=1, source_target_pairs={{0,16},{2,18},{4,20},{6,22},{8,24},{10,26},{12,28},{14,30},{16,0},... | collective-permute-start | bytes 497672 | tf_op jit(solution)/shard_map/ppermute | solution.py:586
  178.5 6.4 %collective-permute-done.25.refs_1_ = bf16[72,1280]{1,0:T(8,128)(2,1)S(1)} collective-permute-done((bf16[72,1280]{1,0:T(8,128)(2,1)S(1)}, bf16[72,1280]{1,0:T(8,128)(2,1)S(1)}, u32[]{:S(2)}, u32[]{:S(2)}) %collective-permute-start.25) | collective-permute-done | bytes 184352 | tf_op jit(solution)/shard_map/ppermute | solution.py:586
  184.9 4.2 %collective-permute-done.27.refs_3_ = bf16[72,1280]{1,0:T(8,128)(2,1)S(1)} collective-permute-done((bf16[72,1280]{1,0:T(8,128)(2,1)S(1)}, bf16[72,1280]{1,0:T(8,128)(2,1)S(1)}, u32[]{:S(2)}, u32[]{:S(2)}) %collective-permute-start.27) | collective-permute-done | bytes 184352 | tf_op jit(solution)/shard_map/ppermute | solution.py:586
  (148 shorter events, 53.2 us)
Async XLA Ops:
  3.3 24.7 %all-to-all-start = ((bf16[16,16,1152]{2,1,0:T(8,128)(2,1)}), bf16[16,16,1152]{2,1,0:T(8,128)(2,1)S(1)}, u32[]{:S(2)}, u32[]{:S(2)}) async-start(bf16[16,16,1152]{2,1,0:T(8,128)(2,1)} %bitcast.41), calls=%async_computation | async-start | bytes 1179648 | tf_op jit(solution)/shard_map/all_to_all | solution.py:590
  53.0 4.0 %collective-permute-start.2 = (bf16[256,1152]{1,0:T(8,128)(2,1)S(1)}, bf16[256,1152]{1,0:T(8,128)(2,1)S(1)}, u32[]{:S(2)}, u32[]{:S(2)}) collective-permute-start(bf16[256,1152]{1,0:T(8,128)(2,1)S(1)} %get-tuple-element.113.refs_4_.refs_5_), channel_id=1, source_target_pairs={{0,1},{1,0},{2,3},{3,2},{4,5},{5,4},{6,7},{7,6},{8,9},{9,8},{10,11... | collective-permute-start | bytes 1769480 | tf_op jit(solution)/shard_map/ppermute | solution.py:578
  53.5 21.3 %collective-permute-start.8 = (bf16[256,1152]{1,0:T(8,128)(2,1)S(1)}, bf16[256,1152]{1,0:T(8,128)(2,1)S(1)}, u32[]{:S(2)}, u32[]{:S(2)}) collective-permute-start(bf16[256,1152]{1,0:T(8,128)(2,1)S(1)} %get-tuple-element.137), channel_id=1, source_target_pairs={{0,8},{2,10},{4,12},{6,14},{8,0},{10,2},{12,4},{14,6},{16,24},{18,... | collective-permute-start | bytes 1769480 | tf_op jit(solution)/shard_map/ppermute | solution.py:586
  55.0 27.8 %collective-permute-start.9 = (bf16[256,1152]{1,0:T(8,128)(2,1)S(1)}, bf16[256,1152]{1,0:T(8,128)(2,1)}, u32[]{:S(2)}, u32[]{:S(2)}) collective-permute-start(bf16[256,1152]{1,0:T(8,128)(2,1)S(1)} %get-tuple-element.137), channel_id=1, source_target_pairs={{0,4},{2,6},{4,0},{6,2},{8,12},{10,14},{12,8},{14,10},{16,20},{18,... | collective-permute-start | bytes 1769480 | tf_op jit(solution)/shard_map/ppermute | solution.py:586
  56.0 26.9 %collective-permute-start.10 = (bf16[256,1152]{1,0:T(8,128)(2,1)S(1)}, bf16[256,1152]{1,0:T(8,128)(2,1)}, u32[]{:S(2)}, u32[]{:S(2)}) collective-permute-start(bf16[256,1152]{1,0:T(8,128)(2,1)S(1)} %get-tuple-element.137), channel_id=1, source_target_pairs={{0,12},{2,14},{4,8},{6,10},{8,4},{10,6},{12,0},{14,2},{16,28},{18,... | collective-permute-start | bytes 1769480 | tf_op jit(solution)/shard_map/ppermute | solution.py:586
  72.7 38.6 %collective-permute-start.7 = (bf16[608,1152]{1,0:T(8,128)(2,1)}, bf16[608,1152]{1,0:T(8,128)(2,1)}, u32[]{:S(2)}, u32[]{:S(2)}) collective-permute-start(bf16[608,1152]{1,0:T(8,128)(2,1)} %get-tuple-element.135), channel_id=1, source_target_pairs={{0,2},{2,0},{4,6},{6,4},{8,10},{10,8},{12,14},{14,12},{16,18},{18,... | collective-permute-start | bytes 4202504 | tf_op jit(solution)/shard_map/ppermute | solution.py:586
  83.7 37.8 %collective-permute-start.16 = (bf16[576,1152]{1,0:T(8,128)(2,1)}, bf16[576,1152]{1,0:T(8,128)(2,1)}, u32[]{:S(2)}, u32[]{:S(2)}) collective-permute-start(bf16[576,1152]{1,0:T(8,128)(2,1)} %get-tuple-element.150), channel_id=1, source_target_pairs={{0,4},{2,6},{4,0},{6,2},{8,12},{10,14},{12,8},{14,10},{16,20},{18,... | collective-permute-start | bytes 3981320 | tf_op jit(solution)/shard_map/ppermute | solution.py:586
  84.7 5.2 %collective-permute-start.12 = (bf16[256,1152]{1,0:T(8,128)(2,1)}, bf16[256,1152]{1,0:T(8,128)(2,1)}, u32[]{:S(2)}, u32[]{:S(2)}) collective-permute-start(bf16[256,1152]{1,0:T(8,128)(2,1)} %collective-permute-done.9.refs_6_), channel_id=1, source_target_pairs={{0,1},{1,0},{2,3},{3,2},{4,5},{5,4},{6,7},{7,6},{8,9},{9,8},{10,11... | collective-permute-start | bytes 1769480 | tf_op jit(solution)/shard_map/ppermute | solution.py:578
  85.7 4.1 %collective-permute-start.13 = (bf16[256,1152]{1,0:T(8,128)(2,1)}, bf16[256,1152]{1,0:T(8,128)(2,1)}, u32[]{:S(2)}, u32[]{:S(2)}) collective-permute-start(bf16[256,1152]{1,0:T(8,128)(2,1)} %collective-permute-done.10.refs_7_), channel_id=1, source_target_pairs={{0,1},{1,0},{2,3},{3,2},{4,5},{5,4},{6,7},{7,6},{8,9},{9,8},{10,11... | collective-permute-start | bytes 1769480 | tf_op jit(solution)/shard_map/ppermute | solution.py:578
  86.0 39.5 %all-to-all-start.1 = ((bf16[16,16,1152]{2,1,0:T(8,128)(2,1)}), bf16[16,16,1152]{2,1,0:T(8,128)(2,1)S(1)}, u32[]{:S(2)}, u32[]{:S(2)}) async-start(bf16[16,16,1152]{2,1,0:T(8,128)(2,1)} %bitcast.10), calls=%async_computation.1 | async-start | bytes 1179648 | tf_op jit(solution)/shard_map/all_to_all | solution.py:590
  108.2 20.3 %collective-permute-start.15 = (bf16[576,640]{1,0:T(8,128)(2,1)}, bf16[576,640]{1,0:T(8,128)(2,1)}, u32[]{:S(2)}, u32[]{:S(2)}) collective-permute-start(bf16[576,640]{1,0:T(8,128)(2,1)} %get-tuple-element.148), channel_id=1, source_target_pairs={{0,2},{2,0},{4,6},{6,4},{8,10},{10,8},{12,14},{14,12},{16,18},{18,... | collective-permute-start | bytes 2211848 | tf_op jit(solution)/shard_map/ppermute | solution.py:586
  113.8 23.8 %collective-permute-start.14 = (bf16[320,1152]{1,0:T(8,128)(2,1)}, bf16[320,1152]{1,0:T(8,128)(2,1)}, u32[]{:S(2)}, u32[]{:S(2)}) collective-permute-start(bf16[320,1152]{1,0:T(8,128)(2,1)} %get-tuple-element.147), channel_id=1, source_target_pairs={{0,4},{2,6},{4,0},{6,2},{8,12},{10,14},{12,8},{14,10},{16,20},{18,... | collective-permute-start | bytes 2211848 | tf_op jit(solution)/shard_map/ppermute | solution.py:586
  114.9 35.4 %collective-permute-start.18 = (bf16[576,640]{1,0:T(8,128)(2,1)}, bf16[576,640]{1,0:T(8,128)(2,1)}, u32[]{:S(2)}, u32[]{:S(2)}) collective-permute-start(bf16[576,640]{1,0:T(8,128)(2,1)} %get-tuple-element.163), channel_id=1, source_target_pairs={{0,16},{2,18},{4,20},{6,22},{8,24},{10,26},{12,28},{14,30},{16,0},... | collective-permute-start | bytes 2211848 | tf_op jit(solution)/shard_map/ppermute | solution.py:586
  124.9 17.1 %collective-permute-start.19 = (bf16[288,1152]{1,0:T(8,128)(2,1)}, bf16[288,1152]{1,0:T(8,128)(2,1)S(1)}, u32[]{:S(2)}, u32[]{:S(2)}) collective-permute-start(bf16[288,1152]{1,0:T(8,128)(2,1)} %get-tuple-element.164), channel_id=1, source_target_pairs={{0,2},{2,0},{4,6},{6,4},{8,10},{10,8},{12,14},{14,12},{16,18},{18,... | collective-permute-start | bytes 1990664 | tf_op jit(solution)/shard_map/ppermute | solution.py:586
  125.5 47.6 %collective-permute-start.6 = (bf16[256,1152]{1,0:T(8,128)(2,1)S(1)}, bf16[256,1152]{1,0:T(8,128)(2,1)S(1)}, u32[]{:S(2)}, u32[]{:S(2)}) collective-permute-start(bf16[256,1152]{1,0:T(8,128)(2,1)S(1)} %bitcast.29), channel_id=1, source_target_pairs={{0,1},{1,0},{2,3},{3,2},{4,5},{5,4},{6,7},{7,6},{8,9},{9,8},{10,11... | collective-permute-start | bytes 1769480 | tf_op jit(solution)/shard_map/ppermute | solution.py:578
  139.0 26.2 %collective-permute-start.17 = (bf16[176,1152]{1,0:T(8,128)(2,1)S(1)}, bf16[176,1152]{1,0:T(8,128)(2,1)S(1)}, u32[]{:S(2)}, u32[]{:S(2)}) collective-permute-start(bf16[176,1152]{1,0:T(8,128)(2,1)S(1)} %get-tuple-element.161), channel_id=1, source_target_pairs={{0,8},{2,10},{4,12},{6,14},{8,0},{10,2},{12,4},{14,6},{16,24},{18,... | collective-permute-start | bytes 1216520 | tf_op jit(solution)/shard_map/ppermute | solution.py:586
  139.7 27.0 %collective-permute-start.23 = (bf16[288,640]{1,0:T(8,128)(2,1)S(1)}, bf16[288,640]{1,0:T(8,128)(2,1)S(1)}, u32[]{:S(2)}, u32[]{:S(2)}) collective-permute-start(bf16[288,640]{1,0:T(8,128)(2,1)S(1)} %get-tuple-element.187), channel_id=1, source_target_pairs={{0,16},{2,18},{4,20},{6,22},{8,24},{10,26},{12,28},{14,30},{16,0},... | collective-permute-start | bytes 1105928 | tf_op jit(solution)/shard_map/ppermute | solution.py:586
  151.6 15.1 %collective-permute-start.24 = (bf16[288,640]{1,0:T(8,128)(2,1)S(1)}, bf16[288,640]{1,0:T(8,128)(2,1)S(1)}, u32[]{:S(2)}, u32[]{:S(2)}) collective-permute-start(bf16[288,640]{1,0:T(8,128)(2,1)S(1)} %get-tuple-element.188), channel_id=1, source_target_pairs={{0,2},{2,0},{4,6},{6,4},{8,10},{10,8},{12,14},{14,12},{16,18},{18,... | collective-permute-start | bytes 1105928 | tf_op jit(solution)/shard_map/ppermute | solution.py:586
  152.7 20.3 %collective-permute-start.21 = (bf16[144,1152]{1,0:T(8,128)(2,1)S(1)}, bf16[144,1152]{1,0:T(8,128)(2,1)S(1)}, u32[]{:S(2)}, u32[]{:S(2)}) collective-permute-start(bf16[144,1152]{1,0:T(8,128)(2,1)S(1)} %get-tuple-element.177), channel_id=1, source_target_pairs={{0,8},{2,10},{4,12},{6,14},{8,0},{10,2},{12,4},{14,6},{16,24},{18,... | collective-permute-start | bytes 995336 | tf_op jit(solution)/shard_map/ppermute | solution.py:586
  165.2 25.2 %collective-permute-start.20 = (bf16[104,1152]{1,0:T(8,128)(2,1)S(1)}, bf16[104,1152]{1,0:T(8,128)(2,1)S(1)}, u32[]{:S(2)}, u32[]{:S(2)}) collective-permute-start(bf16[104,1152]{1,0:T(8,128)(2,1)S(1)} %get-tuple-element.176), channel_id=1, source_target_pairs={{0,16},{2,18},{4,20},{6,22},{8,24},{10,26},{12,28},{14,30},{16,0},... | collective-permute-start | bytes 718856 | tf_op jit(solution)/shard_map/ppermute | solution.py:586
  166.9 18.0 %collective-permute-start.25 = (bf16[72,1280]{1,0:T(8,128)(2,1)S(1)}, bf16[72,1280]{1,0:T(8,128)(2,1)S(1)}, u32[]{:S(2)}, u32[]{:S(2)}) collective-permute-start(bf16[72,1280]{1,0:T(8,128)(2,1)S(1)} %get-tuple-element.190), channel_id=1, source_target_pairs={{0,8},{2,10},{4,12},{6,14},{8,0},{10,2},{12,4},{14,6},{16,24},{18,... | collective-permute-start | bytes 552968 | tf_op jit(solution)/shard_map/ppermute | solution.py:586
  169.4 15.5 %collective-permute-start.26 = (bf16[72,1280]{1,0:T(8,128)(2,1)S(1)}, bf16[72,1280]{1,0:T(8,128)(2,1)S(1)}, u32[]{:S(2)}, u32[]{:S(2)}) collective-permute-start(bf16[72,1280]{1,0:T(8,128)(2,1)S(1)} %get-tuple-element.191), channel_id=1, source_target_pairs={{0,4},{2,6},{4,0},{6,2},{8,12},{10,14},{12,8},{14,10},{16,20},{18,... | collective-permute-start | bytes 552968 | tf_op jit(solution)/shard_map/ppermute | solution.py:586
  173.0 16.1 %collective-permute-start.27 = (bf16[72,1280]{1,0:T(8,128)(2,1)S(1)}, bf16[72,1280]{1,0:T(8,128)(2,1)S(1)}, u32[]{:S(2)}, u32[]{:S(2)}) collective-permute-start(bf16[72,1280]{1,0:T(8,128)(2,1)S(1)} %get-tuple-element.192), channel_id=1, source_target_pairs={{0,12},{2,14},{4,8},{6,10},{8,4},{10,6},{12,0},{14,2},{16,28},{18,... | collective-permute-start | bytes 552968 | tf_op jit(solution)/shard_map/ppermute | solution.py:586
  173.1 17.3 %collective-permute-start.22 = (bf16[72,1152]{1,0:T(8,128)(2,1)S(1)}, bf16[72,1152]{1,0:T(8,128)(2,1)S(1)}, u32[]{:S(2)}, u32[]{:S(2)}) collective-permute-start(bf16[72,1152]{1,0:T(8,128)(2,1)S(1)} %get-tuple-element.181), channel_id=1, source_target_pairs={{0,16},{2,18},{4,20},{6,22},{8,24},{10,26},{12,28},{14,30},{16,0},... | collective-permute-start | bytes 497672 | tf_op jit(solution)/shard_map/ppermute | solution.py:586
  (43 other events, 432.2 us)

commit v4 on v3

v4 whole, which is shorter than its diff:
```python
import functools
import types

import jax
import jax.numpy as jnp
from jax import lax
from jax.experimental import pallas as pl
from jax.experimental.pallas import tpu as pltpu
from jax.sharding import PartitionSpec as P

HD = 72
DP, CORE = "dp", "tensor"
masked_score = -1000000000.0
norm_eps = 1e-06
gelu_scale = 0.7978845608028654
gelu_cubic = 0.044715
f32 = jnp.float32
bf16 = jnp.bfloat16
MIB = 1024 * 1024
NOWHERE = -1e6


def dot(left, right):
    return lax.dot_general(left, right, (((1,), (0,)), ((), ())), preferred_element_type=f32)


def dot_cols(left, right):
    return lax.dot_general(left, right, (((1,), (1,)), ((), ())), preferred_element_type=f32)


def dot_rows(left, right):
    return lax.dot_general(left, right, (((0,), (0,)), ((), ())), preferred_element_type=f32)


def iota(shape, dim):
    return lax.broadcasted_iota(jnp.int32, shape, dim).astype(f32)


def row_sum(values):
    return jnp.sum(values, axis=0, keepdims=True)


def lane_sum(values):
    return jnp.sum(values, axis=1, keepdims=True)


def lane_mean(values):
    return jnp.mean(values, axis=1, keepdims=True)


def lane_pad(size):
    return -(-size // 128) * 128


def put(ref, value):
    ref[...] = value.astype(ref.dtype)


def my_span(lengths, owners, me):
    base = lane_sum(jnp.where(owners < me, lengths, 0.0))
    used = lane_sum(jnp.where(owners == me, lengths, 0.0))
    return base, used


def token_slots(lengths, owners, me, n_dev, tokens, half_rows):
    device = iota((n_dev, lengths.shape[1]), 0)
    base = lane_sum(jnp.where(owners < device, lengths, 0.0))
    pos = iota((1, tokens), 1) * n_dev + me
    below = base <= pos
    target = row_sum(jnp.where(below, 1.0, 0.0)) - 1.0
    start = jnp.max(jnp.where(below, base, -1.0), axis=0, keepdims=True)
    slot = jnp.floor((pos - start) * (1.0 / n_dev))
    half = jnp.floor(slot * (1.0 / half_rows))
    return half, target * half_rows + slot - half * half_rows


def block_slots(base, n_dev, cap, half_rows):
    p = iota((cap, 1), 0)
    pos = base + p
    source = pos - n_dev * jnp.floor(pos * (1.0 / n_dev))
    slot = jnp.floor(p * (1.0 / n_dev))
    half = jnp.floor(slot * (1.0 / half_rows))
    return half, source * half_rows + slot - half * half_rows


def one_hot(index, shape, dim):
    return jnp.where(index == iota(shape, dim), 1.0, 0.0).astype(bf16)


def place():
    return lax.axis_index(DP).astype(f32), lax.axis_index(CORE).astype(f32)


def norm_parts(values):
    centered = values - lane_mean(values)
    scale = lax.rsqrt(lane_mean(centered * centered) + norm_eps)
    return centered * scale, scale


def norm_back(normed, scale, grad, gain):
    inner = grad * gain
    return scale * (inner - lane_mean(inner) - normed * lane_mean(inner * normed))


def gelu_both(values):
    square = values * values
    bent = jnp.tanh(gelu_scale * values * (1.0 + gelu_cubic * square))
    half = 0.5 * (1.0 + bent)
    slope = half + 0.5 * values * (1.0 - bent * bent) * (
        gelu_scale * (1.0 + 3.0 * gelu_cubic * square)
    )
    return values * half, slope


def flip_of(block, order):
    flip = 0 * block
    for step, bit in enumerate(order):
        flip = flip | (((block >> (len(order) - 1 - step)) & 1) << bit)
    return flip


def ordered_rows(out_ref, from_ref, n_dev, order):
    width = from_ref.shape[0]
    owner_rows = width // n_dev
    me = lax.axis_index(DP)
    if owner_rows % 8:
        i = iota((width, 1), 0)
        block = jnp.floor((i + 0.5) * (1.0 / owner_rows))
        owner = (flip_of(block.astype(jnp.int32), order) ^ me).astype(f32)
        pick = one_hot(owner * owner_rows + (i - block * owner_rows), (width, width), 1)
        out_ref[...] = dot(pick, from_ref[...].astype(bf16))
        return
    for block in range(n_dev):
        start = pl.multiple_of((me ^ flip_of(block, order)) * owner_rows, 8)
        rows = slice(block * owner_rows, (block + 1) * owner_rows)
        out_ref[rows, :] = from_ref[pl.ds(start, owner_rows), :]


def parts_between(bounds, group, size, count):
    for i in range(count):
        first, last = max(i * size, bounds[group]), min((i + 1) * size, bounds[group + 1])
        if first < last:
            yield (
                i,
                slice(first - i * size, last - i * size),
                slice(first - bounds[group], last - bounds[group]),
            )


def pieces_of(start, size, columns):
    done = 0
    while done < size:
        row, lane = (start + done) // columns, (start + done) % columns
        now = min(columns - lane, size - done)
        yield slice(done, done + now), slice(row, row + 1), slice(lane, lane + now)
        done += now


def call(body, ins, outs, scratch=(), vmem=16, far=False):
    ins_flat, ins_tree = jax.tree.flatten(ins)
    is_out = lambda x: isinstance(x, tuple)
    outs_flat, outs_tree = jax.tree.flatten(outs, is_leaf=is_out)
    n_in, n_out = len(ins_flat), len(outs_flat)

    def kernel(*refs):
        given, rest = refs[:n_in], refs[n_in + n_out :]
        if far:
            near, sems, rest = rest[:n_in], rest[n_in], rest[n_in + 1 :]
            copies = [
                pltpu.make_async_copy(ref, to, sems.at[i]) for i, (ref, to) in enumerate(zip(given, near))
            ]
            for copy in copies:
                copy.start()

            def arrival(copy, to):
                def wait():
                    copy.wait()
                    return to[...]

                return wait

            given = [arrival(copy, to) for copy, to in zip(copies, near)]
        given = types.SimpleNamespace(**jax.tree.unflatten(ins_tree, given))
        made = types.SimpleNamespace(**jax.tree.unflatten(outs_tree, refs[n_in : n_in + n_out]))
        body(given, made, *rest)

    copies = [pltpu.VMEM(x.shape, x.dtype) for x in ins_flat]
    copies += [pltpu.SemaphoreType.DMA((n_in,))]
    results = pl.pallas_call(
        kernel,
        name=getattr(body, "func", body).__name__,
        out_shape=[jax.ShapeDtypeStruct(shape, dtype) for shape, dtype in outs_flat],
        in_specs=[pl.BlockSpec(memory_space=pltpu.HBM if far else pltpu.VMEM)] * n_in,
        out_specs=[pl.BlockSpec(memory_space=pltpu.VMEM)] * n_out,
        scratch_shapes=(copies if far else []) + list(scratch),
        compiler_params=pltpu.CompilerParams(vmem_limit_bytes=vmem * MIB),
    )(*ins_flat)
    return types.SimpleNamespace(**jax.tree.unflatten(outs_tree, results))


def pack(n_dev, half_rows, tokens, given, made):
    me, core = place()
    lengths, owners = given.lengths().astype(f32), given.owners().astype(f32)
    half, index = token_slots(lengths, owners, me, n_dev, tokens, half_rows)
    target = jnp.floor(index * (1.0 / half_rows))
    index = jnp.where(half == core, index + target * half_rows, NOWHERE)
    shape = (2 * n_dev * half_rows, tokens)
    x_pick, g_pick = one_hot(index, shape, 0), one_hot(index + half_rows, shape, 0)
    rows = dot(x_pick, given.x())
    put(made.send, rows + dot(g_pick, given.g()))


def block_rows(given, n_dev, cap, half_rows, kind):
    me, core = place()
    base, _ = my_span(given.lengths[...].astype(f32), given.owners[...].astype(f32), me)
    half, index = block_slots(base, n_dev, cap, half_rows)
    source = jnp.floor(index * (1.0 / half_rows))
    index = index + (source + kind) * half_rows
    index = jnp.where(half == core, index, index + 2 * n_dev * half_rows)
    pick = one_hot(index, (cap, 2 * cap), 1)
    return dot(pick, jnp.concatenate([given.mine[...], given.other[...]], axis=0))


def unpack(n_dev, half_rows, given, made):
    put(made.g, block_rows(given, n_dev, made.g.shape[0], half_rows, 1))


def image_mask(lengths, owners, cap):
    me, _ = place()
    base, used = my_span(lengths, owners, me)
    n_img = lengths.shape[1]
    starts = lane_sum(jnp.where(iota((n_img, n_img), 1) < iota((n_img, n_img), 0), lengths, 0.0))
    p = iota((1, cap), 1)
    count = row_sum(jnp.where(starts <= base + p, 1.0, 0.0))
    seg_row = jnp.where(p < used, count, 0.0)
    on_diagonal = iota((cap, cap), 0) == iota((cap, cap), 1)
    seg_col = lane_sum(jnp.where(on_diagonal, seg_row, 0.0))
    return jnp.where(seg_col == seg_row, 1.0, 0.0)


class Vectors:
    def __init__(self, **sizes):
        self.names, self.size = list(sizes), 0
        for name, size in sizes.items():
            setattr(self, name, slice(self.size, self.size + size))
            self.size += lane_pad(size)


def attend(n_dev, half_rows, vec, given, made):
    cap = made.x.shape[0]
    same = image_mask(given.lengths[...].astype(f32), given.owners[...].astype(f32), cap)
    put(made.mask, same)
    x = block_rows(given, n_dev, cap, half_rows, 0)
    put(made.x, x)
    row = given.vec
    normed, _ = norm_parts(x)
    h1 = (normed * row[:, vec.gain1] + row[:, vec.shift1]).astype(bf16)
    put(made.h1, h1)
    put(made.q, dot_cols(h1, given.wq[...]) + row[:, vec.bq])
    put(made.k, dot_cols(h1, given.wk[...]))
    put(made.v, dot_cols(h1, given.wv[...]) + row[:, vec.bv])
    for h in range(made.q.shape[1] // HD):
        cols = slice(h * HD, (h + 1) * HD)
        s = dot_cols(made.q[:, cols], made.k[:, cols]) * HD ** (-0.5)
        s = jnp.where(same > 0.5, s, masked_score)
        top = jnp.max(s, axis=1, keepdims=True)
        e = jnp.exp(s - top)
        total = lane_sum(e)
        made.log[:, h : h + 1] = top + jnp.log(total)
        made.att[:, cols] = dot((e / total).astype(bf16), made.v[:, cols]).astype(bf16)
    put(made.branch, dot(made.att[...], given.wo[...]))


def both(mine, other, rows=slice(None)):
    return mine[rows, :].astype(f32) + other[rows, :].astype(f32)


def both_halves(mine, other, rows=slice(None)):
    return jnp.concatenate([both(a, b, rows) for a, b in zip(mine, other)], axis=0)


def chunks_of(width, step):
    full = width // step
    return full, full * step, width - full * step


def mlp(vec, given, made, out_total, dh2_total):
    cap = made.middle.shape[0]
    half = cap // 2
    row = given.vec
    branch = both(given.branch, given.branch_other) + row[:, vec.bo]
    middle = given.x[...].astype(f32) + branch
    put(made.middle, middle)
    normed, _ = norm_parts(middle)
    put(made.h2, normed * row[:, vec.gain2] + row[:, vec.shift2])
    start = pl.multiple_of(lax.axis_index(CORE) * half, half)
    made.halves[:half, :] = made.h2[pl.ds(start, half), :]
    made.halves[half:, :] = given.g[pl.ds(start, half), :]
    step = 512
    full, done, rest = chunks_of(given.we.shape[0], step)
    out_total[...] = jnp.zeros_like(out_total)
    dh2_total[...] = jnp.zeros_like(dh2_total)
    made.be_grad[...] = jnp.zeros_like(made.be_grad)
    first = vec.be.start

    def chunk(rows, bias):
        we, wr = given.we[rows, :], given.wr[rows, :]
        hidden, slope = gelu_both(dot_cols(made.h2[...], we) + row[:, bias])
        dexp = (dot_cols(given.g[...], wr) * slope).astype(bf16)
        made.be_grad[:, rows] = row_sum(dexp.astype(f32))
        out_total[...] += dot(hidden.astype(bf16), wr)
        dh2_total[...] += dot(dexp, we)

    @pl.loop(0, full)
    def _(i):
        at = pl.multiple_of(i * step, step)
        chunk(pl.ds(at, step), pl.ds(pl.multiple_of(first + at, 128), step))

    if rest:
        chunk(slice(done, done + rest), slice(first + done, first + done + rest))
    for i, ref in enumerate(made.sums):
        rows = slice(i * half, (i + 1) * half)
        ref[:half, :] = dh2_total[rows, :].astype(bf16)
        ref[half:, :] = out_total[rows, :].astype(bf16)


def middle_back(vec, given, made):
    width = given.middle.shape[1]
    half = given.sums[0].shape[0] // 2
    g = given.g[...].astype(f32)
    normed, scale = norm_parts(given.middle[...])
    dh2 = both_halves(given.sums, given.sums_other, slice(0, half))
    dmid = g + norm_back(normed, scale, dh2, given.vec[:, vec.gain2])
    put(made.dmid, dmid)
    branch = dmid.astype(bf16)
    put(made.branch_grad, branch)
    put(made.datt, dot_cols(branch, given.wo[...]))
    for i, values in enumerate([branch.astype(f32), dh2 * normed, dh2, g]):
        made.vec_grad[:, i * width : (i + 1) * width] = row_sum(values)


def attend_back(given, made):
    heads_width = made.dq.shape[1]
    same = given.mask[...] > 0.5
    for h in range(heads_width // HD):
        cols = slice(h * HD, (h + 1) * HD)
        q, k, v = given.q[:, cols], given.k[:, cols], given.v[:, cols]
        datt = given.datt[:, cols]
        s = jnp.where(same, dot_cols(q, k) * HD ** (-0.5), masked_score)
        prob = jnp.exp(s - given.log[:, h : h + 1])
        dprob = dot_cols(datt, v)
        ds = (prob * (dprob - lane_sum(prob * dprob))).astype(bf16)
        made.dq[:, cols] = (dot(ds, k) * HD ** (-0.5)).astype(bf16)
        made.dk[:, cols] = (dot_rows(ds, q) * HD ** (-0.5)).astype(bf16)
        made.dv[:, cols] = dot_rows(prob.astype(bf16), datt).astype(bf16)
    dh1 = dot(made.dq[...], given.wq[...])
    dh1 += dot(made.dk[...], given.wk[...])
    dh1 += dot(made.dv[...], given.wv[...])
    half = dh1.shape[0] // 2
    for i, ref in enumerate(made.dh1):
        put(ref, dh1[i * half : (i + 1) * half, :])
    row = made.vec_grad
    row[...] = jnp.zeros_like(row)
    row[:, :heads_width] = row_sum(made.dq[...].astype(f32))
    second = lane_pad(heads_width)
    row[:, second : second + heads_width] = row_sum(made.dv[...].astype(f32))


def put_vectors(give_ref, first, rows, values):
    high = values.astype(bf16)
    low = (values - high.astype(f32)).astype(bf16)
    give_ref[first : first + rows, :] = high
    give_ref[first + rows : first + 2 * rows, :] = low
    return high.astype(f32) + low.astype(f32)


def got_vectors(got_ref, rows):
    first = got_ref.shape[0] - 2 * rows
    high = got_ref[first : first + rows, :].astype(f32)
    return high + got_ref[first + rows :, :].astype(f32)


def attend_weights(n_dev, orders, bounds, given, made, h1_t, branch_t, left, branch_left):
    heads_width = given.right[0].shape[1]
    half = given.h1.shape[1] // 2
    h1_t[...] = jnp.transpose(given.h1[...].astype(f32))
    branch_t[...] = jnp.transpose(given.branch_grad[...].astype(f32))
    made.vec[...] = jnp.zeros_like(made.vec)
    at = 0
    for ref in given.vec_grads:
        for here, row, lanes in pieces_of(at, ref.shape[1], made.vec.shape[1]):
            made.vec[row, lanes] = ref[:, here]
        at += ref.shape[1]
    put(made.vec, put_vectors(made.give[0], half, made.vec.shape[0], made.vec[...]))
    for group, order in enumerate(orders):
        width = bounds[group + 1] - bounds[group]
        ordered_rows(left, h1_t, n_dev, order)
        for i, cols, lanes in parts_between(bounds, group, heads_width, 4):
            if i == 3:
                ordered_rows(branch_left, branch_t, n_dev, order)
            rows = (branch_left if i == 3 else left)[...].astype(bf16)
            product = dot(rows, given.right[i][:, cols]).astype(bf16)
            made.keep[group][:, lanes] = product[:half, :]
            made.give[group][:half, lanes] = product[half:, :]


def first_back(vec, given, made):
    width = given.x.shape[1]
    normed, scale = norm_parts(given.x[...].astype(f32))
    dh1 = both_halves(given.dh1, given.dh1_other)
    made.vec_grad[:, :width] = row_sum(dh1 * normed)
    made.vec_grad[:, width:] = row_sum(dh1)
    gain = given.vec[:, vec.gain1]
    put(made.dx, given.dmid[...] + norm_back(normed, scale, dh1, gain))


def back(n_dev, half_rows, vec, given, made):
    cap = given.dx.shape[0]
    half = given.sums[0].shape[0] // 2
    me, core = place()
    base, _ = my_span(given.lengths[...].astype(f32), given.owners[...].astype(f32), me)
    which, index = block_slots(base, n_dev, cap, half_rows)
    source = jnp.floor(index * (1.0 / half_rows))
    index = jnp.where(which == core, index + source * half_rows, NOWHERE)
    part = both_halves(given.sums, given.sums_other, slice(half, 2 * half))
    out = given.middle[...] + (part + given.vec[:, vec.br])
    rows = dot_rows(one_hot(index, (cap, cap), 1), out.astype(bf16))
    rows += dot_rows(one_hot(index + half_rows, (cap, cap), 1), given.dx[...])
    put(made.back, rows)


def home(n_dev, half_rows, given, made):
    me, core = place()
    tokens = made.mixed.shape[0]
    lengths, owners = given.lengths[...].astype(f32), given.owners[...].astype(f32)
    half, index = token_slots(lengths, owners, me, n_dev, tokens, half_rows)
    index = index + jnp.floor(index * (1.0 / half_rows)) * half_rows
    index = jnp.where(half == core, index, index + 2 * n_dev * half_rows)
    rows = jnp.concatenate([given.mine[...], given.other[...]], axis=0)
    shape = (rows.shape[0], tokens)
    put(made.mixed, dot_rows(one_hot(index, shape, 0), rows))
    put(made.grad, dot_rows(one_hot(index + half_rows, shape, 0), rows))


def share_of(far_bits):
    me = lax.axis_index(DP)
    return 2 * ((me >> far_bits[0]) & 1) + ((me >> far_bits[1]) & 1)


def mlp_weights(
    far_bits, orders, bounds, n_dev, vec, given, made, h2_all, g_all, hidden_all, dexp_all, we_part,
    wr_part, natural, ordered,
):
    cap, width = given.h2.shape
    half_cap = cap // 2
    share = share_of(far_bits)
    part, hidden_width = we_part.shape[0], given.we.shape[0]
    last = hidden_width - 3 * part
    be = vec.be.start
    bias = jnp.zeros((1, part), f32)
    for i in range(4):
        end = min((i + 1) * part, hidden_width)
        piece = given.vec[:, be + i * part : be + end]
        if end < (i + 1) * part:
            piece = jnp.concatenate([piece, jnp.zeros((1, (i + 1) * part - end), f32)], axis=1)
        bias += jnp.where(share == i, piece, 0.0)
    for source, near in ((given.we, we_part), (given.wr, wr_part)):

        @pl.when(share < 3)
        def _():
            near[...] = source[pl.ds(pl.multiple_of(share * part, 16), part), :]

        @pl.when(share == 3)
        def _():
            near[:last, :] = source[3 * part :, :]
            near[last:, :] = jnp.zeros((part - last, width), bf16)

    for k in range(4):
        rows = slice(k * cap, (k + 1) * cap)
        if k == 0:
            h2_all[rows, :] = given.h2[...]
            g_all[rows, :] = given.g[...]
        else:
            for i, ref in enumerate((given.far[k - 1], given.far_other[k - 1])):
                at = slice(k * cap + i * half_cap, k * cap + (i + 1) * half_cap)
                h2_all[at, :] = ref[:half_cap, :]
                g_all[at, :] = ref[half_cap:, :]
        hidden, slope = gelu_both(dot_cols(h2_all[rows, :], we_part[...]) + bias)
        hidden_all[rows, :] = hidden.astype(bf16)
        dexp_all[rows, :] = (dot_cols(g_all[rows, :], wr_part[...]) * slope).astype(bf16)
    half = width // 2
    natural[:, :part] = dot_rows(g_all[...], hidden_all[...])
    natural[:, part : 2 * part] = dot_rows(h2_all[...], dexp_all[...])
    if 2 * part < bounds[-1]:
        natural[:, 2 * part :] = jnp.zeros((width, bounds[-1] - 2 * part), f32)
    for group, order in enumerate(orders):
        lanes = pl.ds(bounds[group], bounds[group + 1] - bounds[group])
        here = ordered.at[:, pl.ds(0, bounds[group + 1] - bounds[group])]
        ordered_rows(here, natural.at[:, lanes], n_dev, order)
        put(made.give[group], here[half:, :])
        put(made.keep[group], here[:half, :])


def turn(vec_rows, given, made):
    rows = given.keep.shape[0]
    total = given.keep[...].astype(f32) + given.got[:rows, :].astype(f32)
    put(made.keep, total[: rows // 2, :])
    made.give[: rows // 2, :] = total[rows // 2 :, :].astype(bf16)
    if vec_rows:
        vec = given.vec[...] + got_vectors(given.got, vec_rows)
        put(made.vec, put_vectors(made.give, rows // 2, vec_rows, vec))


def last_sums(bounds, vec_rows, given, made):
    put(made.vec, given.vec[...] + got_vectors(given.got[0], vec_rows))
    for group, (keep, got) in enumerate(zip(given.keep, given.got)):
        value = keep[...].astype(f32) + got[: keep.shape[0], :].astype(f32)
        for i, cols, lanes in parts_between(bounds, group, made.weights[0].shape[1], 4):
            made.weights[i][:, cols] = value[:, lanes]


def mlp_cut(bounds, given, made):
    rows = given.keep[0].shape[0] // 4
    for group, (keep, got) in enumerate(zip(given.keep, given.got)):
        total = keep[...].astype(f32) + got[...].astype(f32)
        for k, ref in enumerate(made.cuts):
            ref[:, bounds[group] : bounds[group + 1]] = total[k * rows : (k + 1) * rows, :].astype(bf16)


def mlp_last(far_bits, part, given, made):
    share = share_of(far_bits)
    hidden_width = made.weights[0].shape[1]
    pieces = [ref[...].astype(f32) for ref in given.cuts]
    for i in range(4):
        own = jnp.zeros_like(pieces[0])
        for k, piece in enumerate(pieces):
            own += jnp.where((share ^ k) == i, piece, 0.0)
        end = min((i + 1) * part, hidden_width)
        for at, ref in enumerate(made.weights):
            ref[:, i * part : end] = own[:, at * part : at * part + end - i * part]


def swap_cores(values):
    return lax.ppermute(values, CORE, [(0, 1), (1, 0)])


def swap_dp(values, flip):
    return lax.ppermute(values, DP, [(i, i ^ flip) for i in range(lax.axis_size(DP))])


def spread(rows):
    return lax.all_to_all(rows, DP, split_axis=0, concat_axis=0, tiled=True)


def after(values, earlier):
    return lax.optimization_barrier((values, earlier))[0]


def next_step(pair, vec):
    keep, got = pair
    rows = keep.shape[0] // 2
    vec_rows = 0 if vec is None else vec.shape[0]
    if rows % 8:
        total = keep.astype(f32) + got[: 2 * rows].astype(f32)
        kept, give = total[:rows], total[rows:].astype(bf16)
        if vec is not None:
            got = got[2 * rows :].astype(f32)
            vec = vec + (got[:vec_rows] + got[vec_rows:])
            high = vec.astype(bf16)
            low = (vec - high.astype(f32)).astype(bf16)
            vec = high.astype(f32) + low.astype(f32)
            give = jnp.concatenate([give, high, low])
        return kept, give, vec
    columns = keep.shape[1]
    ins, outs = dict(keep=keep, got=got), dict(keep=((rows, columns), f32))
    outs.update(give=((rows + 2 * vec_rows, columns), bf16))
    if vec is not None:
        ins.update(vec=vec)
        outs.update(vec=(vec.shape, f32))
    made = call(functools.partial(turn, vec_rows), ins, outs)
    return made.keep, made.give, None if vec is None else made.vec


class Chains:
    def __init__(self, keep, give, orders, vec=None):
        self.orders, self.vec = orders, vec
        self.done = [1] * len(orders)
        self.pairs = [(k, swap_dp(g, 1 << order[0])) for k, g, order in zip(keep, give, orders)]

    def step(self, group, earlier):
        step = self.done[group]
        self.done[group] += 1
        pair = after(self.pairs[group], earlier)
        keep, give, vec = next_step(pair, None if group else self.vec)
        if not group:
            self.vec = vec
        self.pairs[group] = (keep, swap_dp(give, 1 << self.orders[group][step]))
        return keep

    def finish(self, earlier):
        for group, order in enumerate(self.orders):
            while self.done[group] < len(order):
                earlier = self.step(group, earlier)

    def kept(self):
        return [pair[0] for pair in self.pairs]

    def received(self):
        return [pair[1] for pair in self.pairs]


def on_device(
    patches, cotangent, image_lengths, image_owner, first_gain, first_shift, query_weight,
    query_bias, key_weight, value_weight, value_bias, output_weight, output_bias, second_gain,
    second_shift, expand_weight, expand_bias, reduce_weight, reduce_bias,
):
    n_dev = lax.axis_size(DP)
    tokens, width = patches.shape
    cap = 2 * tokens
    half_rows = cap // n_dev // 2
    heads_width, hidden_width = query_weight.shape[1], expand_weight.shape[1]
    heads = heads_width // HD
    n_bits = n_dev.bit_length() - 1
    far_bits = (1, n_bits - 2)
    flips = [flip_of(k, far_bits) for k in range(4)]
    rest = [bit for bit in range(n_bits) if bit not in far_bits]
    mlp_orders = (rest, rest[::-1])
    others = list(range(2, n_bits - 2))
    attend_orders = (
        [0, 1] + others + [n_bits - 2, n_bits - 1],
        [1, 0] + others + [n_bits - 2, n_bits - 1],
    )
    attend_bounds = (0, 1152, 4 * heads_width)
    wq, wk, wv, wo, we, wr = (
        w.T for w in (query_weight, key_weight, value_weight, output_weight, expand_weight, reduce_weight)
    )
    vec = Vectors(
        gain1=width, shift1=width, bo=width, gain2=width, shift2=width, br=width, be=hidden_width,
        bq=heads_width, bv=heads_width,
    )
    vectors = [
        first_gain, first_shift, output_bias, second_gain, second_shift, reduce_bias, expand_bias,
        query_bias, value_bias,
    ]
    vectors = jnp.concatenate(
        [jnp.pad(v, (0, lane_pad(v.shape[0]) - v.shape[0])) for v in vectors]
    ).reshape(1, -1)
    sizes = dict(lengths=image_lengths.reshape(1, -1), owners=image_owner.reshape(1, -1))
    wide32, wide16 = ((cap, width), f32), ((cap, width), bf16)
    half16 = ((cap // 2, width), bf16)
    head16 = ((cap, heads_width), bf16)
    at_place = lambda body, *more: functools.partial(body, n_dev, half_rows, *more)
    scratch = pltpu.VMEM

    sent = call(
        at_place(pack, tokens), dict(**sizes, x=patches, g=cotangent), dict(send=wide16), far=True, vmem=62
    )
    got = spread(sent.send)
    arrived = dict(**sizes, mine=got, other=swap_cores(got))
    fwd = call(
        at_place(attend, vec),
        dict(**arrived, vec=vectors, wq=wq, wk=wk, wv=wv, wo=wo),
        dict(
            mask=((cap, cap), f32), x=wide16, h1=wide16, q=head16, k=head16, v=head16,
            log=((cap, heads), f32), att=head16, branch=wide16,
        ),
    )
    branch_other = swap_cores(fwd.branch)
    g = call(at_place(unpack), arrived, dict(g=wide16)).g
    mid = call(
        functools.partial(mlp, vec),
        dict(x=fwd.x, branch=fwd.branch, branch_other=branch_other, g=g, vec=vectors, we=we, wr=wr),
        dict(
            middle=wide32, h2=wide16, halves=wide16, sums=[wide16, wide16],
            be_grad=((1, lane_pad(hidden_width)), f32),
        ),
        scratch=[scratch((cap, width), f32)] * 2,
    )
    halves = [swap_dp(mid.halves, flip) for flip in flips[1:]]
    sums = dict(sums=mid.sums, sums_other=[swap_cores(rows) for rows in mid.sums])
    half_back = call(
        functools.partial(middle_back, vec),
        dict(g=g, middle=mid.middle, vec=vectors, wo=wo, **sums),
        dict(dmid=wide32, branch_grad=wide16, datt=head16, vec_grad=((1, 4 * width), f32)),
    )
    att_back = call(
        attend_back,
        dict(
            mask=fwd.mask, q=fwd.q, k=fwd.k, v=fwd.v, datt=half_back.datt, log=fwd.log,
            wq=wq, wk=wk, wv=wv,
        ),
        dict(
            dq=head16, dk=head16, dv=head16, dh1=[half16, half16],
            vec_grad=((1, 2 * lane_pad(heads_width)), f32),
        ),
    )
    first = call(
        functools.partial(first_back, vec),
        dict(
            x=fwd.x, dh1=att_back.dh1, dh1_other=[swap_cores(rows) for rows in att_back.dh1],
            vec=vectors, dmid=half_back.dmid,
        ),
        dict(dx=wide16, vec_grad=((1, 2 * width), f32)),
    )

    columns = attend_bounds[1]
    vec_rows = -(-vec.size // (16 * columns)) * 16
    keeps, gives = [], []
    for i in range(len(attend_orders)):
        span = attend_bounds[i + 1] - attend_bounds[i]
        keeps.append(((width // 2, span), bf16))
        gives.append(((width // 2 + (0 if i else 2 * vec_rows), span), bf16))
    products = call(
        functools.partial(attend_weights, n_dev, attend_orders, attend_bounds),
        dict(
            h1=fwd.h1, branch_grad=half_back.branch_grad,
            right=[att_back.dq, att_back.dk, att_back.dv, fwd.att],
            vec_grads=[first.vec_grad, half_back.vec_grad, mid.be_grad, att_back.vec_grad],
        ),
        dict(vec=((vec_rows, columns), f32), keep=keeps, give=gives),
        scratch=[scratch((width, cap), f32)] * 4,
    )
    a = Chains(products.keep, products.give, attend_orders, products.vec)
    dx = after(first.dx, products.keep[0])
    packed = call(
        at_place(back, vec), dict(**sizes, vec=vectors, middle=mid.middle, dx=dx, **sums), dict(back=wide16)
    ).back
    came = spread(packed)
    far = after(halves, packed)
    far_other = [swap_cores(rows) for rows in far[:2]]
    far[2] = after(far[2], far_other[0])
    far_other.append(swap_cores(far[2]))
    part = -(-hidden_width // 64) * 16
    mlp_bounds = (0, 768, lane_pad(2 * part))
    spans = [after_ - before for before, after_ in zip(mlp_bounds, mlp_bounds[1:])]
    mlp_half = [((width // 2, span), bf16) for span in spans]
    grads = call(
        functools.partial(
            mlp_weights, far_bits, [list(o) + list(far_bits) for o in mlp_orders], mlp_bounds, n_dev, vec
        ),
        dict(vec=vectors, we=we, wr=wr, h2=mid.h2, g=g, far=far, far_other=far_other),
        dict(give=mlp_half, keep=mlp_half),
        scratch=[scratch((4 * cap, width), bf16)] * 2 + [scratch((4 * cap, part), bf16)] * 2
        + [scratch((part, width), bf16)] * 2
        + [scratch((width, mlp_bounds[-1]), f32), scratch((width, max(spans)), f32)],
        vmem=36,
    )
    m = Chains(grads.keep, grads.give, mlp_orders)
    last = grads.keep[0]
    last = a.step(0, last)
    last = a.step(1, last)
    last = m.step(0, last)
    last = a.step(0, last)
    last = a.step(1, last)
    last = m.step(1, last)
    last = a.step(0, last)
    last = a.step(1, last)
    m.finish(last)
    a.finish(last)
    own_rows = width // n_dev
    cut = ((own_rows, mlp_bounds[-1]), bf16)
    cuts = call(
        functools.partial(mlp_cut, mlp_bounds), dict(keep=m.kept(), got=m.received()), dict(cuts=[cut] * 4)
    ).cuts
    cuts = [cuts[0]] + [swap_dp(rows, flip) for rows, flip in zip(cuts[1:], flips[1:])]
    final = call(
        at_place(home), dict(**sizes, mine=came, other=swap_cores(came)),
        dict(mixed=((tokens, width), bf16), grad=((tokens, width), bf16)),
    )
    mlp_own = call(
        functools.partial(mlp_last, far_bits, part), dict(cuts=cuts),
        dict(weights=[((own_rows, hidden_width), f32)] * 2),
    ).weights
    own = call(
        functools.partial(last_sums, attend_bounds, vec_rows),
        dict(vec=a.vec, keep=a.kept(), got=a.received()),
        dict(vec=((vec_rows, columns), f32), weights=[((own_rows, heads_width), f32)] * 4),
    )
    flat = own.vec.reshape(-1)
    total = types.SimpleNamespace(**{name: flat[getattr(vec, name)] for name in vec.names})
    wq_sum, wk_sum, wv_sum, wo_sum = own.weights
    wr_sum, we_sum = mlp_own
    return (
        final.mixed, final.grad, total.gain1, total.shift1, wq_sum, total.bq, wk_sum, wv_sum, total.bv,
        wo_sum, total.bo, total.gain2, total.shift2, we_sum, total.be, wr_sum, total.br,
    )


def solution(mesh):
    rows, all_same = P(DP, None), P()
    cols, vector = P(None, CORE), P(CORE)
    tiles = P(DP, CORE)
    in_specs = (
        rows, rows, all_same, all_same, all_same, all_same, cols, vector, cols, cols, vector, cols,
        all_same, all_same, all_same, cols, vector, cols, all_same,
    )
    out_specs = (
        rows, rows, all_same, all_same, tiles, vector, tiles, tiles, vector, tiles, all_same, all_same,
        all_same, tiles, vector, tiles, all_same,
    )
    return jax.shard_map(
        on_device, mesh=mesh, in_specs=in_specs, out_specs=out_specs, check_vma=False
    )
```

time: 194 us -> 192 us (0.990)
  starting transfers between devices: 35.8 us -> 32.3 us
  local copies, waits for them, and re-layouts: 21.6 us -> 19.4 us
    ppermute x28, starting transfers between devices: 23.5 us -> 20 us  [the longest x18 18.3 us: swap_dp(): lax.ppermute(values, DP, [(i, i ^ flip) for i in range(lax.axis_size(DP))])]
    unnamed x82, local copies, waits for them, and re-layouts: 19.7 us -> 17.5 us
  transfers between devices with their start and end apart: 30 -> 30, of which waited for: 16 -> 14; matrix products, arithmetic and copies ran while one was open for 0% -> 0% of each run, Pallas kernels for 19% -> 20%
where the time goes in v4:
time: 192 us; the launch traced here: 191 us
  waiting for transfers between devices  81.9 us (43%)
  Pallas kernels  55.8 us (29%)
  starting transfers between devices  32.3 us (17%)
  local copies, waits for them, and re-layouts  19.4 us (10%)
    ppermute x18, waiting for transfers between devices, swap_dp(): lax.ppermute(values, DP, [(i, i ^ flip) for i in range(lax.axis_size(DP))])  61 us
    pallas_call x22, Pallas kernels, call(): pl.pallas_call(kernel, name=getattr(body, 'func', body).__name__, out_sha...  55.8 us
    ppermute x18, starting transfers between devices, swap_dp(): lax.ppermute(values, DP, [(i, i ^ flip) for i in range(lax.axis_size(DP))])  18.3 us
    unnamed x82, local copies, waits for them, and re-layouts  17.5 us
    all_to_all x2, waiting for transfers between devices, spread(): return lax.all_to_all(rows, DP, split_axis=0, concat_axis=0, tiled=True)  16.2 us
    all_to_all x2, starting transfers between devices, spread(): return lax.all_to_all(rows, DP, split_axis=0, concat_axis=0, tiled=True)  12.3 us
    ppermute x10, waiting for transfers between devices, swap_cores(): return lax.ppermute(values, CORE, [(0, 1), (1, 0)])  4.64 us
  transfers between devices with their start and end apart: 30, of which 14 were waited for; matrix products, arithmetic and copies ran while one was open for 0% of the time, Pallas kernels for 20%

profile of v4, /device:TPU:0, one launch (start us, length us, event | category | flops | bytes accessed | tf_op | source)
XLA Modules:
  0.0 190.6 jit_solution(16725370490944271981)
XLA Ops:
  0.8 2.5 %pack.1 = bf16[256,1152]{1,0:T(8,128)(2,1)} custom-call(bf16[128,1152]{1,0:T(8,128)(2,1)} %refs_0_.1, s32[1,64]{1,0:T(1,128)} %bitcast.31, s32[1,64]{1,0:T(1,128)} %bitcast.36, bf16[128,1152]{1,0:T(8,128)(2,1)} %refs_3_.1), custom_call_target="tpu_custom_call" | custom-call | tf_op jit(solution)/shard_map/pack/pallas_call | solution.py:189
  3.3 8.5 %all-to-all-start = ((bf16[16,16,1152]{2,1,0:T(8,128)(2,1)}), bf16[16,16,1152]{2,1,0:T(8,128)(2,1)S(1)}, u32[]{:S(2)}, u32[]{:S(2)}) async-start(bf16[16,16,1152]{2,1,0:T(8,128)(2,1)} %bitcast.41), calls=%async_computation | async-start | bytes 1179648 | tf_op jit(solution)/shard_map/all_to_all | solution.py:552
  11.9 16.2 %all-to-all-done = bf16[16,16,1152]{2,1,0:T(8,128)(2,1)S(1)} async-done(((bf16[16,16,1152]{2,1,0:T(8,128)(2,1)}), bf16[16,16,1152]{2,1,0:T(8,128)(2,1)S(1)}, u32[]{:S(2)}, u32[]{:S(2)}) %all-to-all-start) | async-done | bytes 589856 | tf_op jit(solution)/shard_map/all_to_all | solution.py:552
  34.0 5.1 %attend.1 = (bf16[256,576]{1,0:T(8,128)(2,1)S(1)}, bf16[256,1152]{1,0:T(8,128)(2,1)S(1)}, bf16[256,1152]{1,0:T(8,128)(2,1)S(1)}, bf16[256,576]{1,0:T(8,128)(2,1)...) custom-call(s32[1,64]{1,0:T(1,128)S(1)} %bitcast.32, ...), custom_call_target="tpu_custom_call" | custom-call | tf_op jit(solution)/shard_map/attend/pallas_call | solution.py:189
  41.3 2.4 %copy-done.1 = bf16[1152,2152]{0,1:T(8,128)(2,1)S(1)} copy-done((bf16[1152,2152]{0,1:T(8,128)(2,1)S(1)}, bf16[1152,2152]{0,1:T(8,128)(2,1)}, u32[]{:S(2)}) %copy-start.1) | copy-done | bytes 4958232
  43.7 8.6 %mlp.1 = (f32[1,2176]{1,0:T(1,128)S(1)}, bf16[256,1152]{1,0:T(8,128)(2,1)S(1)}, bf16[256,1152]{1,0:T(8,128)(2,1)S(1)}, f32[256,1152]{1,0:T(8,128)S(1)}, bf16[256...) custom-call(bf16[256,1152]{1,0:T(8,128)(2,1)S(1)} %get-tuple-element.106.refs_0_, ...), custom_call_target="tpu_custom_call" | custom-call | tf_op jit(solution)/shard_map/mlp/pallas_call | solution.py:189
  59.2 5.5 %attend_back.1 = (bf16[128,1152]{1,0:T(8,128)(2,1)S(1)}, bf16[128,1152]{1,0:T(8,128)(2,1)S(1)}, bf16[256,576]{1,0:T(8,128)(2,1)S(1)}, bf16[256,576]{1,0:T(8,128)...) custom-call(bf16[256,576]{1,0:T(8,128)(2,1)S(1)} %get-tuple-element.111.refs_0_, ...), custom_call_target="tpu_custom_call" | custom-call | tf_op jit(solution)/shard_map/attend_back/pallas_call | solution.py:189
  67.8 3.8 %attend_weights.1 = (bf16[608,1152]{1,0:T(8,128)(2,1)}, bf16[576,1152]{1,0:T(8,128)(2,1)}, bf16[576,1152]{1,0:T(8,128)(2,1)S(1)}, bf16[576,1152]{1,0:T(8,128)(2,1)S(1)}, f32[16,1152]{1,0:T(8,128)S(1)}) custom-call(bf16[256,1152]{1,0:T(8,128)(2,1)S(1)} %get-tuple-element.121.refs_0_, bf16[256,1152]{1,0:T(8,128)(2,1)S(1)} %get-tuple-element.122.refs_1_, ...), custom_call_target="tpu_custom_call" | custom-call | tf_op jit(solution)/shard_map/attend_weights/pallas_call | solution.py:189
  73.7 9.2 %collective-permute-done.9.refs_1_ = bf16[256,1152]{1,0:T(8,128)(2,1)} collective-permute-done((bf16[256,1152]{1,0:T(8,128)(2,1)S(1)}, bf16[256,1152]{1,0:T(8,128)(2,1)}, u32[]{:S(2)}, u32[]{:S(2)}) %collective-permute-start.9) | collective-permute-done | bytes 589856 | tf_op jit(solution)/shard_map/ppermute | solution.py:548
  86.0 3.8 %all-to-all-start.1 = ((bf16[16,16,1152]{2,1,0:T(8,128)(2,1)}), bf16[16,16,1152]{2,1,0:T(8,128)(2,1)S(1)}, u32[]{:S(2)}, u32[]{:S(2)}) async-start(bf16[16,16,1152]{2,1,0:T(8,128)(2,1)} %bitcast.10), calls=%async_computation.1 | async-start | bytes 1179648 | tf_op jit(solution)/shard_map/all_to_all | solution.py:552
  89.9 2.4 %copy-done = bf16[1152,2152]{0,1:T(8,128)(2,1)S(1)} copy-done((bf16[1152,2152]{0,1:T(8,128)(2,1)S(1)}, bf16[1152,2152]{0,1:T(8,128)(2,1)}, u32[]{:S(2)}) %copy-start) | copy-done | bytes 4958232
  92.3 2.4 %copy-done.2 = bf16[1152,2152]{0,1:T(8,128)(2,1)S(1)} copy-done((bf16[1152,2152]{0,1:T(8,128)(2,1)S(1)}, bf16[1152,2152]{0,1:T(8,128)(2,1)}, u32[]{:S(2)}) %copy-start.2) | copy-done | bytes 4958232
  96.8 11.6 %mlp_weights.1 = (bf16[576,768]{1,0:T(8,128)(2,1)}, bf16[576,384]{1,0:T(8,128)(2,1)}, bf16[576,768]{1,0:T(8,128)(2,1)S(1)}, bf16[576,384]{1,0:T(8,128)(2,1)S(1)}) custom-call(bf16[256,1152]{1,0:T(8,128)(2,1)S(1)} %copy-done.19, bf16[256,1152]{1,0:T(8,128)(2,1)} %collective-permute-done.9.refs_1_, bf16[256,1152]{1,0:T(8,128)(2,1)} %collective-permute-done.10.refs_2_, ...), custom_call_target="tpu_custom_call" | custom-call | tf_op jit(solution)/shard_map/mlp_weights/pallas_call | solution.py:189
  110.3 2.5 %turn.8 = (bf16[320,1152]{1,0:T(8,128)(2,1)}, f32[288,1152]{1,0:T(8,128)S(1)}, f32[16,1152]{1,0:T(8,128)S(1)}) custom-call(bf16[608,1152]{1,0:T(8,128)(2,1)} %collective-permute-done.7.refs_0_, bf16[576,1152]{1,0:T(8,128)(2,1)S(1)} %copy-done.13, f32[16,1152]{1,0:T(8,128)S(1)} %get-tuple-element.145.refs_2_), custom_call_target="tpu_custom_call" | custom-call | tf_op jit(solution)/shard_map/turn/pallas_call | solution.py:189
  114.3 7.1 %collective-permute-done.16.refs_0_ = bf16[576,1152]{1,0:T(8,128)(2,1)} collective-permute-done((bf16[576,1152]{1,0:T(8,128)(2,1)}, bf16[576,1152]{1,0:T(8,128)(2,1)}, u32[]{:S(2)}, u32[]{:S(2)}) %collective-permute-start.16) | collective-permute-done | bytes 1327136 | tf_op jit(solution)/shard_map/ppermute | solution.py:548
  121.5 2.3 %turn.9 = (bf16[288,1152]{1,0:T(8,128)(2,1)}, f32[288,1152]{1,0:T(8,128)S(1)}) custom-call(bf16[576,1152]{1,0:T(8,128)(2,1)} %collective-permute-done.16.refs_0_, bf16[576,1152]{1,0:T(8,128)(2,1)S(1)} %get-tuple-element.152.refs_1_), custom_call_target="tpu_custom_call" | custom-call | tf_op jit(solution)/shard_map/turn/pallas_call | solution.py:189
  125.2 6.1 %collective-permute-done.15.refs_0_ = bf16[576,768]{1,0:T(8,128)(2,1)} collective-permute-done((bf16[576,768]{1,0:T(8,128)(2,1)}, bf16[576,768]{1,0:T(8,128)(2,1)}, u32[]{:S(2)}, u32[]{:S(2)}) %collective-permute-start.15) | collective-permute-done | bytes 884768 | tf_op jit(solution)/shard_map/ppermute | solution.py:548
  133.8 3.9 %collective-permute-done.14.refs_0_ = bf16[320,1152]{1,0:T(8,128)(2,1)} collective-permute-done((bf16[320,1152]{1,0:T(8,128)(2,1)}, bf16[320,1152]{1,0:T(8,128)(2,1)}, u32[]{:S(2)}, u32[]{:S(2)}) %collective-permute-start.14) | collective-permute-done | bytes 737312 | tf_op jit(solution)/shard_map/ppermute | solution.py:548
  141.2 3.6 %collective-permute-done.19.refs_0_ = bf16[288,1152]{1,0:T(8,128)(2,1)} collective-permute-done((bf16[288,1152]{1,0:T(8,128)(2,1)}, bf16[288,1152]{1,0:T(8,128)(2,1)}, u32[]{:S(2)}, u32[]{:S(2)}) %collective-permute-start.19) | collective-permute-done | bytes 663584 | tf_op jit(solution)/shard_map/ppermute | solution.py:548
  150.0 9.6 %collective-permute-done.17.refs_0_ = bf16[176,1152]{1,0:T(8,128)(2,1)S(1)} collective-permute-done((bf16[176,1152]{1,0:T(8,128)(2,1)S(1)}, bf16[176,1152]{1,0:T(8,128)(2,1)S(1)}, u32[]{:S(2)}, u32[]{:S(2)}) %collective-permute-start.17) | collective-permute-done | bytes 405536 | tf_op jit(solution)/shard_map/ppermute | solution.py:548
  159.8 5.7 %collective-permute-done.23.refs_0_ = bf16[288,768]{1,0:T(8,128)(2,1)S(1)} collective-permute-done((bf16[288,768]{1,0:T(8,128)(2,1)S(1)}, bf16[288,768]{1,0:T(8,128)(2,1)S(1)}, u32[]{:S(2)}, u32[]{:S(2)}) %collective-permute-start.23) | collective-permute-done | bytes 442400 | tf_op jit(solution)/shard_map/ppermute | solution.py:548
  166.8 9.8 %collective-permute-done.21.refs_0_ = bf16[144,1152]{1,0:T(8,128)(2,1)S(1)} collective-permute-done((bf16[144,1152]{1,0:T(8,128)(2,1)S(1)}, bf16[144,1152]{1,0:T(8,128)(2,1)S(1)}, u32[]{:S(2)}, u32[]{:S(2)}) %collective-permute-start.21) | collective-permute-done | bytes 331808 | tf_op jit(solution)/shard_map/ppermute | solution.py:548
  176.7 2.2 %collective-permute-start.22 = (bf16[72,1152]{1,0:T(8,128)(2,1)S(1)}, bf16[72,1152]{1,0:T(8,128)(2,1)S(1)}, u32[]{:S(2)}, u32[]{:S(2)}) collective-permute-start(bf16[72,1152]{1,0:T(8,128)(2,1)S(1)} %get-tuple-element.179), channel_id=1, source_target_pairs={{0,16},{2,18},{4,20},{6,22},{8,24},{10,26},{12,28},{14,30},{16,0},... | collective-permute-start | bytes 497672 | tf_op jit(solution)/shard_map/ppermute | solution.py:548
  180.3 6.0 %collective-permute-done.27.refs_3_ = bf16[72,1152]{1,0:T(8,128)(2,1)S(1)} collective-permute-done((bf16[72,1152]{1,0:T(8,128)(2,1)S(1)}, bf16[72,1152]{1,0:T(8,128)(2,1)S(1)}, u32[]{:S(2)}, u32[]{:S(2)}) %collective-permute-start.27) | collective-permute-done | bytes 165920 | tf_op jit(solution)/shard_map/ppermute | solution.py:548
  (148 shorter events, 48.6 us)
Async XLA Ops:
  3.3 24.7 %all-to-all-start = ((bf16[16,16,1152]{2,1,0:T(8,128)(2,1)}), bf16[16,16,1152]{2,1,0:T(8,128)(2,1)S(1)}, u32[]{:S(2)}, u32[]{:S(2)}) async-start(bf16[16,16,1152]{2,1,0:T(8,128)(2,1)} %bitcast.41), calls=%async_computation | async-start | bytes 1179648 | tf_op jit(solution)/shard_map/all_to_all | solution.py:552
  53.1 4.0 %collective-permute-start.2 = (bf16[256,1152]{1,0:T(8,128)(2,1)S(1)}, bf16[256,1152]{1,0:T(8,128)(2,1)S(1)}, u32[]{:S(2)}, u32[]{:S(2)}) collective-permute-start(bf16[256,1152]{1,0:T(8,128)(2,1)S(1)} %get-tuple-element.109.refs_2_.refs_4_), channel_id=1, source_target_pairs={{0,1},{1,0},{2,3},{3,2},{4,5},{5,4},{6,7},{7,6},{8,9},{9,8},{10,11... | collective-permute-start | bytes 1769480 | tf_op jit(solution)/shard_map/ppermute | solution.py:544
  53.6 20.1 %collective-permute-start.8 = (bf16[256,1152]{1,0:T(8,128)(2,1)S(1)}, bf16[256,1152]{1,0:T(8,128)(2,1)S(1)}, u32[]{:S(2)}, u32[]{:S(2)}) collective-permute-start(bf16[256,1152]{1,0:T(8,128)(2,1)S(1)} %get-tuple-element.136), channel_id=1, source_target_pairs={{0,8},{2,10},{4,12},{6,14},{8,0},{10,2},{12,4},{14,6},{16,24},{18,... | collective-permute-start | bytes 1769480 | tf_op jit(solution)/shard_map/ppermute | solution.py:548
  55.0 27.9 %collective-permute-start.9 = (bf16[256,1152]{1,0:T(8,128)(2,1)S(1)}, bf16[256,1152]{1,0:T(8,128)(2,1)}, u32[]{:S(2)}, u32[]{:S(2)}) collective-permute-start(bf16[256,1152]{1,0:T(8,128)(2,1)S(1)} %get-tuple-element.136), channel_id=1, source_target_pairs={{0,4},{2,6},{4,0},{6,2},{8,12},{10,14},{12,8},{14,10},{16,20},{18,... | collective-permute-start | bytes 1769480 | tf_op jit(solution)/shard_map/ppermute | solution.py:548
  56.0 26.9 %collective-permute-start.10 = (bf16[256,1152]{1,0:T(8,128)(2,1)S(1)}, bf16[256,1152]{1,0:T(8,128)(2,1)}, u32[]{:S(2)}, u32[]{:S(2)}) collective-permute-start(bf16[256,1152]{1,0:T(8,128)(2,1)S(1)} %get-tuple-element.136), channel_id=1, source_target_pairs={{0,12},{2,14},{4,8},{6,10},{8,4},{10,6},{12,0},{14,2},{16,28},{18,... | collective-permute-start | bytes 1769480 | tf_op jit(solution)/shard_map/ppermute | solution.py:548
  71.6 38.7 %collective-permute-start.7 = (bf16[608,1152]{1,0:T(8,128)(2,1)}, bf16[608,1152]{1,0:T(8,128)(2,1)}, u32[]{:S(2)}, u32[]{:S(2)}) collective-permute-start(bf16[608,1152]{1,0:T(8,128)(2,1)} %get-tuple-element.135), channel_id=1, source_target_pairs={{0,2},{2,0},{4,6},{6,4},{8,10},{10,8},{12,14},{14,12},{16,18},{18,... | collective-permute-start | bytes 4202504 | tf_op jit(solution)/shard_map/ppermute | solution.py:548
  83.7 37.8 %collective-permute-start.16 = (bf16[576,1152]{1,0:T(8,128)(2,1)}, bf16[576,1152]{1,0:T(8,128)(2,1)}, u32[]{:S(2)}, u32[]{:S(2)}) collective-permute-start(bf16[576,1152]{1,0:T(8,128)(2,1)} %get-tuple-element.150), channel_id=1, source_target_pairs={{0,4},{2,6},{4,0},{6,2},{8,12},{10,14},{12,8},{14,10},{16,20},{18,... | collective-permute-start | bytes 3981320 | tf_op jit(solution)/shard_map/ppermute | solution.py:548
  84.7 5.2 %collective-permute-start.12 = (bf16[256,1152]{1,0:T(8,128)(2,1)}, bf16[256,1152]{1,0:T(8,128)(2,1)}, u32[]{:S(2)}, u32[]{:S(2)}) collective-permute-start(bf16[256,1152]{1,0:T(8,128)(2,1)} %collective-permute-done.9.refs_1_), channel_id=1, source_target_pairs={{0,1},{1,0},{2,3},{3,2},{4,5},{5,4},{6,7},{7,6},{8,9},{9,8},{10,11... | collective-permute-start | bytes 1769480 | tf_op jit(solution)/shard_map/ppermute | solution.py:544
  85.7 4.1 %collective-permute-start.13 = (bf16[256,1152]{1,0:T(8,128)(2,1)}, bf16[256,1152]{1,0:T(8,128)(2,1)}, u32[]{:S(2)}, u32[]{:S(2)}) collective-permute-start(bf16[256,1152]{1,0:T(8,128)(2,1)} %collective-permute-done.10.refs_2_), channel_id=1, source_target_pairs={{0,1},{1,0},{2,3},{3,2},{4,5},{5,4},{6,7},{7,6},{8,9},{9,8},{10,11... | collective-permute-start | bytes 1769480 | tf_op jit(solution)/shard_map/ppermute | solution.py:544
  86.0 39.2 %all-to-all-start.1 = ((bf16[16,16,1152]{2,1,0:T(8,128)(2,1)}), bf16[16,16,1152]{2,1,0:T(8,128)(2,1)S(1)}, u32[]{:S(2)}, u32[]{:S(2)}) async-start(bf16[16,16,1152]{2,1,0:T(8,128)(2,1)} %bitcast.10), calls=%async_computation.1 | async-start | bytes 1179648 | tf_op jit(solution)/shard_map/all_to_all | solution.py:552
  108.5 22.8 %collective-permute-start.15 = (bf16[576,768]{1,0:T(8,128)(2,1)}, bf16[576,768]{1,0:T(8,128)(2,1)}, u32[]{:S(2)}, u32[]{:S(2)}) collective-permute-start(bf16[576,768]{1,0:T(8,128)(2,1)} %get-tuple-element.148), channel_id=1, source_target_pairs={{0,2},{2,0},{4,6},{6,4},{8,10},{10,8},{12,14},{14,12},{16,18},{18,... | collective-permute-start | bytes 2654216 | tf_op jit(solution)/shard_map/ppermute | solution.py:548
  112.8 24.9 %collective-permute-start.14 = (bf16[320,1152]{1,0:T(8,128)(2,1)}, bf16[320,1152]{1,0:T(8,128)(2,1)}, u32[]{:S(2)}, u32[]{:S(2)}) collective-permute-start(bf16[320,1152]{1,0:T(8,128)(2,1)} %get-tuple-element.147), channel_id=1, source_target_pairs={{0,4},{2,6},{4,0},{6,2},{8,12},{10,14},{12,8},{14,10},{16,20},{18,... | collective-permute-start | bytes 2211848 | tf_op jit(solution)/shard_map/ppermute | solution.py:548
  123.8 20.9 %collective-permute-start.19 = (bf16[288,1152]{1,0:T(8,128)(2,1)}, bf16[288,1152]{1,0:T(8,128)(2,1)}, u32[]{:S(2)}, u32[]{:S(2)}) collective-permute-start(bf16[288,1152]{1,0:T(8,128)(2,1)} %get-tuple-element.164), channel_id=1, source_target_pairs={{0,2},{2,0},{4,6},{6,4},{8,10},{10,8},{12,14},{14,12},{16,18},{18,... | collective-permute-start | bytes 1990664 | tf_op jit(solution)/shard_map/ppermute | solution.py:548
  124.4 23.0 %collective-permute-start.18 = (bf16[576,384]{1,0:T(8,128)(2,1)}, bf16[576,384]{1,0:T(8,128)(2,1)}, u32[]{:S(2)}, u32[]{:S(2)}) collective-permute-start(bf16[576,384]{1,0:T(8,128)(2,1)} %get-tuple-element.163), channel_id=1, source_target_pairs={{0,16},{2,18},{4,20},{6,22},{8,24},{10,26},{12,28},{14,30},{16,0},... | collective-permute-start | bytes 1327112 | tf_op jit(solution)/shard_map/ppermute | solution.py:548
  125.2 51.5 %collective-permute-start.6 = (bf16[256,1152]{1,0:T(8,128)(2,1)S(1)}, bf16[256,1152]{1,0:T(8,128)(2,1)S(1)}, u32[]{:S(2)}, u32[]{:S(2)}) collective-permute-start(bf16[256,1152]{1,0:T(8,128)(2,1)S(1)} %bitcast.29), channel_id=1, source_target_pairs={{0,1},{1,0},{2,3},{3,2},{4,5},{5,4},{6,7},{7,6},{8,9},{9,8},{10,11... | collective-permute-start | bytes 1769480 | tf_op jit(solution)/shard_map/ppermute | solution.py:544
  139.0 20.6 %collective-permute-start.17 = (bf16[176,1152]{1,0:T(8,128)(2,1)S(1)}, bf16[176,1152]{1,0:T(8,128)(2,1)S(1)}, u32[]{:S(2)}, u32[]{:S(2)}) collective-permute-start(bf16[176,1152]{1,0:T(8,128)(2,1)S(1)} %get-tuple-element.161), channel_id=1, source_target_pairs={{0,8},{2,10},{4,12},{6,14},{8,0},{10,2},{12,4},{14,6},{16,24},{18,... | collective-permute-start | bytes 1216520 | tf_op jit(solution)/shard_map/ppermute | solution.py:548
  139.7 25.7 %collective-permute-start.23 = (bf16[288,768]{1,0:T(8,128)(2,1)S(1)}, bf16[288,768]{1,0:T(8,128)(2,1)S(1)}, u32[]{:S(2)}, u32[]{:S(2)}) collective-permute-start(bf16[288,768]{1,0:T(8,128)(2,1)S(1)} %get-tuple-element.187), channel_id=1, source_target_pairs={{0,16},{2,18},{4,20},{6,22},{8,24},{10,26},{12,28},{14,30},{16,0},... | collective-permute-start | bytes 1327112 | tf_op jit(solution)/shard_map/ppermute | solution.py:548
  146.0 30.7 %collective-permute-start.21 = (bf16[144,1152]{1,0:T(8,128)(2,1)S(1)}, bf16[144,1152]{1,0:T(8,128)(2,1)S(1)}, u32[]{:S(2)}, u32[]{:S(2)}) collective-permute-start(bf16[144,1152]{1,0:T(8,128)(2,1)S(1)} %get-tuple-element.175), channel_id=1, source_target_pairs={{0,8},{2,10},{4,12},{6,14},{8,0},{10,2},{12,4},{14,6},{16,24},{18,... | collective-permute-start | bytes 995336 | tf_op jit(solution)/shard_map/ppermute | solution.py:548
  148.5 11.3 %collective-permute-start.24 = (bf16[288,384]{1,0:T(8,128)(2,1)S(1)}, bf16[288,384]{1,0:T(8,128)(2,1)S(1)}, u32[]{:S(2)}, u32[]{:S(2)}) collective-permute-start(bf16[288,384]{1,0:T(8,128)(2,1)S(1)} %get-tuple-element.188), channel_id=1, source_target_pairs={{0,2},{2,0},{4,6},{6,4},{8,10},{10,8},{12,14},{14,12},{16,18},{18,... | collective-permute-start | bytes 663560 | tf_op jit(solution)/shard_map/ppermute | solution.py:548
  159.7 28.1 %collective-permute-start.20 = (bf16[104,1152]{1,0:T(8,128)(2,1)S(1)}, bf16[104,1152]{1,0:T(8,128)(2,1)S(1)}, u32[]{:S(2)}, u32[]{:S(2)}) collective-permute-start(bf16[104,1152]{1,0:T(8,128)(2,1)S(1)} %get-tuple-element.174), channel_id=1, source_target_pairs={{0,16},{2,18},{4,20},{6,22},{8,24},{10,26},{12,28},{14,30},{16,0},... | collective-permute-start | bytes 718856 | tf_op jit(solution)/shard_map/ppermute | solution.py:548
  165.6 14.7 %collective-permute-start.25 = (bf16[72,1152]{1,0:T(8,128)(2,1)S(1)}, bf16[72,1152]{1,0:T(8,128)(2,1)S(1)}, u32[]{:S(2)}, u32[]{:S(2)}) collective-permute-start(bf16[72,1152]{1,0:T(8,128)(2,1)S(1)} %get-tuple-element.190), channel_id=1, source_target_pairs={{0,8},{2,10},{4,12},{6,14},{8,0},{10,2},{12,4},{14,6},{16,24},{18,... | collective-permute-start | bytes 497672 | tf_op jit(solution)/shard_map/ppermute | solution.py:548
  165.7 14.6 %collective-permute-start.26 = (bf16[72,1152]{1,0:T(8,128)(2,1)S(1)}, bf16[72,1152]{1,0:T(8,128)(2,1)S(1)}, u32[]{:S(2)}, u32[]{:S(2)}) collective-permute-start(bf16[72,1152]{1,0:T(8,128)(2,1)S(1)} %get-tuple-element.191), channel_id=1, source_target_pairs={{0,4},{2,6},{4,0},{6,2},{8,12},{10,14},{12,8},{14,10},{16,20},{18,... | collective-permute-start | bytes 497672 | tf_op jit(solution)/shard_map/ppermute | solution.py:548
  176.6 9.7 %collective-permute-start.27 = (bf16[72,1152]{1,0:T(8,128)(2,1)S(1)}, bf16[72,1152]{1,0:T(8,128)(2,1)S(1)}, u32[]{:S(2)}, u32[]{:S(2)}) collective-permute-start(bf16[72,1152]{1,0:T(8,128)(2,1)S(1)} %get-tuple-element.192), channel_id=1, source_target_pairs={{0,12},{2,14},{4,8},{6,10},{8,4},{10,6},{12,0},{14,2},{16,28},{18,... | collective-permute-start | bytes 497672 | tf_op jit(solution)/shard_map/ppermute | solution.py:548
  176.7 11.0 %collective-permute-start.22 = (bf16[72,1152]{1,0:T(8,128)(2,1)S(1)}, bf16[72,1152]{1,0:T(8,128)(2,1)S(1)}, u32[]{:S(2)}, u32[]{:S(2)}) collective-permute-start(bf16[72,1152]{1,0:T(8,128)(2,1)S(1)} %get-tuple-element.179), channel_id=1, source_target_pairs={{0,16},{2,18},{4,20},{6,22},{8,24},{10,26},{12,28},{14,30},{16,0},... | collective-permute-start | bytes 497672 | tf_op jit(solution)/shard_map/ppermute | solution.py:548
  (43 other events, 440.6 us)

commit v5 on v4

--- a/solution.py
+++ b/solution.py
@@ -156,7 +156,7 @@
         done += now
 
 
-def call(body, ins, outs, scratch=(), vmem=16, far=False):
+def call(body, ins, outs, scratch=(), vmem=16, far=False, us=0):
     ins_flat, ins_tree = jax.tree.flatten(ins)
     is_out = lambda x: isinstance(x, tuple)
     outs_flat, outs_tree = jax.tree.flatten(outs, is_leaf=is_out)
@@ -193,6 +193,7 @@
         in_specs=[pl.BlockSpec(memory_space=pltpu.HBM if far else pltpu.VMEM)] * n_in,
         out_specs=[pl.BlockSpec(memory_space=pltpu.VMEM)] * n_out,
         scratch_shapes=(copies if far else []) + list(scratch),
+        cost_estimate=pl.CostEstimate(flops=us * 10**9, bytes_accessed=us * 10**6, transcendentals=0),
         compiler_params=pltpu.CompilerParams(vmem_limit_bytes=vmem * MIB),
     )(*ins_flat)
     return types.SimpleNamespace(**jax.tree.unflatten(outs_tree, results))
@@ -219,10 +220,6 @@
     index = jnp.where(half == core, index, index + 2 * n_dev * half_rows)
     pick = one_hot(index, (cap, 2 * cap), 1)
     return dot(pick, jnp.concatenate([given.mine[...], given.other[...]], axis=0))
-
-
-def unpack(n_dev, half_rows, given, made):
-    put(made.g, block_rows(given, n_dev, made.g.shape[0], half_rows, 1))
 
 
 def image_mask(lengths, owners, cap):
@@ -246,23 +243,26 @@
             self.size += lane_pad(size)
 
 
-def attend(n_dev, half_rows, vec, given, made):
+def arrive(n_dev, half_rows, vec, given, made):
     cap = made.x.shape[0]
-    same = image_mask(given.lengths[...].astype(f32), given.owners[...].astype(f32), cap)
-    put(made.mask, same)
     x = block_rows(given, n_dev, cap, half_rows, 0)
     put(made.x, x)
-    row = given.vec
     normed, _ = norm_parts(x)
-    h1 = (normed * row[:, vec.gain1] + row[:, vec.shift1]).astype(bf16)
-    put(made.h1, h1)
+    put(made.h1, normed * given.vec[:, vec.gain1] + given.vec[:, vec.shift1])
+    put(made.g, block_rows(given, n_dev, cap, half_rows, 1))
+    put(made.mask, image_mask(given.lengths[...].astype(f32), given.owners[...].astype(f32), cap))
+
+
+def attend(vec, given, made):
+    same = given.mask[...] > 0.5
+    row, h1 = given.vec, given.h1[...]
     put(made.q, dot_cols(h1, given.wq[...]) + row[:, vec.bq])
     put(made.k, dot_cols(h1, given.wk[...]))
     put(made.v, dot_cols(h1, given.wv[...]) + row[:, vec.bv])
     for h in range(made.q.shape[1] // HD):
         cols = slice(h * HD, (h + 1) * HD)
         s = dot_cols(made.q[:, cols], made.k[:, cols]) * HD ** (-0.5)
-        s = jnp.where(same > 0.5, s, masked_score)
+        s = jnp.where(same, s, masked_score)
         top = jnp.max(s, axis=1, keepdims=True)
         e = jnp.exp(s - top)
         total = lane_sum(e)
@@ -311,7 +311,7 @@
         out_total[...] += dot(hidden.astype(bf16), wr)
         dh2_total[...] += dot(dexp, we)
 
-    @pl.loop(0, full)
+    @pl.loop(0, full, unroll=True)
     def _(i):
         at = pl.multiple_of(i * step, step)
         chunk(pl.ds(at, step), pl.ds(pl.multiple_of(first + at, 128), step))
@@ -448,14 +448,13 @@
 
 
 def mlp_weights(
-    far_bits, orders, bounds, n_dev, vec, given, made, h2_all, g_all, hidden_all, dexp_all, we_part,
-    wr_part, natural, ordered,
+    far_bits, orders, bounds, n_dev, vec, hidden_width, given, made, h2_all, g_all, hidden_all, dexp_all,
+    natural, ordered,
 ):
     cap, width = given.h2.shape
     half_cap = cap // 2
     share = share_of(far_bits)
-    part, hidden_width = we_part.shape[0], given.we.shape[0]
-    last = hidden_width - 3 * part
+    part = given.we_part.shape[0]
     be = vec.be.start
     bias = jnp.zeros((1, part), f32)
     for i in range(4):
@@ -464,17 +463,6 @@
         if end < (i + 1) * part:
             piece = jnp.concatenate([piece, jnp.zeros((1, (i + 1) * part - end), f32)], axis=1)
         bias += jnp.where(share == i, piece, 0.0)
-    for source, near in ((given.we, we_part), (given.wr, wr_part)):
-
-        @pl.when(share < 3)
-        def _():
-            near[...] = source[pl.ds(pl.multiple_of(share * part, 16), part), :]
-
-        @pl.when(share == 3)
-        def _():
-            near[:last, :] = source[3 * part :, :]
-            near[last:, :] = jnp.zeros((part - last, width), bf16)
-
     for k in range(4):
         rows = slice(k * cap, (k + 1) * cap)
         if k == 0:
@@ -485,9 +473,9 @@
                 at = slice(k * cap + i * half_cap, k * cap + (i + 1) * half_cap)
                 h2_all[at, :] = ref[:half_cap, :]
                 g_all[at, :] = ref[half_cap:, :]
-        hidden, slope = gelu_both(dot_cols(h2_all[rows, :], we_part[...]) + bias)
+        hidden, slope = gelu_both(dot_cols(h2_all[rows, :], given.we_part[...]) + bias)
         hidden_all[rows, :] = hidden.astype(bf16)
-        dexp_all[rows, :] = (dot_cols(g_all[rows, :], wr_part[...]) * slope).astype(bf16)
+        dexp_all[rows, :] = (dot_cols(g_all[rows, :], given.wr_part[...]) * slope).astype(bf16)
     half = width // 2
     natural[:, :part] = dot_rows(g_all[...], hidden_all[...])
     natural[:, part : 2 * part] = dot_rows(h2_all[...], dexp_all[...])
@@ -511,8 +499,12 @@
         put(made.vec, put_vectors(made.give, rows // 2, vec_rows, vec))
 
 
-def last_sums(bounds, vec_rows, given, made):
-    put(made.vec, given.vec[...] + got_vectors(given.got[0], vec_rows))
+def last_sums(bounds, vec_rows, vec, given, made):
+    sums = given.vec[...] + got_vectors(given.got[0], vec_rows)
+    for name, ref in zip(vec.names, made.vectors):
+        at = getattr(vec, name)
+        for here, row, lanes in pieces_of(at.start, at.stop - at.start, sums.shape[1]):
+            ref[here] = sums[row, lanes].reshape(here.stop - here.start)
     for group, (keep, got) in enumerate(zip(given.keep, given.got)):
         value = keep[...].astype(f32) + got[: keep.shape[0], :].astype(f32)
         for i, cols, lanes in parts_between(bounds, group, made.weights[0].shape[1], 4):
@@ -638,12 +630,12 @@
         gain1=width, shift1=width, bo=width, gain2=width, shift2=width, br=width, be=hidden_width,
         bq=heads_width, bv=heads_width,
     )
-    vectors = [
+    vector_args = [
         first_gain, first_shift, output_bias, second_gain, second_shift, reduce_bias, expand_bias,
         query_bias, value_bias,
     ]
     vectors = jnp.concatenate(
-        [jnp.pad(v, (0, lane_pad(v.shape[0]) - v.shape[0])) for v in vectors]
+        [jnp.pad(v, (0, lane_pad(v.shape[0]) - v.shape[0])) for v in vector_args]
     ).reshape(1, -1)
     sizes = dict(lengths=image_lengths.reshape(1, -1), owners=image_owner.reshape(1, -1))
     wide32, wide16 = ((cap, width), f32), ((cap, width), bf16)
@@ -655,21 +647,29 @@
     sent = call(
         at_place(pack, tokens), dict(**sizes, x=patches, g=cotangent), dict(send=wide16), far=True, vmem=62
     )
-    got = spread(sent.send)
+    part = -(-hidden_width // 64) * 16
+    at_share = share_of(far_bits) * part
+    padding = ((0, 4 * part - hidden_width), (0, 0))
+    we_part, wr_part = (
+        lax.dynamic_slice_in_dim(jnp.pad(w, padding), at_share, part, 0) for w in (we, wr)
+    )
+    got, we_part, wr_part = lax.optimization_barrier((spread(sent.send), we_part, wr_part))
     arrived = dict(**sizes, mine=got, other=swap_cores(got))
+    came_in = call(
+        at_place(arrive, vec), dict(**arrived, vec=vectors),
+        dict(mask=((cap, cap), f32), x=wide16, h1=wide16, g=wide16), us=6,
+    )
+    mask, x, h1, g = came_in.mask, came_in.x, came_in.h1, came_in.g
     fwd = call(
-        at_place(attend, vec),
-        dict(**arrived, vec=vectors, wq=wq, wk=wk, wv=wv, wo=wo),
-        dict(
-            mask=((cap, cap), f32), x=wide16, h1=wide16, q=head16, k=head16, v=head16,
-            log=((cap, heads), f32), att=head16, branch=wide16,
-        ),
+        functools.partial(attend, vec),
+        dict(h1=h1, mask=mask, vec=vectors, wq=wq, wk=wk, wv=wv, wo=wo),
+        dict(q=head16, k=head16, v=head16, log=((cap, heads), f32), att=head16, branch=wide16),
+        us=5,
     )
     branch_other = swap_cores(fwd.branch)
-    g = call(at_place(unpack), arrived, dict(g=wide16)).g
     mid = call(
         functools.partial(mlp, vec),
-        dict(x=fwd.x, branch=fwd.branch, branch_other=branch_other, g=g, vec=vectors, we=we, wr=wr),
+        dict(x=x, branch=fwd.branch, branch_other=branch_other, g=g, vec=vectors, we=we, wr=wr),
         dict(
             middle=wide32, h2=wide16, halves=wide16, sums=[wide16, wide16],
             be_grad=((1, lane_pad(hidden_width)), f32),
@@ -686,7 +686,7 @@
     att_back = call(
         attend_back,
         dict(
-            mask=fwd.mask, q=fwd.q, k=fwd.k, v=fwd.v, datt=half_back.datt, log=fwd.log,
+            mask=mask, q=fwd.q, k=fwd.k, v=fwd.v, datt=half_back.datt, log=fwd.log,
             wq=wq, wk=wk, wv=wv,
         ),
         dict(
@@ -697,7 +697,7 @@
     first = call(
         functools.partial(first_back, vec),
         dict(
-            x=fwd.x, dh1=att_back.dh1, dh1_other=[swap_cores(rows) for rows in att_back.dh1],
+            x=x, dh1=att_back.dh1, dh1_other=[swap_cores(rows) for rows in att_back.dh1],
             vec=vectors, dmid=half_back.dmid,
         ),
         dict(dx=wide16, vec_grad=((1, 2 * width), f32)),
@@ -713,7 +713,7 @@
     products = call(
         functools.partial(attend_weights, n_dev, attend_orders, attend_bounds),
         dict(
-            h1=fwd.h1, branch_grad=half_back.branch_grad,
+            h1=h1, branch_grad=half_back.branch_grad,
             right=[att_back.dq, att_back.dk, att_back.dv, fwd.att],
             vec_grads=[first.vec_grad, half_back.vec_grad, mid.be_grad, att_back.vec_grad],
         ),
@@ -730,18 +730,17 @@
     far_other = [swap_cores(rows) for rows in far[:2]]
     far[2] = after(far[2], far_other[0])
     far_other.append(swap_cores(far[2]))
-    part = -(-hidden_width // 64) * 16
     mlp_bounds = (0, 768, lane_pad(2 * part))
     spans = [after_ - before for before, after_ in zip(mlp_bounds, mlp_bounds[1:])]
     mlp_half = [((width // 2, span), bf16) for span in spans]
     grads = call(
         functools.partial(
-            mlp_weights, far_bits, [list(o) + list(far_bits) for o in mlp_orders], mlp_bounds, n_dev, vec
+            mlp_weights, far_bits, [list(o) + list(far_bits) for o in mlp_orders], mlp_bounds, n_dev, vec,
+            hidden_width,
         ),
-        dict(vec=vectors, we=we, wr=wr, h2=mid.h2, g=g, far=far, far_other=far_other),
+        dict(vec=vectors, we_part=we_part, wr_part=wr_part, h2=mid.h2, g=g, far=far, far_other=far_other),
         dict(give=mlp_half, keep=mlp_half),
         scratch=[scratch((4 * cap, width), bf16)] * 2 + [scratch((4 * cap, part), bf16)] * 2
-        + [scratch((part, width), bf16)] * 2
         + [scratch((width, mlp_bounds[-1]), f32), scratch((width, max(spans)), f32)],
         vmem=36,
     )
@@ -772,12 +771,14 @@
         dict(weights=[((own_rows, hidden_width), f32)] * 2),
     ).weights
     own = call(
-        functools.partial(last_sums, attend_bounds, vec_rows),
+        functools.partial(last_sums, attend_bounds, vec_rows, vec),
         dict(vec=a.vec, keep=a.kept(), got=a.received()),
-        dict(vec=((vec_rows, columns), f32), weights=[((own_rows, heads_width), f32)] * 4),
-    )
-    flat = own.vec.reshape(-1)
-    total = types.SimpleNamespace(**{name: flat[getattr(vec, name)] for name in vec.names})
+        dict(
+            vectors=[((v.shape[0],), f32) for v in vector_args],
+            weights=[((own_rows, heads_width), f32)] * 4,
+        ),
+    )
+    total = types.SimpleNamespace(**dict(zip(vec.names, own.vectors)))
     wq_sum, wk_sum, wv_sum, wo_sum = own.weights
     wr_sum, we_sum = mlp_own
     return (

time: 192 us -> 184 us (0.958)
  local copies, waits for them, and re-layouts: 19.4 us -> 10.3 us
    unnamed x82 -> x84, local copies, waits for them, and re-layouts: 17.5 us -> 8.33 us
    ppermute x18, waiting for transfers between devices: 61 us -> 65 us  [swap_dp(): lax.ppermute(values, DP, [(i, i ^ flip) for i in range(lax.axis_size(DP))])]
    all_to_all x2, waiting for transfers between devices: 16.2 us -> 14.2 us  [spread(): return lax.all_to_all(rows, DP, split_axis=0, concat_axis=0, tiled=True)]
  transfers between devices with their start and end apart: 30 -> 30, of which waited for: 14 -> 16; matrix products, arithmetic and copies ran while one was open for 0% -> 1% of each run, Pallas kernels for 20% -> 21%
where the time goes in v5:
time: 184 us; the launch traced here: 183 us
  waiting for transfers between devices  83.7 us (45%)
  Pallas kernels  55.4 us (30%)
  starting transfers between devices  32.3 us (18%)
  local copies, waits for them, and re-layouts  10.3 us (6%)
    ppermute x18, waiting for transfers between devices, swap_dp(): lax.ppermute(values, DP, [(i, i ^ flip) for i in range(lax.axis_size(DP))])  65 us
    pallas_call x22, Pallas kernels, call(): pl.pallas_call(kernel, name=getattr(body, 'func', body).__name__, out_sha...  55.4 us
    ppermute x18, starting transfers between devices, swap_dp(): lax.ppermute(values, DP, [(i, i ^ flip) for i in range(lax.axis_size(DP))])  17.7 us
    all_to_all x2, waiting for transfers between devices, spread(): return lax.all_to_all(rows, DP, split_axis=0, concat_axis=0, tiled=True)  14.2 us
    all_to_all x2, starting transfers between devices, spread(): return lax.all_to_all(rows, DP, split_axis=0, concat_axis=0, tiled=True)  12.8 us
    unnamed x84, local copies, waits for them, and re-layouts  8.33 us
    ppermute x10, waiting for transfers between devices, swap_cores(): return lax.ppermute(values, CORE, [(0, 1), (1, 0)])  4.46 us
  transfers between devices with their start and end apart: 30, of which 16 were waited for; matrix products, arithmetic and copies ran while one was open for 1% of the time, Pallas kernels for 21%

profile of v5, /device:TPU:0, one launch (start us, length us, event | category | flops | bytes accessed | tf_op | source)
XLA Modules:
  0.0 183.0 jit_solution(13084170233050609875)
XLA Ops:
  0.7 2.4 %pack.1 = bf16[256,1152]{1,0:T(8,128)(2,1)} custom-call(bf16[128,1152]{1,0:T(8,128)(2,1)} %refs_0_.1, s32[1,64]{1,0:T(1,128)} %bitcast.31, s32[1,64]{1,0:T(1,128)} %bitcast.35, bf16[128,1152]{1,0:T(8,128)(2,1)} %refs_3_.1), custom_call_target="tpu_custom_call" | custom-call | tf_op jit(solution)/shard_map/pack/pallas_call | solution.py:189
  3.1 8.3 %all-to-all-start = ((bf16[16,16,1152]{2,1,0:T(8,128)(2,1)}), bf16[16,16,1152]{2,1,0:T(8,128)(2,1)S(1)}, u32[]{:S(2)}, u32[]{:S(2)}) async-start(bf16[16,16,1152]{2,1,0:T(8,128)(2,1)} %bitcast.39), calls=%async_computation | async-start | bytes 1179648 | tf_op jit(solution)/shard_map/all_to_all | solution.py:544
  13.5 14.2 %all-to-all-done = bf16[16,16,1152]{2,1,0:T(8,128)(2,1)S(1)} async-done(((bf16[16,16,1152]{2,1,0:T(8,128)(2,1)}), bf16[16,16,1152]{2,1,0:T(8,128)(2,1)S(1)}, u32[]{:S(2)}, u32[]{:S(2)}) %all-to-all-start) | async-done | bytes 589856 | tf_op jit(solution)/shard_map/all_to_all | solution.py:544
  32.5 4.8 %attend.1 = (bf16[256,576]{1,0:T(8,128)(2,1)S(1)}, bf16[256,1152]{1,0:T(8,128)(2,1)S(1)}, bf16[256,576]{1,0:T(8,128)(2,1)S(1)}, f32[256,8]{1,0:T(8,128)S(1)}, bf...) custom-call(bf16[256,1152]{1,0:T(8,128)(2,1)S(1)} %get-tuple-element.120.refs_0_.refs_1_, ...), custom_call_target="tpu_custom_call" | custom-call | flops 5000000000 | bytes 5000000 | tf_op jit(solution)/shard_map/attend/pallas_call | solution.py:189
  37.4 2.0 %collective-permute-done.1.refs_1_ = bf16[256,1152]{1,0:T(8,128)(2,1)S(1)} collective-permute-done((bf16[256,1152]{1,0:T(8,128)(2,1)S(1)}, bf16[256,1152]{1,0:T(8,128)(2,1)S(1)}, u32[]{:S(2)}, u32[]{:S(2)}) %collective-permute-start.1) | collective-permute-done | bytes 589856 | tf_op jit(solution)/shard_map/ppermute | solution.py:536
  39.4 7.5 %mlp.1 = (f32[1,2176]{1,0:T(1,128)S(1)}, bf16[256,1152]{1,0:T(8,128)(2,1)S(1)}, bf16[256,1152]{1,0:T(8,128)(2,1)S(1)}, f32[256,1152]{1,0:T(8,128)S(1)}, bf16[256...) custom-call(bf16[256,1152]{1,0:T(8,128)(2,1)S(1)} %get-tuple-element.122.refs_0_, ...), custom_call_target="tpu_custom_call" | custom-call | tf_op jit(solution)/shard_map/mlp/pallas_call | solution.py:189
  52.7 5.6 %attend_back.1 = (bf16[128,1152]{1,0:T(8,128)(2,1)S(1)}, bf16[128,1152]{1,0:T(8,128)(2,1)S(1)}, bf16[256,576]{1,0:T(8,128)(2,1)S(1)}, bf16[256,576]{1,0:T(8,128)...) custom-call(bf16[256,576]{1,0:T(8,128)(2,1)S(1)} %get-tuple-element.127.refs_0_, ...), custom_call_target="tpu_custom_call" | custom-call | tf_op jit(solution)/shard_map/attend_back/pallas_call | solution.py:189
  61.4 3.8 %attend_weights.1 = (bf16[608,1152]{1,0:T(8,128)(2,1)}, bf16[576,1152]{1,0:T(8,128)(2,1)}, bf16[576,1152]{1,0:T(8,128)(2,1)S(1)}, bf16[576,1152]{1,0:T(8,128)(2,1)S(1)}, f32[16,1152]{1,0:T(8,128)S(1)}) custom-call(bf16[256,1152]{1,0:T(8,128)(2,1)S(1)} %get-tuple-element.136.refs_0_, bf16[256,1152]{1,0:T(8,128)(2,1)S(1)} %get-tuple-element.120.refs_0_.refs_1_, ...), custom_call_target="tpu_custom_call" | custom-call | tf_op jit(solution)/shard_map/attend_weights/pallas_call | solution.py:189
  66.8 10.1 %collective-permute-done.9.refs_1_ = bf16[256,1152]{1,0:T(8,128)(2,1)} collective-permute-done((bf16[256,1152]{1,0:T(8,128)(2,1)S(1)}, bf16[256,1152]{1,0:T(8,128)(2,1)}, u32[]{:S(2)}, u32[]{:S(2)}) %collective-permute-start.9) | collective-permute-done | bytes 589856 | tf_op jit(solution)/shard_map/ppermute | solution.py:540
  80.0 4.5 %all-to-all-start.1 = ((bf16[16,16,1152]{2,1,0:T(8,128)(2,1)}), bf16[16,16,1152]{2,1,0:T(8,128)(2,1)}, u32[]{:S(2)}, u32[]{:S(2)}) async-start(bf16[16,16,1152]{2,1,0:T(8,128)(2,1)} %bitcast.20), calls=%async_computation.1 | async-start | bytes 1179648 | tf_op jit(solution)/shard_map/all_to_all | solution.py:544
  87.7 11.6 %mlp_weights.1 = (bf16[576,768]{1,0:T(8,128)(2,1)}, bf16[576,384]{1,0:T(8,128)(2,1)}, bf16[576,768]{1,0:T(8,128)(2,1)S(1)}, bf16[576,384]{1,0:T(8,128)(2,1)S(1)}) custom-call(bf16[256,1152]{1,0:T(8,128)(2,1)S(1)} %copy-done.14, bf16[256,1152]{1,0:T(8,128)(2,1)} %collective-permute-done.9.refs_1_, bf16[256,1152]{1,0:T(8,128)(2,1)} %collective-permute-done.10.refs_2_, ...), custom_call_target="tpu_custom_call" | custom-call | tf_op jit(solution)/shard_map/mlp_weights/pallas_call | solution.py:189
  100.8 3.0 %collective-permute-done.7.refs_0_ = bf16[608,1152]{1,0:T(8,128)(2,1)} collective-permute-done((bf16[608,1152]{1,0:T(8,128)(2,1)}, bf16[608,1152]{1,0:T(8,128)(2,1)}, u32[]{:S(2)}, u32[]{:S(2)}) %collective-permute-start.7) | collective-permute-done | bytes 1400864 | tf_op jit(solution)/shard_map/ppermute | solution.py:540
  103.8 2.7 %turn.8 = (bf16[320,1152]{1,0:T(8,128)(2,1)}, f32[288,1152]{1,0:T(8,128)S(1)}, f32[16,1152]{1,0:T(8,128)S(1)}) custom-call(bf16[608,1152]{1,0:T(8,128)(2,1)} %collective-permute-done.7.refs_0_, bf16[576,1152]{1,0:T(8,128)(2,1)S(1)} %copy-done.8, f32[16,1152]{1,0:T(8,128)S(1)} %get-tuple-element.161.refs_2_), custom_call_target="tpu_custom_call" | custom-call | tf_op jit(solution)/shard_map/turn/pallas_call | solution.py:189
  108.2 7.3 %collective-permute-done.16.refs_0_ = bf16[576,1152]{1,0:T(8,128)(2,1)} collective-permute-done((bf16[576,1152]{1,0:T(8,128)(2,1)}, bf16[576,1152]{1,0:T(8,128)(2,1)}, u32[]{:S(2)}, u32[]{:S(2)}) %collective-permute-start.16) | collective-permute-done | bytes 1327136 | tf_op jit(solution)/shard_map/ppermute | solution.py:540
  115.5 2.4 %turn.9 = (bf16[288,1152]{1,0:T(8,128)(2,1)}, f32[288,1152]{1,0:T(8,128)S(1)}) custom-call(bf16[576,1152]{1,0:T(8,128)(2,1)} %collective-permute-done.16.refs_0_, bf16[576,1152]{1,0:T(8,128)(2,1)S(1)} %copy-done.2), custom_call_target="tpu_custom_call" | custom-call | tf_op jit(solution)/shard_map/turn/pallas_call | solution.py:189
  119.3 5.0 %collective-permute-done.15.refs_0_ = bf16[576,768]{1,0:T(8,128)(2,1)} collective-permute-done((bf16[576,768]{1,0:T(8,128)(2,1)}, bf16[576,768]{1,0:T(8,128)(2,1)}, u32[]{:S(2)}, u32[]{:S(2)}) %collective-permute-start.15) | collective-permute-done | bytes 884768 | tf_op jit(solution)/shard_map/ppermute | solution.py:540
  125.7 6.0 %collective-permute-done.14.refs_0_ = bf16[320,1152]{1,0:T(8,128)(2,1)} collective-permute-done((bf16[320,1152]{1,0:T(8,128)(2,1)}, bf16[320,1152]{1,0:T(8,128)(2,1)}, u32[]{:S(2)}, u32[]{:S(2)}) %collective-permute-start.14) | collective-permute-done | bytes 737312 | tf_op jit(solution)/shard_map/ppermute | solution.py:540
  135.2 2.6 %collective-permute-done.19.refs_0_ = bf16[288,1152]{1,0:T(8,128)(2,1)} collective-permute-done((bf16[288,1152]{1,0:T(8,128)(2,1)}, bf16[288,1152]{1,0:T(8,128)(2,1)}, u32[]{:S(2)}, u32[]{:S(2)}) %collective-permute-start.19) | collective-permute-done | bytes 663584 | tf_op jit(solution)/shard_map/ppermute | solution.py:540
  143.2 10.4 %collective-permute-done.17.refs_0_ = bf16[176,1152]{1,0:T(8,128)(2,1)S(1)} collective-permute-done((bf16[176,1152]{1,0:T(8,128)(2,1)S(1)}, bf16[176,1152]{1,0:T(8,128)(2,1)S(1)}, u32[]{:S(2)}, u32[]{:S(2)}) %collective-permute-start.17) | collective-permute-done | bytes 405536 | tf_op jit(solution)/shard_map/ppermute | solution.py:540
  153.8 5.7 %collective-permute-done.23.refs_0_ = bf16[288,768]{1,0:T(8,128)(2,1)S(1)} collective-permute-done((bf16[288,768]{1,0:T(8,128)(2,1)S(1)}, bf16[288,768]{1,0:T(8,128)(2,1)S(1)}, u32[]{:S(2)}, u32[]{:S(2)}) %collective-permute-start.23) | collective-permute-done | bytes 442400 | tf_op jit(solution)/shard_map/ppermute | solution.py:540
  160.9 9.8 %collective-permute-done.21.refs_0_ = bf16[144,1152]{1,0:T(8,128)(2,1)S(1)} collective-permute-done((bf16[144,1152]{1,0:T(8,128)(2,1)S(1)}, bf16[144,1152]{1,0:T(8,128)(2,1)S(1)}, u32[]{:S(2)}, u32[]{:S(2)}) %collective-permute-start.21) | collective-permute-done | bytes 331808 | tf_op jit(solution)/shard_map/ppermute | solution.py:540
  170.8 2.2 %collective-permute-start.22 = (bf16[72,1152]{1,0:T(8,128)(2,1)S(1)}, bf16[72,1152]{1,0:T(8,128)(2,1)S(1)}, u32[]{:S(2)}, u32[]{:S(2)}) collective-permute-start(bf16[72,1152]{1,0:T(8,128)(2,1)S(1)} %get-tuple-element.195), channel_id=1, source_target_pairs={{0,16},{2,18},{4,20},{6,22},{8,24},{10,26},{12,28},{14,30},{16,0},... | collective-permute-start | bytes 497672 | tf_op jit(solution)/shard_map/ppermute | solution.py:540
  173.0 2.4 %home.1 = (bf16[128,1152]{1,0:T(8,128)(2,1)}, bf16[128,1152]{1,0:T(8,128)(2,1)}) custom-call(s32[1,64]{1,0:T(1,128)S(1)} %bitcast.34, bf16[256,1152]{1,0:T(8,128)(2,1)} %bitcast.11.refs_1_, bf16[256,1152]{1,0:T(8,128)(2,1)S(1)} %collective-permute-done.6.refs_2_, s32[1,64]{1,0:T(1,128)S(1)} %bitcast.38), custom_call_target="tpu_custom_call" | custom-call | tf_op jit(solution)/shard_map/home/pallas_call | solution.py:189
  175.4 4.9 %collective-permute-done.27.refs_3_ = bf16[72,1152]{1,0:T(8,128)(2,1)S(1)} collective-permute-done((bf16[72,1152]{1,0:T(8,128)(2,1)S(1)}, bf16[72,1152]{1,0:T(8,128)(2,1)S(1)}, u32[]{:S(2)}, u32[]{:S(2)}) %collective-permute-start.27) | collective-permute-done | bytes 165920 | tf_op jit(solution)/shard_map/ppermute | solution.py:540
  (148 shorter events, 42.4 us)
Async XLA Ops:
  3.1 24.6 %all-to-all-start = ((bf16[16,16,1152]{2,1,0:T(8,128)(2,1)}), bf16[16,16,1152]{2,1,0:T(8,128)(2,1)S(1)}, u32[]{:S(2)}, u32[]{:S(2)}) async-start(bf16[16,16,1152]{2,1,0:T(8,128)(2,1)} %bitcast.39), calls=%async_computation | async-start | bytes 1179648 | tf_op jit(solution)/shard_map/all_to_all | solution.py:544
  47.0 4.1 %collective-permute-start.2 = (bf16[256,1152]{1,0:T(8,128)(2,1)S(1)}, bf16[256,1152]{1,0:T(8,128)(2,1)S(1)}, u32[]{:S(2)}, u32[]{:S(2)}) collective-permute-start(bf16[256,1152]{1,0:T(8,128)(2,1)S(1)} %get-tuple-element.125.refs_2_.refs_4_), channel_id=1, source_target_pairs={{0,1},{1,0},{2,3},{3,2},{4,5},{5,4},{6,7},{7,6},{8,9},{9,8},{10,11... | collective-permute-start | bytes 1769480 | tf_op jit(solution)/shard_map/ppermute | solution.py:536
  47.6 19.2 %collective-permute-start.8 = (bf16[256,1152]{1,0:T(8,128)(2,1)S(1)}, bf16[256,1152]{1,0:T(8,128)(2,1)S(1)}, u32[]{:S(2)}, u32[]{:S(2)}) collective-permute-start(bf16[256,1152]{1,0:T(8,128)(2,1)S(1)} %get-tuple-element.150), channel_id=1, source_target_pairs={{0,8},{2,10},{4,12},{6,14},{8,0},{10,2},{12,4},{14,6},{16,24},{18,... | collective-permute-start | bytes 1769480 | tf_op jit(solution)/shard_map/ppermute | solution.py:540
  49.1 27.8 %collective-permute-start.9 = (bf16[256,1152]{1,0:T(8,128)(2,1)S(1)}, bf16[256,1152]{1,0:T(8,128)(2,1)}, u32[]{:S(2)}, u32[]{:S(2)}) collective-permute-start(bf16[256,1152]{1,0:T(8,128)(2,1)S(1)} %get-tuple-element.150), channel_id=1, source_target_pairs={{0,4},{2,6},{4,0},{6,2},{8,12},{10,14},{12,8},{14,10},{16,20},{18,... | collective-permute-start | bytes 1769480 | tf_op jit(solution)/shard_map/ppermute | solution.py:540
  50.0 26.9 %collective-permute-start.10 = (bf16[256,1152]{1,0:T(8,128)(2,1)S(1)}, bf16[256,1152]{1,0:T(8,128)(2,1)}, u32[]{:S(2)}, u32[]{:S(2)}) collective-permute-start(bf16[256,1152]{1,0:T(8,128)(2,1)S(1)} %get-tuple-element.150), channel_id=1, source_target_pairs={{0,12},{2,14},{4,8},{6,10},{8,4},{10,6},{12,0},{14,2},{16,28},{18,... | collective-permute-start | bytes 1769480 | tf_op jit(solution)/shard_map/ppermute | solution.py:540
  65.2 38.6 %collective-permute-start.7 = (bf16[608,1152]{1,0:T(8,128)(2,1)}, bf16[608,1152]{1,0:T(8,128)(2,1)}, u32[]{:S(2)}, u32[]{:S(2)}) collective-permute-start(bf16[608,1152]{1,0:T(8,128)(2,1)} %get-tuple-element.149), channel_id=1, source_target_pairs={{0,2},{2,0},{4,6},{6,4},{8,10},{10,8},{12,14},{14,12},{16,18},{18,... | collective-permute-start | bytes 4202504 | tf_op jit(solution)/shard_map/ppermute | solution.py:540
  77.7 37.8 %collective-permute-start.16 = (bf16[576,1152]{1,0:T(8,128)(2,1)}, bf16[576,1152]{1,0:T(8,128)(2,1)}, u32[]{:S(2)}, u32[]{:S(2)}) collective-permute-start(bf16[576,1152]{1,0:T(8,128)(2,1)} %get-tuple-element.166), channel_id=1, source_target_pairs={{0,4},{2,6},{4,0},{6,2},{8,12},{10,14},{12,8},{14,10},{16,20},{18,... | collective-permute-start | bytes 3981320 | tf_op jit(solution)/shard_map/ppermute | solution.py:540
  78.7 5.8 %collective-permute-start.12 = (bf16[256,1152]{1,0:T(8,128)(2,1)}, bf16[256,1152]{1,0:T(8,128)(2,1)}, u32[]{:S(2)}, u32[]{:S(2)}) collective-permute-start(bf16[256,1152]{1,0:T(8,128)(2,1)} %collective-permute-done.9.refs_1_), channel_id=1, source_target_pairs={{0,1},{1,0},{2,3},{3,2},{4,5},{5,4},{6,7},{7,6},{8,9},{9,8},{10,11... | collective-permute-start | bytes 1769480 | tf_op jit(solution)/shard_map/ppermute | solution.py:536
  79.7 4.8 %collective-permute-start.13 = (bf16[256,1152]{1,0:T(8,128)(2,1)}, bf16[256,1152]{1,0:T(8,128)(2,1)}, u32[]{:S(2)}, u32[]{:S(2)}) collective-permute-start(bf16[256,1152]{1,0:T(8,128)(2,1)} %collective-permute-done.10.refs_2_), channel_id=1, source_target_pairs={{0,1},{1,0},{2,3},{3,2},{4,5},{5,4},{6,7},{7,6},{8,9},{9,8},{10,11... | collective-permute-start | bytes 1769480 | tf_op jit(solution)/shard_map/ppermute | solution.py:536
  80.0 39.3 %all-to-all-start.1 = ((bf16[16,16,1152]{2,1,0:T(8,128)(2,1)}), bf16[16,16,1152]{2,1,0:T(8,128)(2,1)}, u32[]{:S(2)}, u32[]{:S(2)}) async-start(bf16[16,16,1152]{2,1,0:T(8,128)(2,1)} %bitcast.20), calls=%async_computation.1 | async-start | bytes 1179648 | tf_op jit(solution)/shard_map/all_to_all | solution.py:544
  99.3 25.0 %collective-permute-start.15 = (bf16[576,768]{1,0:T(8,128)(2,1)}, bf16[576,768]{1,0:T(8,128)(2,1)}, u32[]{:S(2)}, u32[]{:S(2)}) collective-permute-start(bf16[576,768]{1,0:T(8,128)(2,1)} %get-tuple-element.164), channel_id=1, source_target_pairs={{0,2},{2,0},{4,6},{6,4},{8,10},{10,8},{12,14},{14,12},{16,18},{18,... | collective-permute-start | bytes 2654216 | tf_op jit(solution)/shard_map/ppermute | solution.py:540
  107.1 24.6 %collective-permute-start.14 = (bf16[320,1152]{1,0:T(8,128)(2,1)}, bf16[320,1152]{1,0:T(8,128)(2,1)}, u32[]{:S(2)}, u32[]{:S(2)}) collective-permute-start(bf16[320,1152]{1,0:T(8,128)(2,1)} %get-tuple-element.163), channel_id=1, source_target_pairs={{0,4},{2,6},{4,0},{6,2},{8,12},{10,14},{12,8},{14,10},{16,20},{18,... | collective-permute-start | bytes 2211848 | tf_op jit(solution)/shard_map/ppermute | solution.py:540
  117.9 19.8 %collective-permute-start.19 = (bf16[288,1152]{1,0:T(8,128)(2,1)}, bf16[288,1152]{1,0:T(8,128)(2,1)}, u32[]{:S(2)}, u32[]{:S(2)}) collective-permute-start(bf16[288,1152]{1,0:T(8,128)(2,1)} %get-tuple-element.180), channel_id=1, source_target_pairs={{0,2},{2,0},{4,6},{6,4},{8,10},{10,8},{12,14},{14,12},{16,18},{18,... | collective-permute-start | bytes 1990664 | tf_op jit(solution)/shard_map/ppermute | solution.py:540
  118.5 22.1 %collective-permute-start.18 = (bf16[576,384]{1,0:T(8,128)(2,1)}, bf16[576,384]{1,0:T(8,128)(2,1)}, u32[]{:S(2)}, u32[]{:S(2)}) collective-permute-start(bf16[576,384]{1,0:T(8,128)(2,1)} %get-tuple-element.179), channel_id=1, source_target_pairs={{0,16},{2,18},{4,20},{6,22},{8,24},{10,26},{12,28},{14,30},{16,0},... | collective-permute-start | bytes 1327112 | tf_op jit(solution)/shard_map/ppermute | solution.py:540
  119.3 51.5 %collective-permute-start.6 = (bf16[256,1152]{1,0:T(8,128)(2,1)}, bf16[256,1152]{1,0:T(8,128)(2,1)S(1)}, u32[]{:S(2)}, u32[]{:S(2)}) collective-permute-start(bf16[256,1152]{1,0:T(8,128)(2,1)} %bitcast.11.refs_1_), channel_id=1, source_target_pairs={{0,1},{1,0},{2,3},{3,2},{4,5},{5,4},{6,7},{7,6},{8,9},{9,8},{10,11... | collective-permute-start | bytes 1769480 | tf_op jit(solution)/shard_map/ppermute | solution.py:536
  133.0 20.6 %collective-permute-start.17 = (bf16[176,1152]{1,0:T(8,128)(2,1)S(1)}, bf16[176,1152]{1,0:T(8,128)(2,1)S(1)}, u32[]{:S(2)}, u32[]{:S(2)}) collective-permute-start(bf16[176,1152]{1,0:T(8,128)(2,1)S(1)} %get-tuple-element.177), channel_id=1, source_target_pairs={{0,8},{2,10},{4,12},{6,14},{8,0},{10,2},{12,4},{14,6},{16,24},{18,... | collective-permute-start | bytes 1216520 | tf_op jit(solution)/shard_map/ppermute | solution.py:540
  133.7 25.8 %collective-permute-start.23 = (bf16[288,768]{1,0:T(8,128)(2,1)S(1)}, bf16[288,768]{1,0:T(8,128)(2,1)S(1)}, u32[]{:S(2)}, u32[]{:S(2)}) collective-permute-start(bf16[288,768]{1,0:T(8,128)(2,1)S(1)} %get-tuple-element.209), channel_id=1, source_target_pairs={{0,16},{2,18},{4,20},{6,22},{8,24},{10,26},{12,28},{14,30},{16,0},... | collective-permute-start | bytes 1327112 | tf_op jit(solution)/shard_map/ppermute | solution.py:540
  138.9 31.8 %collective-permute-start.21 = (bf16[144,1152]{1,0:T(8,128)(2,1)S(1)}, bf16[144,1152]{1,0:T(8,128)(2,1)S(1)}, u32[]{:S(2)}, u32[]{:S(2)}) collective-permute-start(bf16[144,1152]{1,0:T(8,128)(2,1)S(1)} %get-tuple-element.191), channel_id=1, source_target_pairs={{0,8},{2,10},{4,12},{6,14},{8,0},{10,2},{12,4},{14,6},{16,24},{18,... | collective-permute-start | bytes 995336 | tf_op jit(solution)/shard_map/ppermute | solution.py:540
  141.7 12.1 %collective-permute-start.24 = (bf16[288,384]{1,0:T(8,128)(2,1)S(1)}, bf16[288,384]{1,0:T(8,128)(2,1)S(1)}, u32[]{:S(2)}, u32[]{:S(2)}) collective-permute-start(bf16[288,384]{1,0:T(8,128)(2,1)S(1)} %get-tuple-element.210), channel_id=1, source_target_pairs={{0,2},{2,0},{4,6},{6,4},{8,10},{10,8},{12,14},{14,12},{16,18},{18,... | collective-permute-start | bytes 663560 | tf_op jit(solution)/shard_map/ppermute | solution.py:540
  153.7 28.2 %collective-permute-start.20 = (bf16[104,1152]{1,0:T(8,128)(2,1)S(1)}, bf16[104,1152]{1,0:T(8,128)(2,1)S(1)}, u32[]{:S(2)}, u32[]{:S(2)}) collective-permute-start(bf16[104,1152]{1,0:T(8,128)(2,1)S(1)} %get-tuple-element.190), channel_id=1, source_target_pairs={{0,16},{2,18},{4,20},{6,22},{8,24},{10,26},{12,28},{14,30},{16,0},... | collective-permute-start | bytes 718856 | tf_op jit(solution)/shard_map/ppermute | solution.py:540
  159.7 15.8 %collective-permute-start.25 = (bf16[72,1152]{1,0:T(8,128)(2,1)S(1)}, bf16[72,1152]{1,0:T(8,128)(2,1)S(1)}, u32[]{:S(2)}, u32[]{:S(2)}) collective-permute-start(bf16[72,1152]{1,0:T(8,128)(2,1)S(1)} %get-tuple-element.212), channel_id=1, source_target_pairs={{0,8},{2,10},{4,12},{6,14},{8,0},{10,2},{12,4},{14,6},{16,24},{18,... | collective-permute-start | bytes 497672 | tf_op jit(solution)/shard_map/ppermute | solution.py:540
  159.7 15.7 %collective-permute-start.26 = (bf16[72,1152]{1,0:T(8,128)(2,1)S(1)}, bf16[72,1152]{1,0:T(8,128)(2,1)S(1)}, u32[]{:S(2)}, u32[]{:S(2)}) collective-permute-start(bf16[72,1152]{1,0:T(8,128)(2,1)S(1)} %get-tuple-element.213), channel_id=1, source_target_pairs={{0,4},{2,6},{4,0},{6,2},{8,12},{10,14},{12,8},{14,10},{16,20},{18,... | collective-permute-start | bytes 497672 | tf_op jit(solution)/shard_map/ppermute | solution.py:540
  170.7 9.7 %collective-permute-start.27 = (bf16[72,1152]{1,0:T(8,128)(2,1)S(1)}, bf16[72,1152]{1,0:T(8,128)(2,1)S(1)}, u32[]{:S(2)}, u32[]{:S(2)}) collective-permute-start(bf16[72,1152]{1,0:T(8,128)(2,1)S(1)} %get-tuple-element.214), channel_id=1, source_target_pairs={{0,12},{2,14},{4,8},{6,10},{8,4},{10,6},{12,0},{14,2},{16,28},{18,... | collective-permute-start | bytes 497672 | tf_op jit(solution)/shard_map/ppermute | solution.py:540
  170.8 11.1 %collective-permute-start.22 = (bf16[72,1152]{1,0:T(8,128)(2,1)S(1)}, bf16[72,1152]{1,0:T(8,128)(2,1)S(1)}, u32[]{:S(2)}, u32[]{:S(2)}) collective-permute-start(bf16[72,1152]{1,0:T(8,128)(2,1)S(1)} %get-tuple-element.195), channel_id=1, source_target_pairs={{0,16},{2,18},{4,20},{6,22},{8,24},{10,26},{12,28},{14,30},{16,0},... | collective-permute-start | bytes 497672 | tf_op jit(solution)/shard_map/ppermute | solution.py:540
  (44 other events, 327.9 us)

commit v6 on v5

--- a/solution.py
+++ b/solution.py
@@ -296,7 +296,7 @@
     start = pl.multiple_of(lax.axis_index(CORE) * half, half)
     made.halves[:half, :] = made.h2[pl.ds(start, half), :]
     made.halves[half:, :] = given.g[pl.ds(start, half), :]
-    step = 512
+    step = 1024
     full, done, rest = chunks_of(given.we.shape[0], step)
     out_total[...] = jnp.zeros_like(out_total)
     dh2_total[...] = jnp.zeros_like(dh2_total)
@@ -395,11 +395,18 @@
     for group, order in enumerate(orders):
         width = bounds[group + 1] - bounds[group]
         ordered_rows(left, h1_t, n_dev, order)
-        for i, cols, lanes in parts_between(bounds, group, heads_width, 4):
-            if i == 3:
+        parts = list(parts_between(bounds, group, heads_width, 4))
+        for shift in (False, True):
+            chosen = [part for part in parts if (part[0] == 3) == shift]
+            if not chosen:
+                continue
+            if shift:
                 ordered_rows(branch_left, branch_t, n_dev, order)
-            rows = (branch_left if i == 3 else left)[...].astype(bf16)
-            product = dot(rows, given.right[i][:, cols]).astype(bf16)
+            rows = (branch_left if shift else left)[...].astype(bf16)
+            right = [given.right[i][:, cols] for i, cols, _ in chosen]
+            right = jnp.concatenate(right, axis=1) if len(right) > 1 else right[0]
+            product = dot(rows, right).astype(bf16)
+            lanes = slice(chosen[0][2].start, chosen[-1][2].stop)
             made.keep[group][:, lanes] = product[:half, :]
             made.give[group][:half, lanes] = product[half:, :]
 
@@ -620,7 +627,7 @@
     others = list(range(2, n_bits - 2))
     attend_orders = (
         [0, 1] + others + [n_bits - 2, n_bits - 1],
-        [1, 0] + others + [n_bits - 2, n_bits - 1],
+        [n_bits - 2, 1, 0] + others + [n_bits - 1],
     )
     attend_bounds = (0, 1152, 4 * heads_width)
     wq, wk, wv, wo, we, wr = (
@@ -653,8 +660,9 @@
     we_part, wr_part = (
         lax.dynamic_slice_in_dim(jnp.pad(w, padding), at_share, part, 0) for w in (we, wr)
     )
-    got, we_part, wr_part = lax.optimization_barrier((spread(sent.send), we_part, wr_part))
-    arrived = dict(**sizes, mine=got, other=swap_cores(got))
+    got = spread(sent.send)
+    got_late, we_part, wr_part = lax.optimization_barrier((got, we_part, wr_part))
+    arrived = dict(**sizes, mine=got, other=swap_cores(got_late))
     came_in = call(
         at_place(arrive, vec), dict(**arrived, vec=vectors),
         dict(mask=((cap, cap), f32), x=wide16, h1=wide16, g=wide16), us=6,

time: 184 us -> 182 us (0.989)
    ppermute x18, waiting for transfers between devices: 65 us -> 61.1 us  [swap_dp(): lax.ppermute(values, DP, [(i, i ^ flip) for i in range(lax.axis_size(DP))])]
    all_to_all x2, waiting for transfers between devices: 14.2 us -> 16.2 us  [spread(): return lax.all_to_all(rows, DP, split_axis=0, concat_axis=0, tiled=True)]
  transfers between devices with their start and end apart: 30 -> 30, of which waited for: 16 -> 17; matrix products, arithmetic and copies ran while one was open for 1% -> 1% of each run, Pallas kernels for 21% -> 21%
where the time goes in v6:
time: 182 us
  waiting for transfers between devices  82.1 us (45%)
  Pallas kernels  55.3 us (30%)
  starting transfers between devices  32.6 us (18%)
  local copies, waits for them, and re-layouts  10.3 us (6%)
    ppermute x18, waiting for transfers between devices, swap_dp(): lax.ppermute(values, DP, [(i, i ^ flip) for i in range(lax.axis_size(DP))])  61.1 us
    pallas_call x22, Pallas kernels, call(): pl.pallas_call(kernel, name=getattr(body, 'func', body).__name__, out_sha...  55.3 us
    ppermute x18, starting transfers between devices, swap_dp(): lax.ppermute(values, DP, [(i, i ^ flip) for i in range(lax.axis_size(DP))])  18.2 us
    all_to_all x2, waiting for transfers between devices, spread(): return lax.all_to_all(rows, DP, split_axis=0, concat_axis=0, tiled=True)  16.2 us
    all_to_all x2, starting transfers between devices, spread(): return lax.all_to_all(rows, DP, split_axis=0, concat_axis=0, tiled=True)  12.8 us
    unnamed x84, local copies, waits for them, and re-layouts  8.35 us
    ppermute x10, waiting for transfers between devices, swap_cores(): return lax.ppermute(values, CORE, [(0, 1), (1, 0)])  4.75 us
  transfers between devices with their start and end apart: 30, of which 17 were waited for; matrix products, arithmetic and copies ran while one was open for 1% of the time, Pallas kernels for 21%

profile of v6, /device:TPU:0, one launch (start us, length us, event | category | flops | bytes accessed | tf_op | source)
XLA Modules:
  0.0 181.6 jit_solution(17908614908947730630)
XLA Ops:
  0.7 2.4 %pack.1 = bf16[256,1152]{1,0:T(8,128)(2,1)} custom-call(bf16[128,1152]{1,0:T(8,128)(2,1)} %refs_0_.1, s32[1,64]{1,0:T(1,128)} %bitcast.31, s32[1,64]{1,0:T(1,128)} %bitcast.35, bf16[128,1152]{1,0:T(8,128)(2,1)} %refs_3_.1), custom_call_target="tpu_custom_call" | custom-call | tf_op jit(solution)/shard_map/pack/pallas_call | solution.py:189
  3.1 8.3 %all-to-all-start = ((bf16[16,16,1152]{2,1,0:T(8,128)(2,1)}), bf16[16,16,1152]{2,1,0:T(8,128)(2,1)S(1)}, u32[]{:S(2)}, u32[]{:S(2)}) async-start(bf16[16,16,1152]{2,1,0:T(8,128)(2,1)} %bitcast.39), calls=%async_computation | async-start | bytes 1179648 | tf_op jit(solution)/shard_map/all_to_all | solution.py:551
  13.5 14.2 %all-to-all-done = bf16[16,16,1152]{2,1,0:T(8,128)(2,1)S(1)} async-done(((bf16[16,16,1152]{2,1,0:T(8,128)(2,1)}), bf16[16,16,1152]{2,1,0:T(8,128)(2,1)S(1)}, u32[]{:S(2)}, u32[]{:S(2)}) %all-to-all-start) | async-done | bytes 589856 | tf_op jit(solution)/shard_map/all_to_all | solution.py:551
  32.5 4.8 %attend.1 = (bf16[256,576]{1,0:T(8,128)(2,1)S(1)}, bf16[256,1152]{1,0:T(8,128)(2,1)S(1)}, bf16[256,576]{1,0:T(8,128)(2,1)S(1)}, f32[256,8]{1,0:T(8,128)S(1)}, bf...) custom-call(bf16[256,1152]{1,0:T(8,128)(2,1)S(1)} %get-tuple-element.120.refs_0_.refs_1_, ...), custom_call_target="tpu_custom_call" | custom-call | flops 5000000000 | bytes 5000000 | tf_op jit(solution)/shard_map/attend/pallas_call | solution.py:189
  39.4 7.4 %mlp.1 = (f32[1,2176]{1,0:T(1,128)S(1)}, bf16[256,1152]{1,0:T(8,128)(2,1)S(1)}, bf16[256,1152]{1,0:T(8,128)(2,1)S(1)}, f32[256,1152]{1,0:T(8,128)S(1)}, bf16[256...) custom-call(bf16[256,1152]{1,0:T(8,128)(2,1)S(1)} %get-tuple-element.122.refs_0_, ...), custom_call_target="tpu_custom_call" | custom-call | tf_op jit(solution)/shard_map/mlp/pallas_call | solution.py:189
  52.7 5.6 %attend_back.1 = (bf16[128,1152]{1,0:T(8,128)(2,1)S(1)}, bf16[128,1152]{1,0:T(8,128)(2,1)S(1)}, bf16[256,576]{1,0:T(8,128)(2,1)S(1)}, bf16[256,576]{1,0:T(8,128)...) custom-call(bf16[256,576]{1,0:T(8,128)(2,1)S(1)} %get-tuple-element.127.refs_0_, ...), custom_call_target="tpu_custom_call" | custom-call | tf_op jit(solution)/shard_map/attend_back/pallas_call | solution.py:189
  61.4 3.7 %attend_weights.1 = (bf16[608,1152]{1,0:T(8,128)(2,1)}, bf16[576,1152]{1,0:T(8,128)(2,1)}, bf16[576,1152]{1,0:T(8,128)(2,1)S(1)}, bf16[576,1152]{1,0:T(8,128)(2,1)S(1)}, f32[16,1152]{1,0:T(8,128)S(1)}) custom-call(bf16[256,1152]{1,0:T(8,128)(2,1)S(1)} %get-tuple-element.136.refs_0_, bf16[256,1152]{1,0:T(8,128)(2,1)S(1)} %get-tuple-element.120.refs_0_.refs_1_, ...), custom_call_target="tpu_custom_call" | custom-call | tf_op jit(solution)/shard_map/attend_weights/pallas_call | solution.py:189
  66.7 10.0 %collective-permute-done.9.refs_1_ = bf16[256,1152]{1,0:T(8,128)(2,1)} collective-permute-done((bf16[256,1152]{1,0:T(8,128)(2,1)S(1)}, bf16[256,1152]{1,0:T(8,128)(2,1)}, u32[]{:S(2)}, u32[]{:S(2)}) %collective-permute-start.9) | collective-permute-done | bytes 589856 | tf_op jit(solution)/shard_map/ppermute | solution.py:547
  79.7 4.5 %all-to-all-start.1 = ((bf16[16,16,1152]{2,1,0:T(8,128)(2,1)}), bf16[16,16,1152]{2,1,0:T(8,128)(2,1)}, u32[]{:S(2)}, u32[]{:S(2)}) async-start(bf16[16,16,1152]{2,1,0:T(8,128)(2,1)} %bitcast.20), calls=%async_computation.1 | async-start | bytes 1179648 | tf_op jit(solution)/shard_map/all_to_all | solution.py:551
  87.4 11.6 %mlp_weights.1 = (bf16[576,768]{1,0:T(8,128)(2,1)}, bf16[576,384]{1,0:T(8,128)(2,1)}, bf16[576,768]{1,0:T(8,128)(2,1)S(1)}, bf16[576,384]{1,0:T(8,128)(2,1)S(1)}) custom-call(bf16[256,1152]{1,0:T(8,128)(2,1)S(1)} %copy-done.14, bf16[256,1152]{1,0:T(8,128)(2,1)} %collective-permute-done.9.refs_1_, bf16[256,1152]{1,0:T(8,128)(2,1)} %collective-permute-done.10.refs_2_, ...), custom_call_target="tpu_custom_call" | custom-call | tf_op jit(solution)/shard_map/mlp_weights/pallas_call | solution.py:189
  100.5 2.7 %turn.8 = (bf16[320,1152]{1,0:T(8,128)(2,1)}, f32[288,1152]{1,0:T(8,128)S(1)}, f32[16,1152]{1,0:T(8,128)S(1)}) custom-call(bf16[608,1152]{1,0:T(8,128)(2,1)} %collective-permute-done.7.refs_0_, bf16[576,1152]{1,0:T(8,128)(2,1)S(1)} %copy-done.8, f32[16,1152]{1,0:T(8,128)S(1)} %get-tuple-element.161.refs_2_), custom_call_target="tpu_custom_call" | custom-call | tf_op jit(solution)/shard_map/turn/pallas_call | solution.py:189
  105.3 10.6 %collective-permute-done.16.refs_0_ = bf16[576,1152]{1,0:T(8,128)(2,1)} collective-permute-done((bf16[576,1152]{1,0:T(8,128)(2,1)}, bf16[576,1152]{1,0:T(8,128)(2,1)}, u32[]{:S(2)}, u32[]{:S(2)}) %collective-permute-start.16) | collective-permute-done | bytes 1327136 | tf_op jit(solution)/shard_map/ppermute | solution.py:547
  115.8 2.4 %turn.9 = (bf16[288,1152]{1,0:T(8,128)(2,1)}, f32[288,1152]{1,0:T(8,128)S(1)}) custom-call(bf16[576,1152]{1,0:T(8,128)(2,1)} %collective-permute-done.16.refs_0_, bf16[576,1152]{1,0:T(8,128)(2,1)S(1)} %copy-done.2), custom_call_target="tpu_custom_call" | custom-call | tf_op jit(solution)/shard_map/turn/pallas_call | solution.py:189
  118.3 2.0 %all-to-all-done.1 = bf16[16,16,1152]{2,1,0:T(8,128)(2,1)} async-done(((bf16[16,16,1152]{2,1,0:T(8,128)(2,1)}), bf16[16,16,1152]{2,1,0:T(8,128)(2,1)}, u32[]{:S(2)}, u32[]{:S(2)}) %all-to-all-start.1) | async-done | bytes 589856 | tf_op jit(solution)/shard_map/all_to_all | solution.py:551
  120.3 4.1 %collective-permute-done.15.refs_0_ = bf16[576,768]{1,0:T(8,128)(2,1)} collective-permute-done((bf16[576,768]{1,0:T(8,128)(2,1)}, bf16[576,768]{1,0:T(8,128)(2,1)}, u32[]{:S(2)}, u32[]{:S(2)}) %collective-permute-start.15) | collective-permute-done | bytes 884768 | tf_op jit(solution)/shard_map/ppermute | solution.py:547
  129.5 2.4 %collective-permute-start.23 = (bf16[288,768]{1,0:T(8,128)(2,1)S(1)}, bf16[288,768]{1,0:T(8,128)(2,1)S(1)}, u32[]{:S(2)}, u32[]{:S(2)}) collective-permute-start(bf16[288,768]{1,0:T(8,128)(2,1)S(1)} %get-tuple-element.209), channel_id=1, source_target_pairs={{0,16},{2,18},{4,20},{6,22},{8,24},{10,26},{12,28},{14,30},{16,0},... | collective-permute-start | bytes 1327112 | tf_op jit(solution)/shard_map/ppermute | solution.py:547
  131.9 7.8 %collective-permute-done.19.refs_0_ = bf16[288,1152]{1,0:T(8,128)(2,1)} collective-permute-done((bf16[288,1152]{1,0:T(8,128)(2,1)}, bf16[288,1152]{1,0:T(8,128)(2,1)}, u32[]{:S(2)}, u32[]{:S(2)}) %collective-permute-start.19) | collective-permute-done | bytes 663584 | tf_op jit(solution)/shard_map/ppermute | solution.py:547
  144.2 3.8 %collective-permute-done.17.refs_0_ = bf16[176,1152]{1,0:T(8,128)(2,1)S(1)} collective-permute-done((bf16[176,1152]{1,0:T(8,128)(2,1)S(1)}, bf16[176,1152]{1,0:T(8,128)(2,1)S(1)}, u32[]{:S(2)}, u32[]{:S(2)}) %collective-permute-start.17) | collective-permute-done | bytes 405536 | tf_op jit(solution)/shard_map/ppermute | solution.py:547
  148.1 6.2 %collective-permute-done.24.refs_1_ = bf16[288,384]{1,0:T(8,128)(2,1)S(1)} collective-permute-done((bf16[288,384]{1,0:T(8,128)(2,1)S(1)}, bf16[288,384]{1,0:T(8,128)(2,1)S(1)}, u32[]{:S(2)}, u32[]{:S(2)}) %collective-permute-start.24) | collective-permute-done | bytes 221216 | tf_op jit(solution)/shard_map/ppermute | solution.py:547
  154.3 8.3 %collective-permute-done.23.refs_0_ = bf16[288,768]{1,0:T(8,128)(2,1)S(1)} collective-permute-done((bf16[288,768]{1,0:T(8,128)(2,1)S(1)}, bf16[288,768]{1,0:T(8,128)(2,1)S(1)}, u32[]{:S(2)}, u32[]{:S(2)}) %collective-permute-start.23) | collective-permute-done | bytes 442400 | tf_op jit(solution)/shard_map/ppermute | solution.py:547
  164.2 2.1 %collective-permute-start.27 = (bf16[72,1152]{1,0:T(8,128)(2,1)S(1)}, bf16[72,1152]{1,0:T(8,128)(2,1)S(1)}, u32[]{:S(2)}, u32[]{:S(2)}) collective-permute-start(bf16[72,1152]{1,0:T(8,128)(2,1)S(1)} %get-tuple-element.214), channel_id=1, source_target_pairs={{0,12},{2,14},{4,8},{6,10},{8,4},{10,6},{12,0},{14,2},{16,28},{18,... | collective-permute-start | bytes 497672 | tf_op jit(solution)/shard_map/ppermute | solution.py:547
  167.1 2.4 %home.1 = (bf16[128,1152]{1,0:T(8,128)(2,1)}, bf16[128,1152]{1,0:T(8,128)(2,1)}) custom-call(s32[1,64]{1,0:T(1,128)S(1)} %bitcast.34, bf16[256,1152]{1,0:T(8,128)(2,1)} %bitcast.11.refs_1_, bf16[256,1152]{1,0:T(8,128)(2,1)S(1)} %collective-permute-done.6.refs_2_, s32[1,64]{1,0:T(1,128)S(1)} %bitcast.38), custom_call_target="tpu_custom_call" | custom-call | tf_op jit(solution)/shard_map/home/pallas_call | solution.py:189
  169.6 5.2 %collective-permute-done.25.refs_1_ = bf16[72,1152]{1,0:T(8,128)(2,1)S(1)} collective-permute-done((bf16[72,1152]{1,0:T(8,128)(2,1)S(1)}, bf16[72,1152]{1,0:T(8,128)(2,1)S(1)}, u32[]{:S(2)}, u32[]{:S(2)}) %collective-permute-start.25) | collective-permute-done | bytes 165920 | tf_op jit(solution)/shard_map/ppermute | solution.py:547
  174.8 4.2 %collective-permute-done.27.refs_3_ = bf16[72,1152]{1,0:T(8,128)(2,1)S(1)} collective-permute-done((bf16[72,1152]{1,0:T(8,128)(2,1)S(1)}, bf16[72,1152]{1,0:T(8,128)(2,1)S(1)}, u32[]{:S(2)}, u32[]{:S(2)}) %collective-permute-start.27) | collective-permute-done | bytes 165920 | tf_op jit(solution)/shard_map/ppermute | solution.py:547
  (148 shorter events, 43.6 us)
Async XLA Ops:
  3.1 24.6 %all-to-all-start = ((bf16[16,16,1152]{2,1,0:T(8,128)(2,1)}), bf16[16,16,1152]{2,1,0:T(8,128)(2,1)S(1)}, u32[]{:S(2)}, u32[]{:S(2)}) async-start(bf16[16,16,1152]{2,1,0:T(8,128)(2,1)} %bitcast.39), calls=%async_computation | async-start | bytes 1179648 | tf_op jit(solution)/shard_map/all_to_all | solution.py:551
  46.9 4.1 %collective-permute-start.2 = (bf16[256,1152]{1,0:T(8,128)(2,1)S(1)}, bf16[256,1152]{1,0:T(8,128)(2,1)S(1)}, u32[]{:S(2)}, u32[]{:S(2)}) collective-permute-start(bf16[256,1152]{1,0:T(8,128)(2,1)S(1)} %get-tuple-element.125.refs_2_.refs_4_), channel_id=1, source_target_pairs={{0,1},{1,0},{2,3},{3,2},{4,5},{5,4},{6,7},{7,6},{8,9},{9,8},{10,11... | collective-permute-start | bytes 1769480 | tf_op jit(solution)/shard_map/ppermute | solution.py:543
  47.4 19.3 %collective-permute-start.8 = (bf16[256,1152]{1,0:T(8,128)(2,1)S(1)}, bf16[256,1152]{1,0:T(8,128)(2,1)S(1)}, u32[]{:S(2)}, u32[]{:S(2)}) collective-permute-start(bf16[256,1152]{1,0:T(8,128)(2,1)S(1)} %get-tuple-element.150), channel_id=1, source_target_pairs={{0,8},{2,10},{4,12},{6,14},{8,0},{10,2},{12,4},{14,6},{16,24},{18,... | collective-permute-start | bytes 1769480 | tf_op jit(solution)/shard_map/ppermute | solution.py:547
  48.9 27.8 %collective-permute-start.9 = (bf16[256,1152]{1,0:T(8,128)(2,1)S(1)}, bf16[256,1152]{1,0:T(8,128)(2,1)}, u32[]{:S(2)}, u32[]{:S(2)}) collective-permute-start(bf16[256,1152]{1,0:T(8,128)(2,1)S(1)} %get-tuple-element.150), channel_id=1, source_target_pairs={{0,4},{2,6},{4,0},{6,2},{8,12},{10,14},{12,8},{14,10},{16,20},{18,... | collective-permute-start | bytes 1769480 | tf_op jit(solution)/shard_map/ppermute | solution.py:547
  49.9 26.9 %collective-permute-start.10 = (bf16[256,1152]{1,0:T(8,128)(2,1)S(1)}, bf16[256,1152]{1,0:T(8,128)(2,1)}, u32[]{:S(2)}, u32[]{:S(2)}) collective-permute-start(bf16[256,1152]{1,0:T(8,128)(2,1)S(1)} %get-tuple-element.150), channel_id=1, source_target_pairs={{0,12},{2,14},{4,8},{6,10},{8,4},{10,6},{12,0},{14,2},{16,28},{18,... | collective-permute-start | bytes 1769480 | tf_op jit(solution)/shard_map/ppermute | solution.py:547
  65.1 35.4 %collective-permute-start.7 = (bf16[608,1152]{1,0:T(8,128)(2,1)}, bf16[608,1152]{1,0:T(8,128)(2,1)}, u32[]{:S(2)}, u32[]{:S(2)}) collective-permute-start(bf16[608,1152]{1,0:T(8,128)(2,1)} %get-tuple-element.149), channel_id=1, source_target_pairs={{0,2},{2,0},{4,6},{6,4},{8,10},{10,8},{12,14},{14,12},{16,18},{18,... | collective-permute-start | bytes 4202504 | tf_op jit(solution)/shard_map/ppermute | solution.py:547
  77.5 38.3 %collective-permute-start.16 = (bf16[576,1152]{1,0:T(8,128)(2,1)}, bf16[576,1152]{1,0:T(8,128)(2,1)}, u32[]{:S(2)}, u32[]{:S(2)}) collective-permute-start(bf16[576,1152]{1,0:T(8,128)(2,1)} %get-tuple-element.166), channel_id=1, source_target_pairs={{0,8},{2,10},{4,12},{6,14},{8,0},{10,2},{12,4},{14,6},{16,24},{18,... | collective-permute-start | bytes 3981320 | tf_op jit(solution)/shard_map/ppermute | solution.py:547
  78.2 6.0 %collective-permute-start.12 = (bf16[256,1152]{1,0:T(8,128)(2,1)}, bf16[256,1152]{1,0:T(8,128)(2,1)}, u32[]{:S(2)}, u32[]{:S(2)}) collective-permute-start(bf16[256,1152]{1,0:T(8,128)(2,1)} %collective-permute-done.9.refs_1_), channel_id=1, source_target_pairs={{0,1},{1,0},{2,3},{3,2},{4,5},{5,4},{6,7},{7,6},{8,9},{9,8},{10,11... | collective-permute-start | bytes 1769480 | tf_op jit(solution)/shard_map/ppermute | solution.py:543
  79.6 4.6 %collective-permute-start.13 = (bf16[256,1152]{1,0:T(8,128)(2,1)}, bf16[256,1152]{1,0:T(8,128)(2,1)}, u32[]{:S(2)}, u32[]{:S(2)}) collective-permute-start(bf16[256,1152]{1,0:T(8,128)(2,1)} %collective-permute-done.10.refs_2_), channel_id=1, source_target_pairs={{0,1},{1,0},{2,3},{3,2},{4,5},{5,4},{6,7},{7,6},{8,9},{9,8},{10,11... | collective-permute-start | bytes 1769480 | tf_op jit(solution)/shard_map/ppermute | solution.py:543
  79.7 40.6 %all-to-all-start.1 = ((bf16[16,16,1152]{2,1,0:T(8,128)(2,1)}), bf16[16,16,1152]{2,1,0:T(8,128)(2,1)}, u32[]{:S(2)}, u32[]{:S(2)}) async-start(bf16[16,16,1152]{2,1,0:T(8,128)(2,1)} %bitcast.20), calls=%async_computation.1 | async-start | bytes 1179648 | tf_op jit(solution)/shard_map/all_to_all | solution.py:551
  98.9 25.4 %collective-permute-start.15 = (bf16[576,768]{1,0:T(8,128)(2,1)}, bf16[576,768]{1,0:T(8,128)(2,1)}, u32[]{:S(2)}, u32[]{:S(2)}) collective-permute-start(bf16[576,768]{1,0:T(8,128)(2,1)} %get-tuple-element.164), channel_id=1, source_target_pairs={{0,2},{2,0},{4,6},{6,4},{8,10},{10,8},{12,14},{14,12},{16,18},{18,... | collective-permute-start | bytes 2654216 | tf_op jit(solution)/shard_map/ppermute | solution.py:547
  103.8 22.9 %collective-permute-start.14 = (bf16[320,1152]{1,0:T(8,128)(2,1)}, bf16[320,1152]{1,0:T(8,128)(2,1)}, u32[]{:S(2)}, u32[]{:S(2)}) collective-permute-start(bf16[320,1152]{1,0:T(8,128)(2,1)} %get-tuple-element.163), channel_id=1, source_target_pairs={{0,4},{2,6},{4,0},{6,2},{8,12},{10,14},{12,8},{14,10},{16,20},{18,... | collective-permute-start | bytes 2211848 | tf_op jit(solution)/shard_map/ppermute | solution.py:547
  118.3 21.4 %collective-permute-start.19 = (bf16[288,1152]{1,0:T(8,128)(2,1)}, bf16[288,1152]{1,0:T(8,128)(2,1)}, u32[]{:S(2)}, u32[]{:S(2)}) collective-permute-start(bf16[288,1152]{1,0:T(8,128)(2,1)} %get-tuple-element.180), channel_id=1, source_target_pairs={{0,4},{2,6},{4,0},{6,2},{8,12},{10,14},{12,8},{14,10},{16,20},{18,... | collective-permute-start | bytes 1990664 | tf_op jit(solution)/shard_map/ppermute | solution.py:547
  118.3 23.5 %collective-permute-start.18 = (bf16[576,384]{1,0:T(8,128)(2,1)}, bf16[576,384]{1,0:T(8,128)(2,1)}, u32[]{:S(2)}, u32[]{:S(2)}) collective-permute-start(bf16[576,384]{1,0:T(8,128)(2,1)} %get-tuple-element.179), channel_id=1, source_target_pairs={{0,16},{2,18},{4,20},{6,22},{8,24},{10,26},{12,28},{14,30},{16,0},... | collective-permute-start | bytes 1327112 | tf_op jit(solution)/shard_map/ppermute | solution.py:547
  120.3 46.2 %collective-permute-start.6 = (bf16[256,1152]{1,0:T(8,128)(2,1)}, bf16[256,1152]{1,0:T(8,128)(2,1)S(1)}, u32[]{:S(2)}, u32[]{:S(2)}) collective-permute-start(bf16[256,1152]{1,0:T(8,128)(2,1)} %bitcast.11.refs_1_), channel_id=1, source_target_pairs={{0,1},{1,0},{2,3},{3,2},{4,5},{5,4},{6,7},{7,6},{8,9},{9,8},{10,11... | collective-permute-start | bytes 1769480 | tf_op jit(solution)/shard_map/ppermute | solution.py:543
  127.9 20.0 %collective-permute-start.17 = (bf16[176,1152]{1,0:T(8,128)(2,1)S(1)}, bf16[176,1152]{1,0:T(8,128)(2,1)S(1)}, u32[]{:S(2)}, u32[]{:S(2)}) collective-permute-start(bf16[176,1152]{1,0:T(8,128)(2,1)S(1)} %get-tuple-element.177), channel_id=1, source_target_pairs={{0,8},{2,10},{4,12},{6,14},{8,0},{10,2},{12,4},{14,6},{16,24},{18,... | collective-permute-start | bytes 1216520 | tf_op jit(solution)/shard_map/ppermute | solution.py:547
  129.5 33.1 %collective-permute-start.23 = (bf16[288,768]{1,0:T(8,128)(2,1)S(1)}, bf16[288,768]{1,0:T(8,128)(2,1)S(1)}, u32[]{:S(2)}, u32[]{:S(2)}) collective-permute-start(bf16[288,768]{1,0:T(8,128)(2,1)S(1)} %get-tuple-element.209), channel_id=1, source_target_pairs={{0,16},{2,18},{4,20},{6,22},{8,24},{10,26},{12,28},{14,30},{16,0},... | collective-permute-start | bytes 1327112 | tf_op jit(solution)/shard_map/ppermute | solution.py:547
  140.9 23.3 %collective-permute-start.21 = (bf16[144,1152]{1,0:T(8,128)(2,1)S(1)}, bf16[144,1152]{1,0:T(8,128)(2,1)S(1)}, u32[]{:S(2)}, u32[]{:S(2)}) collective-permute-start(bf16[144,1152]{1,0:T(8,128)(2,1)S(1)} %get-tuple-element.191), channel_id=1, source_target_pairs={{0,2},{2,0},{4,6},{6,4},{8,10},{10,8},{12,14},{14,12},{16,18},{18,... | collective-permute-start | bytes 995336 | tf_op jit(solution)/shard_map/ppermute | solution.py:547
  142.9 11.5 %collective-permute-start.24 = (bf16[288,384]{1,0:T(8,128)(2,1)S(1)}, bf16[288,384]{1,0:T(8,128)(2,1)S(1)}, u32[]{:S(2)}, u32[]{:S(2)}) collective-permute-start(bf16[288,384]{1,0:T(8,128)(2,1)S(1)} %get-tuple-element.210), channel_id=1, source_target_pairs={{0,2},{2,0},{4,6},{6,4},{8,10},{10,8},{12,14},{14,12},{16,18},{18,... | collective-permute-start | bytes 663560 | tf_op jit(solution)/shard_map/ppermute | solution.py:547
  148.0 32.5 %collective-permute-start.20 = (bf16[104,1152]{1,0:T(8,128)(2,1)S(1)}, bf16[104,1152]{1,0:T(8,128)(2,1)S(1)}, u32[]{:S(2)}, u32[]{:S(2)}) collective-permute-start(bf16[104,1152]{1,0:T(8,128)(2,1)S(1)} %get-tuple-element.190), channel_id=1, source_target_pairs={{0,16},{2,18},{4,20},{6,22},{8,24},{10,26},{12,28},{14,30},{16,0},... | collective-permute-start | bytes 718856 | tf_op jit(solution)/shard_map/ppermute | solution.py:547
  162.8 12.0 %collective-permute-start.25 = (bf16[72,1152]{1,0:T(8,128)(2,1)S(1)}, bf16[72,1152]{1,0:T(8,128)(2,1)S(1)}, u32[]{:S(2)}, u32[]{:S(2)}) collective-permute-start(bf16[72,1152]{1,0:T(8,128)(2,1)S(1)} %get-tuple-element.212), channel_id=1, source_target_pairs={{0,8},{2,10},{4,12},{6,14},{8,0},{10,2},{12,4},{14,6},{16,24},{18,... | collective-permute-start | bytes 497672 | tf_op jit(solution)/shard_map/ppermute | solution.py:547
  162.9 11.9 %collective-permute-start.26 = (bf16[72,1152]{1,0:T(8,128)(2,1)S(1)}, bf16[72,1152]{1,0:T(8,128)(2,1)S(1)}, u32[]{:S(2)}, u32[]{:S(2)}) collective-permute-start(bf16[72,1152]{1,0:T(8,128)(2,1)S(1)} %get-tuple-element.213), channel_id=1, source_target_pairs={{0,4},{2,6},{4,0},{6,2},{8,12},{10,14},{12,8},{14,10},{16,20},{18,... | collective-permute-start | bytes 497672 | tf_op jit(solution)/shard_map/ppermute | solution.py:547
  164.2 14.8 %collective-permute-start.27 = (bf16[72,1152]{1,0:T(8,128)(2,1)S(1)}, bf16[72,1152]{1,0:T(8,128)(2,1)S(1)}, u32[]{:S(2)}, u32[]{:S(2)}) collective-permute-start(bf16[72,1152]{1,0:T(8,128)(2,1)S(1)} %get-tuple-element.214), channel_id=1, source_target_pairs={{0,12},{2,14},{4,8},{6,10},{8,4},{10,6},{12,0},{14,2},{16,28},{18,... | collective-permute-start | bytes 497672 | tf_op jit(solution)/shard_map/ppermute | solution.py:547
  166.4 14.1 %collective-permute-start.22 = (bf16[72,1152]{1,0:T(8,128)(2,1)S(1)}, bf16[72,1152]{1,0:T(8,128)(2,1)S(1)}, u32[]{:S(2)}, u32[]{:S(2)}) collective-permute-start(bf16[72,1152]{1,0:T(8,128)(2,1)S(1)} %get-tuple-element.195), channel_id=1, source_target_pairs={{0,16},{2,18},{4,20},{6,22},{8,24},{10,26},{12,28},{14,30},{16,0},... | collective-permute-start | bytes 497672 | tf_op jit(solution)/shard_map/ppermute | solution.py:547
  (44 other events, 322.4 us)

commit v7 on v6

--- a/solution.py
+++ b/solution.py
@@ -267,7 +267,7 @@
         e = jnp.exp(s - top)
         total = lane_sum(e)
         made.log[:, h : h + 1] = top + jnp.log(total)
-        made.att[:, cols] = dot((e / total).astype(bf16), made.v[:, cols]).astype(bf16)
+        made.att[:, cols] = dot((e * (1.0 / total)).astype(bf16), made.v[:, cols]).astype(bf16)
     put(made.branch, dot(made.att[...], given.wo[...]))
 
 
@@ -367,17 +367,13 @@
 
 
 def put_vectors(give_ref, first, rows, values):
-    high = values.astype(bf16)
-    low = (values - high.astype(f32)).astype(bf16)
-    give_ref[first : first + rows, :] = high
-    give_ref[first + rows : first + 2 * rows, :] = low
-    return high.astype(f32) + low.astype(f32)
+    rounded = values.astype(bf16)
+    give_ref[first : first + rows, :] = rounded
+    return rounded.astype(f32)
 
 
 def got_vectors(got_ref, rows):
-    first = got_ref.shape[0] - 2 * rows
-    high = got_ref[first : first + rows, :].astype(f32)
-    return high + got_ref[first + rows :, :].astype(f32)
+    return got_ref[got_ref.shape[0] - rows :, :].astype(f32)
 
 
 def attend_weights(n_dev, orders, bounds, given, made, h1_t, branch_t, left, branch_left):
@@ -563,16 +559,13 @@
         total = keep.astype(f32) + got[: 2 * rows].astype(f32)
         kept, give = total[:rows], total[rows:].astype(bf16)
         if vec is not None:
-            got = got[2 * rows :].astype(f32)
-            vec = vec + (got[:vec_rows] + got[vec_rows:])
-            high = vec.astype(bf16)
-            low = (vec - high.astype(f32)).astype(bf16)
-            vec = high.astype(f32) + low.astype(f32)
-            give = jnp.concatenate([give, high, low])
+            rounded = (vec + got[2 * rows :].astype(f32)).astype(bf16)
+            vec = rounded.astype(f32)
+            give = jnp.concatenate([give, rounded])
         return kept, give, vec
     columns = keep.shape[1]
     ins, outs = dict(keep=keep, got=got), dict(keep=((rows, columns), f32))
-    outs.update(give=((rows + 2 * vec_rows, columns), bf16))
+    outs.update(give=((rows + vec_rows, columns), bf16))
     if vec is not None:
         ins.update(vec=vec)
         outs.update(vec=(vec.shape, f32))
@@ -717,7 +710,7 @@
     for i in range(len(attend_orders)):
         span = attend_bounds[i + 1] - attend_bounds[i]
         keeps.append(((width // 2, span), bf16))
-        gives.append(((width // 2 + (0 if i else 2 * vec_rows), span), bf16))
+        gives.append(((width // 2 + (0 if i else vec_rows), span), bf16))
     products = call(
         functools.partial(attend_weights, n_dev, attend_orders, attend_bounds),
         dict(
@@ -737,7 +730,8 @@
     far = after(halves, packed)
     far_other = [swap_cores(rows) for rows in far[:2]]
     far[2] = after(far[2], far_other[0])
-    far_other.append(swap_cores(far[2]))
+    cut_at = 4 * cap // 8
+    far_other.append(jnp.concatenate([swap_cores(far[2][:cut_at]), swap_cores(far[2][cut_at:])]))
     mlp_bounds = (0, 768, lane_pad(2 * part))
     spans = [after_ - before for before, after_ in zip(mlp_bounds, mlp_bounds[1:])]
     mlp_half = [((width // 2, span), bf16) for span in spans]
@@ -755,11 +749,11 @@
     m = Chains(grads.keep, grads.give, mlp_orders)
     last = grads.keep[0]
     last = a.step(0, last)
+    last = m.step(1, last)
     last = a.step(1, last)
     last = m.step(0, last)
     last = a.step(0, last)
     last = a.step(1, last)
-    last = m.step(1, last)
     last = a.step(0, last)
     last = a.step(1, last)
     m.finish(last)

time: 182 us -> 180 us (0.989)
  waiting for transfers between devices: 82.1 us -> 71.2 us
  starting transfers between devices: 32.6 us -> 40.4 us
    ppermute x18, waiting for transfers between devices: 61.1 us -> 52 us  [swap_dp(): lax.ppermute(values, DP, [(i, i ^ flip) for i in range(lax.axis_size(DP))])]
    ppermute x18, starting transfers between devices: 18.2 us -> 25.6 us  [swap_dp(): lax.ppermute(values, DP, [(i, i ^ flip) for i in range(lax.axis_size(DP))])]
    all_to_all x2, waiting for transfers between devices: 16.2 us -> 14.2 us  [spread(): return lax.all_to_all(rows, DP, split_axis=0, concat_axis=0, tiled=True)]
    ppermute x10 -> x11, waiting for transfers between devices: 4.75 us -> 5.1 us  [swap_cores(): return lax.ppermute(values, CORE, [(0, 1), (1, 0)])]
    unnamed x84 -> x92, local copies, waits for them, and re-layouts: 8.35 us -> 8.08 us
  transfers between devices with their start and end apart: 30 -> 31, of which waited for: 17 -> 15; matrix products, arithmetic and copies ran while one was open for 1% -> 2% of each run, Pallas kernels for 21% -> 21%
where the time goes in v7:
time: 180 us; the launch traced here: 179 us
  waiting for transfers between devices  71.2 us (40%)
  Pallas kernels  53.8 us (30%)
  starting transfers between devices  40.4 us (22%)
  local copies, waits for them, and re-layouts  10.9 us (6%)
    pallas_call x22, Pallas kernels, call(): pl.pallas_call(kernel, name=getattr(body, 'func', body).__name__, out_sha...  53.8 us
    ppermute x18, waiting for transfers between devices, swap_dp(): lax.ppermute(values, DP, [(i, i ^ flip) for i in range(lax.axis_size(DP))])  52 us
    ppermute x18, starting transfers between devices, swap_dp(): lax.ppermute(values, DP, [(i, i ^ flip) for i in range(lax.axis_size(DP))])  25.6 us
    all_to_all x2, waiting for transfers between devices, spread(): return lax.all_to_all(rows, DP, split_axis=0, concat_axis=0, tiled=True)  14.2 us
    all_to_all x2, starting transfers between devices, spread(): return lax.all_to_all(rows, DP, split_axis=0, concat_axis=0, tiled=True)  12.8 us
    unnamed x92, local copies, waits for them, and re-layouts  8.08 us
    ppermute x11, waiting for transfers between devices, swap_cores(): return lax.ppermute(values, CORE, [(0, 1), (1, 0)])  5.1 us
  transfers between devices with their start and end apart: 31, of which 15 were waited for; matrix products, arithmetic and copies ran while one was open for 2% of the time, Pallas kernels for 21%

profile of v7, /device:TPU:0, one launch (start us, length us, event | category | flops | bytes accessed | tf_op | source)
XLA Modules:
  0.0 178.8 jit_solution(9719077937753633382)
XLA Ops:
  0.7 2.4 %pack.1 = bf16[256,1152]{1,0:T(8,128)(2,1)} custom-call(bf16[128,1152]{1,0:T(8,128)(2,1)} %refs_0_.1, s32[1,64]{1,0:T(1,128)} %bitcast.31, s32[1,64]{1,0:T(1,128)} %bitcast.35, bf16[128,1152]{1,0:T(8,128)(2,1)} %refs_3_.1), custom_call_target="tpu_custom_call" | custom-call | tf_op jit(solution)/shard_map/pack/pallas_call | solution.py:189
  3.1 8.3 %all-to-all-start = ((bf16[16,16,1152]{2,1,0:T(8,128)(2,1)}), bf16[16,16,1152]{2,1,0:T(8,128)(2,1)S(1)}, u32[]{:S(2)}, u32[]{:S(2)}) async-start(bf16[16,16,1152]{2,1,0:T(8,128)(2,1)} %bitcast.39), calls=%async_computation | async-start | bytes 1179648 | tf_op jit(solution)/shard_map/all_to_all | solution.py:547
  13.5 14.2 %all-to-all-done = bf16[16,16,1152]{2,1,0:T(8,128)(2,1)S(1)} async-done(((bf16[16,16,1152]{2,1,0:T(8,128)(2,1)}), bf16[16,16,1152]{2,1,0:T(8,128)(2,1)S(1)}, u32[]{:S(2)}, u32[]{:S(2)}) %all-to-all-start) | async-done | bytes 589856 | tf_op jit(solution)/shard_map/all_to_all | solution.py:547
  32.5 4.8 %attend.1 = (bf16[256,576]{1,0:T(8,128)(2,1)S(1)}, bf16[256,1152]{1,0:T(8,128)(2,1)S(1)}, bf16[256,576]{1,0:T(8,128)(2,1)S(1)}, f32[256,8]{1,0:T(8,128)S(1)}, bf...) custom-call(bf16[256,1152]{1,0:T(8,128)(2,1)S(1)} %get-tuple-element.120.refs_0_.refs_1_, ...), custom_call_target="tpu_custom_call" | custom-call | flops 5000000000 | bytes 5000000 | tf_op jit(solution)/shard_map/attend/pallas_call | solution.py:189
  39.4 7.4 %mlp.1 = (f32[1,2176]{1,0:T(1,128)S(1)}, bf16[256,1152]{1,0:T(8,128)(2,1)S(1)}, bf16[256,1152]{1,0:T(8,128)(2,1)S(1)}, f32[256,1152]{1,0:T(8,128)S(1)}, bf16[256...) custom-call(bf16[256,1152]{1,0:T(8,128)(2,1)S(1)} %get-tuple-element.122.refs_0_, ...), custom_call_target="tpu_custom_call" | custom-call | tf_op jit(solution)/shard_map/mlp/pallas_call | solution.py:189
  52.7 5.6 %attend_back.1 = (bf16[128,1152]{1,0:T(8,128)(2,1)S(1)}, bf16[128,1152]{1,0:T(8,128)(2,1)S(1)}, bf16[256,576]{1,0:T(8,128)(2,1)S(1)}, bf16[256,576]{1,0:T(8,128)...) custom-call(bf16[256,576]{1,0:T(8,128)(2,1)S(1)} %get-tuple-element.127.refs_0_, ...), custom_call_target="tpu_custom_call" | custom-call | tf_op jit(solution)/shard_map/attend_back/pallas_call | solution.py:189
  61.3 3.6 %attend_weights.1 = (bf16[592,1152]{1,0:T(8,128)(2,1)}, bf16[576,1152]{1,0:T(8,128)(2,1)}, bf16[576,1152]{1,0:T(8,128)(2,1)S(1)}, bf16[576,1152]{1,0:T(8,128)(2,1)S(1)}, f32[16,1152]{1,0:T(8,128)S(1)}) custom-call(bf16[256,1152]{1,0:T(8,128)(2,1)S(1)} %get-tuple-element.136.refs_0_, bf16[256,1152]{1,0:T(8,128)(2,1)S(1)} %get-tuple-element.120.refs_0_.refs_1_, ...), custom_call_target="tpu_custom_call" | custom-call | tf_op jit(solution)/shard_map/attend_weights/pallas_call | solution.py:189
  67.2 9.5 %collective-permute-done.9.refs_1_ = bf16[256,1152]{1,0:T(8,128)(2,1)} collective-permute-done((bf16[256,1152]{1,0:T(8,128)(2,1)S(1)}, bf16[256,1152]{1,0:T(8,128)(2,1)}, u32[]{:S(2)}, u32[]{:S(2)}) %collective-permute-start.9) | collective-permute-done | bytes 589856 | tf_op jit(solution)/shard_map/ppermute | solution.py:543
  81.8 4.5 %all-to-all-start.1 = ((bf16[16,16,1152]{2,1,0:T(8,128)(2,1)}), bf16[16,16,1152]{2,1,0:T(8,128)(2,1)}, u32[]{:S(2)}, u32[]{:S(2)}) async-start(bf16[16,16,1152]{2,1,0:T(8,128)(2,1)} %bitcast.20), calls=%async_computation.1 | async-start | bytes 1179648 | tf_op jit(solution)/shard_map/all_to_all | solution.py:547
  89.8 11.0 %mlp_weights.1 = (bf16[576,768]{1,0:T(8,128)(2,1)}, bf16[576,384]{1,0:T(8,128)(2,1)S(1)}, bf16[576,768]{1,0:T(8,128)(2,1)S(1)}, bf16[576,384]{1,0:T(8,128)(2,1)S(1)}) custom-call(bf16[256,1152]{1,0:T(8,128)(2,1)S(1)} %copy-done.16, bf16[256,1152]{1,0:T(8,128)(2,1)} %collective-permute-done.9.refs_1_, bf16[256,1152]{1,0:T(8,128)(2,1)S(1)} %copy-done.1, ...), custom_call_target="tpu_custom_call" | custom-call | tf_op jit(solution)/shard_map/mlp_weights/pallas_call | solution.py:189
  100.8 2.7 %collective-permute-start.18 = (bf16[576,384]{1,0:T(8,128)(2,1)S(1)}, bf16[576,384]{1,0:T(8,128)(2,1)S(1)}, u32[]{:S(2)}, u32[]{:S(2)}) collective-permute-start(bf16[576,384]{1,0:T(8,128)(2,1)S(1)} %get-tuple-element.168), channel_id=1, source_target_pairs={{0,16},{2,18},{4,20},{6,22},{8,24},{10,26},{12,28},{14,30},{16,0},... | collective-permute-start | bytes 1327112 | tf_op jit(solution)/shard_map/ppermute | solution.py:543
  105.0 6.3 %collective-permute-done.7.refs_0_ = bf16[592,1152]{1,0:T(8,128)(2,1)} collective-permute-done((bf16[592,1152]{1,0:T(8,128)(2,1)}, bf16[592,1152]{1,0:T(8,128)(2,1)}, u32[]{:S(2)}, u32[]{:S(2)}) %collective-permute-start.7) | collective-permute-done | bytes 1364000 | tf_op jit(solution)/shard_map/ppermute | solution.py:543
  111.3 2.6 %turn.8 = (bf16[304,1152]{1,0:T(8,128)(2,1)}, f32[288,1152]{1,0:T(8,128)S(1)}, f32[16,1152]{1,0:T(8,128)S(1)}) custom-call(bf16[592,1152]{1,0:T(8,128)(2,1)} %collective-permute-done.7.refs_0_, bf16[576,1152]{1,0:T(8,128)(2,1)S(1)} %copy-done.10, f32[16,1152]{1,0:T(8,128)S(1)} %get-tuple-element.161.refs_2_), custom_call_target="tpu_custom_call" | custom-call | tf_op jit(solution)/shard_map/turn/pallas_call | solution.py:189
  114.9 14.8 %collective-permute-done.18.refs_0_ = bf16[576,384]{1,0:T(8,128)(2,1)S(1)} collective-permute-done((bf16[576,384]{1,0:T(8,128)(2,1)S(1)}, bf16[576,384]{1,0:T(8,128)(2,1)S(1)}, u32[]{:S(2)}, u32[]{:S(2)}) %collective-permute-start.18) | collective-permute-done | bytes 442400 | tf_op jit(solution)/shard_map/ppermute | solution.py:543
  129.9 2.6 %turn.10 = (bf16[288,1152]{1,0:T(8,128)(2,1)}, f32[288,1152]{1,0:T(8,128)S(1)}) custom-call(bf16[576,1152]{1,0:T(8,128)(2,1)} %collective-permute-done.17.refs_0_, bf16[576,1152]{1,0:T(8,128)(2,1)S(1)} %copy-done.4), custom_call_target="tpu_custom_call" | custom-call | tf_op jit(solution)/shard_map/turn/pallas_call | solution.py:189
  138.1 2.4 %collective-permute-start.19 = (bf16[160,1152]{1,0:T(8,128)(2,1)S(1)}, bf16[160,1152]{1,0:T(8,128)(2,1)S(1)}, u32[]{:S(2)}, u32[]{:S(2)}) collective-permute-start(bf16[160,1152]{1,0:T(8,128)(2,1)S(1)} %get-tuple-element.182), channel_id=1, source_target_pairs={{0,8},{2,10},{4,12},{6,14},{8,0},{10,2},{12,4},{14,6},{16,24},{18,... | collective-permute-start | bytes 1105928 | tf_op jit(solution)/shard_map/ppermute | solution.py:543
  140.5 8.4 %collective-permute-done.20.refs_0_ = bf16[288,1152]{1,0:T(8,128)(2,1)} collective-permute-done((bf16[288,1152]{1,0:T(8,128)(2,1)}, bf16[288,1152]{1,0:T(8,128)(2,1)}, u32[]{:S(2)}, u32[]{:S(2)}) %collective-permute-start.20) | collective-permute-done | bytes 663584 | tf_op jit(solution)/shard_map/ppermute | solution.py:543
  150.3 2.0 %collective-permute-start.25 = (bf16[288,384]{1,0:T(8,128)(2,1)S(1)}, bf16[288,384]{1,0:T(8,128)(2,1)S(1)}, u32[]{:S(2)}, u32[]{:S(2)}) collective-permute-start(bf16[288,384]{1,0:T(8,128)(2,1)S(1)} %copy-done.28), channel_id=1, source_target_pairs={{0,2},{2,0},{4,6},{6,4},{8,10},{10,8},{12,14},{14,12},{16,18},{18,... | collective-permute-start | bytes 663560 | tf_op jit(solution)/shard_map/ppermute | solution.py:543
  154.2 4.8 %collective-permute-start.21 = (bf16[88,1152]{1,0:T(8,128)(2,1)S(1)}, bf16[88,1152]{1,0:T(8,128)(2,1)S(1)}, u32[]{:S(2)}, u32[]{:S(2)}) collective-permute-start(bf16[88,1152]{1,0:T(8,128)(2,1)S(1)} %get-tuple-element.190), channel_id=1, source_target_pairs={{0,16},{2,18},{4,20},{6,22},{8,24},{10,26},{12,28},{14,30},{16,0},... | collective-permute-start | bytes 608264 | tf_op jit(solution)/shard_map/ppermute | solution.py:543
  159.1 3.9 %collective-permute-done.25.refs_1_ = bf16[288,384]{1,0:T(8,128)(2,1)S(1)} collective-permute-done((bf16[288,384]{1,0:T(8,128)(2,1)S(1)}, bf16[288,384]{1,0:T(8,128)(2,1)S(1)}, u32[]{:S(2)}, u32[]{:S(2)}) %collective-permute-start.25) | collective-permute-done | bytes 221216 | tf_op jit(solution)/shard_map/ppermute | solution.py:543
  164.1 2.7 %collective-permute-start.28 = (bf16[72,1152]{1,0:T(8,128)(2,1)S(1)}, bf16[72,1152]{1,0:T(8,128)(2,1)S(1)}, u32[]{:S(2)}, u32[]{:S(2)}) collective-permute-start(bf16[72,1152]{1,0:T(8,128)(2,1)S(1)} %get-tuple-element.214), channel_id=1, source_target_pairs={{0,12},{2,14},{4,8},{6,10},{8,4},{10,6},{12,0},{14,2},{16,28},{18,... | collective-permute-start | bytes 497672 | tf_op jit(solution)/shard_map/ppermute | solution.py:543
  167.6 2.4 %home.1 = (bf16[128,1152]{1,0:T(8,128)(2,1)}, bf16[128,1152]{1,0:T(8,128)(2,1)}) custom-call(s32[1,64]{1,0:T(1,128)S(1)} %bitcast.34, bf16[256,1152]{1,0:T(8,128)(2,1)} %bitcast.11.refs_1_, bf16[256,1152]{1,0:T(8,128)(2,1)S(1)} %collective-permute-done.6.refs_2_, s32[1,64]{1,0:T(1,128)S(1)} %bitcast.38), custom_call_target="tpu_custom_call" | custom-call | tf_op jit(solution)/shard_map/home/pallas_call | solution.py:189
  170.0 2.9 %collective-permute-done.26.refs_1_ = bf16[72,1152]{1,0:T(8,128)(2,1)S(1)} collective-permute-done((bf16[72,1152]{1,0:T(8,128)(2,1)S(1)}, bf16[72,1152]{1,0:T(8,128)(2,1)S(1)}, u32[]{:S(2)}, u32[]{:S(2)}) %collective-permute-start.26) | collective-permute-done | bytes 165920 | tf_op jit(solution)/shard_map/ppermute | solution.py:543
  172.9 3.3 %collective-permute-done.28.refs_3_ = bf16[72,1152]{1,0:T(8,128)(2,1)S(1)} collective-permute-done((bf16[72,1152]{1,0:T(8,128)(2,1)S(1)}, bf16[72,1152]{1,0:T(8,128)(2,1)S(1)}, u32[]{:S(2)}, u32[]{:S(2)}) %collective-permute-start.28) | collective-permute-done | bytes 165920 | tf_op jit(solution)/shard_map/ppermute | solution.py:543
  (160 shorter events, 44.2 us)
Async XLA Ops:
  3.1 24.6 %all-to-all-start = ((bf16[16,16,1152]{2,1,0:T(8,128)(2,1)}), bf16[16,16,1152]{2,1,0:T(8,128)(2,1)S(1)}, u32[]{:S(2)}, u32[]{:S(2)}) async-start(bf16[16,16,1152]{2,1,0:T(8,128)(2,1)} %bitcast.39), calls=%async_computation | async-start | bytes 1179648 | tf_op jit(solution)/shard_map/all_to_all | solution.py:547
  47.4 19.8 %collective-permute-start.8 = (bf16[256,1152]{1,0:T(8,128)(2,1)S(1)}, bf16[256,1152]{1,0:T(8,128)(2,1)S(1)}, u32[]{:S(2)}, u32[]{:S(2)}) collective-permute-start(bf16[256,1152]{1,0:T(8,128)(2,1)S(1)} %get-tuple-element.150), channel_id=1, source_target_pairs={{0,8},{2,10},{4,12},{6,14},{8,0},{10,2},{12,4},{14,6},{16,24},{18,... | collective-permute-start | bytes 1769480 | tf_op jit(solution)/shard_map/ppermute | solution.py:543
  48.9 27.8 %collective-permute-start.9 = (bf16[256,1152]{1,0:T(8,128)(2,1)S(1)}, bf16[256,1152]{1,0:T(8,128)(2,1)}, u32[]{:S(2)}, u32[]{:S(2)}) collective-permute-start(bf16[256,1152]{1,0:T(8,128)(2,1)S(1)} %get-tuple-element.150), channel_id=1, source_target_pairs={{0,4},{2,6},{4,0},{6,2},{8,12},{10,14},{12,8},{14,10},{16,20},{18,... | collective-permute-start | bytes 1769480 | tf_op jit(solution)/shard_map/ppermute | solution.py:543
  49.8 26.9 %collective-permute-start.10 = (bf16[256,1152]{1,0:T(8,128)(2,1)S(1)}, bf16[256,1152]{1,0:T(8,128)(2,1)S(1)}, u32[]{:S(2)}, u32[]{:S(2)}) collective-permute-start(bf16[256,1152]{1,0:T(8,128)(2,1)S(1)} %get-tuple-element.150), channel_id=1, source_target_pairs={{0,12},{2,14},{4,8},{6,10},{8,4},{10,6},{12,0},{14,2},{16,28},{18,... | collective-permute-start | bytes 1769480 | tf_op jit(solution)/shard_map/ppermute | solution.py:543
  76.7 34.6 %collective-permute-start.7 = (bf16[592,1152]{1,0:T(8,128)(2,1)}, bf16[592,1152]{1,0:T(8,128)(2,1)}, u32[]{:S(2)}, u32[]{:S(2)}) collective-permute-start(bf16[592,1152]{1,0:T(8,128)(2,1)} %get-tuple-element.149), channel_id=1, source_target_pairs={{0,2},{2,0},{4,6},{6,4},{8,10},{10,8},{12,14},{14,12},{16,18},{18,... | collective-permute-start | bytes 4091912 | tf_op jit(solution)/shard_map/ppermute | solution.py:543
  77.3 10.2 %collective-permute-start.12 = (bf16[256,1152]{1,0:T(8,128)(2,1)}, bf16[256,1152]{1,0:T(8,128)(2,1)}, u32[]{:S(2)}, u32[]{:S(2)}) collective-permute-start(bf16[256,1152]{1,0:T(8,128)(2,1)} %collective-permute-done.9.refs_1_), channel_id=1, source_target_pairs={{0,1},{1,0},{2,3},{3,2},{4,5},{5,4},{6,7},{7,6},{8,9},{9,8},{10,11... | collective-permute-start | bytes 1769480 | tf_op jit(solution)/shard_map/ppermute | solution.py:539
  77.5 52.4 %collective-permute-start.17 = (bf16[576,1152]{1,0:T(8,128)(2,1)}, bf16[576,1152]{1,0:T(8,128)(2,1)}, u32[]{:S(2)}, u32[]{:S(2)}) collective-permute-start(bf16[576,1152]{1,0:T(8,128)(2,1)} %get-tuple-element.166), channel_id=1, source_target_pairs={{0,8},{2,10},{4,12},{6,14},{8,0},{10,2},{12,4},{14,6},{16,24},{18,... | collective-permute-start | bytes 3981320 | tf_op jit(solution)/shard_map/ppermute | solution.py:543
  81.3 5.1 %collective-permute-start.14 = (bf16[128,1152]{1,0:T(8,128)(2,1)}, bf16[128,1152]{1,0:T(8,128)(2,1)S(1)}, u32[]{:S(2)}, u32[]{:S(2)}) collective-permute-start(bf16[128,1152]{1,0:T(8,128)(2,1)} %get-tuple-element.220), channel_id=1, source_target_pairs={{0,1},{1,0},{2,3},{3,2},{4,5},{5,4},{6,7},{7,6},{8,9},{9,8},{10,11... | collective-permute-start | bytes 884744 | tf_op jit(solution)/shard_map/ppermute | solution.py:539
  81.4 4.9 %collective-permute-start.13 = (bf16[128,1152]{1,0:T(8,128)(2,1)}, bf16[128,1152]{1,0:T(8,128)(2,1)}, u32[]{:S(2)}, u32[]{:S(2)}) collective-permute-start(bf16[128,1152]{1,0:T(8,128)(2,1)} %get-tuple-element.219), channel_id=1, source_target_pairs={{0,1},{1,0},{2,3},{3,2},{4,5},{5,4},{6,7},{7,6},{8,9},{9,8},{10,11... | collective-permute-start | bytes 884744 | tf_op jit(solution)/shard_map/ppermute | solution.py:539
  81.8 52.0 %all-to-all-start.1 = ((bf16[16,16,1152]{2,1,0:T(8,128)(2,1)}), bf16[16,16,1152]{2,1,0:T(8,128)(2,1)}, u32[]{:S(2)}, u32[]{:S(2)}) async-start(bf16[16,16,1152]{2,1,0:T(8,128)(2,1)} %bitcast.20), calls=%async_computation.1 | async-start | bytes 1179648 | tf_op jit(solution)/shard_map/all_to_all | solution.py:547
  100.8 28.9 %collective-permute-start.18 = (bf16[576,384]{1,0:T(8,128)(2,1)S(1)}, bf16[576,384]{1,0:T(8,128)(2,1)S(1)}, u32[]{:S(2)}, u32[]{:S(2)}) collective-permute-start(bf16[576,384]{1,0:T(8,128)(2,1)S(1)} %get-tuple-element.168), channel_id=1, source_target_pairs={{0,16},{2,18},{4,20},{6,22},{8,24},{10,26},{12,28},{14,30},{16,0},... | collective-permute-start | bytes 1327112 | tf_op jit(solution)/shard_map/ppermute | solution.py:543
  103.5 31.1 %collective-permute-start.16 = (bf16[576,768]{1,0:T(8,128)(2,1)}, bf16[576,768]{1,0:T(8,128)(2,1)}, u32[]{:S(2)}, u32[]{:S(2)}) collective-permute-start(bf16[576,768]{1,0:T(8,128)(2,1)} %get-tuple-element.164), channel_id=1, source_target_pairs={{0,2},{2,0},{4,6},{6,4},{8,10},{10,8},{12,14},{14,12},{16,18},{18,... | collective-permute-start | bytes 2654216 | tf_op jit(solution)/shard_map/ppermute | solution.py:543
  113.9 23.0 %collective-permute-start.15 = (bf16[304,1152]{1,0:T(8,128)(2,1)}, bf16[304,1152]{1,0:T(8,128)(2,1)}, u32[]{:S(2)}, u32[]{:S(2)}) collective-permute-start(bf16[304,1152]{1,0:T(8,128)(2,1)} %get-tuple-element.163), channel_id=1, source_target_pairs={{0,4},{2,6},{4,0},{6,2},{8,12},{10,14},{12,8},{14,10},{16,20},{18,... | collective-permute-start | bytes 2101256 | tf_op jit(solution)/shard_map/ppermute | solution.py:543
  132.5 16.5 %collective-permute-start.20 = (bf16[288,1152]{1,0:T(8,128)(2,1)}, bf16[288,1152]{1,0:T(8,128)(2,1)}, u32[]{:S(2)}, u32[]{:S(2)}) collective-permute-start(bf16[288,1152]{1,0:T(8,128)(2,1)} %get-tuple-element.183), channel_id=1, source_target_pairs={{0,4},{2,6},{4,0},{6,2},{8,12},{10,14},{12,8},{14,10},{16,20},{18,... | collective-permute-start | bytes 1990664 | tf_op jit(solution)/shard_map/ppermute | solution.py:543
  133.8 33.0 %collective-permute-start.6 = (bf16[256,1152]{1,0:T(8,128)(2,1)}, bf16[256,1152]{1,0:T(8,128)(2,1)S(1)}, u32[]{:S(2)}, u32[]{:S(2)}) collective-permute-start(bf16[256,1152]{1,0:T(8,128)(2,1)} %bitcast.11.refs_1_), channel_id=1, source_target_pairs={{0,1},{1,0},{2,3},{3,2},{4,5},{5,4},{6,7},{7,6},{8,9},{9,8},{10,11... | collective-permute-start | bytes 1769480 | tf_op jit(solution)/shard_map/ppermute | solution.py:539
  136.0 27.0 %collective-permute-start.24 = (bf16[288,768]{1,0:T(8,128)(2,1)S(1)}, bf16[288,768]{1,0:T(8,128)(2,1)S(1)}, u32[]{:S(2)}, u32[]{:S(2)}) collective-permute-start(bf16[288,768]{1,0:T(8,128)(2,1)S(1)} %get-tuple-element.209), channel_id=1, source_target_pairs={{0,16},{2,18},{4,20},{6,22},{8,24},{10,26},{12,28},{14,30},{16,0},... | collective-permute-start | bytes 1327112 | tf_op jit(solution)/shard_map/ppermute | solution.py:543
  138.1 16.0 %collective-permute-start.19 = (bf16[160,1152]{1,0:T(8,128)(2,1)S(1)}, bf16[160,1152]{1,0:T(8,128)(2,1)S(1)}, u32[]{:S(2)}, u32[]{:S(2)}) collective-permute-start(bf16[160,1152]{1,0:T(8,128)(2,1)S(1)} %get-tuple-element.182), channel_id=1, source_target_pairs={{0,8},{2,10},{4,12},{6,14},{8,0},{10,2},{12,4},{14,6},{16,24},{18,... | collective-permute-start | bytes 1105928 | tf_op jit(solution)/shard_map/ppermute | solution.py:543
  150.2 13.9 %collective-permute-start.22 = (bf16[144,1152]{1,0:T(8,128)(2,1)S(1)}, bf16[144,1152]{1,0:T(8,128)(2,1)S(1)}, u32[]{:S(2)}, u32[]{:S(2)}) collective-permute-start(bf16[144,1152]{1,0:T(8,128)(2,1)S(1)} %get-tuple-element.191), channel_id=1, source_target_pairs={{0,2},{2,0},{4,6},{6,4},{8,10},{10,8},{12,14},{14,12},{16,18},{18,... | collective-permute-start | bytes 995336 | tf_op jit(solution)/shard_map/ppermute | solution.py:543
  150.3 12.8 %collective-permute-start.25 = (bf16[288,384]{1,0:T(8,128)(2,1)S(1)}, bf16[288,384]{1,0:T(8,128)(2,1)S(1)}, u32[]{:S(2)}, u32[]{:S(2)}) collective-permute-start(bf16[288,384]{1,0:T(8,128)(2,1)S(1)} %copy-done.28), channel_id=1, source_target_pairs={{0,2},{2,0},{4,6},{6,4},{8,10},{10,8},{12,14},{14,12},{16,18},{18,... | collective-permute-start | bytes 663560 | tf_op jit(solution)/shard_map/ppermute | solution.py:543
  154.2 23.4 %collective-permute-start.21 = (bf16[88,1152]{1,0:T(8,128)(2,1)S(1)}, bf16[88,1152]{1,0:T(8,128)(2,1)S(1)}, u32[]{:S(2)}, u32[]{:S(2)}) collective-permute-start(bf16[88,1152]{1,0:T(8,128)(2,1)S(1)} %get-tuple-element.190), channel_id=1, source_target_pairs={{0,16},{2,18},{4,20},{6,22},{8,24},{10,26},{12,28},{14,30},{16,0},... | collective-permute-start | bytes 608264 | tf_op jit(solution)/shard_map/ppermute | solution.py:543
  163.2 9.7 %collective-permute-start.26 = (bf16[72,1152]{1,0:T(8,128)(2,1)S(1)}, bf16[72,1152]{1,0:T(8,128)(2,1)S(1)}, u32[]{:S(2)}, u32[]{:S(2)}) collective-permute-start(bf16[72,1152]{1,0:T(8,128)(2,1)S(1)} %get-tuple-element.212), channel_id=1, source_target_pairs={{0,8},{2,10},{4,12},{6,14},{8,0},{10,2},{12,4},{14,6},{16,24},{18,... | collective-permute-start | bytes 497672 | tf_op jit(solution)/shard_map/ppermute | solution.py:543
  163.3 9.6 %collective-permute-start.27 = (bf16[72,1152]{1,0:T(8,128)(2,1)S(1)}, bf16[72,1152]{1,0:T(8,128)(2,1)S(1)}, u32[]{:S(2)}, u32[]{:S(2)}) collective-permute-start(bf16[72,1152]{1,0:T(8,128)(2,1)S(1)} %get-tuple-element.213), channel_id=1, source_target_pairs={{0,4},{2,6},{4,0},{6,2},{8,12},{10,14},{12,8},{14,10},{16,20},{18,... | collective-permute-start | bytes 497672 | tf_op jit(solution)/shard_map/ppermute | solution.py:543
  164.1 12.2 %collective-permute-start.28 = (bf16[72,1152]{1,0:T(8,128)(2,1)S(1)}, bf16[72,1152]{1,0:T(8,128)(2,1)S(1)}, u32[]{:S(2)}, u32[]{:S(2)}) collective-permute-start(bf16[72,1152]{1,0:T(8,128)(2,1)S(1)} %get-tuple-element.214), channel_id=1, source_target_pairs={{0,12},{2,14},{4,8},{6,10},{8,4},{10,6},{12,0},{14,2},{16,28},{18,... | collective-permute-start | bytes 497672 | tf_op jit(solution)/shard_map/ppermute | solution.py:543
  166.8 10.9 %collective-permute-start.23 = (bf16[72,1152]{1,0:T(8,128)(2,1)S(1)}, bf16[72,1152]{1,0:T(8,128)(2,1)S(1)}, u32[]{:S(2)}, u32[]{:S(2)}) collective-permute-start(bf16[72,1152]{1,0:T(8,128)(2,1)S(1)} %get-tuple-element.195), channel_id=1, source_target_pairs={{0,16},{2,18},{4,20},{6,22},{8,24},{10,26},{12,28},{14,30},{16,0},... | collective-permute-start | bytes 497672 | tf_op jit(solution)/shard_map/ppermute | solution.py:543
  (49 other events, 386.5 us)
